TPU v7x, 256 devices: a whole 4x4x8 slice. The times are simulated.
256 devices in a mesh: lmaj: 16 (over z_lo, x, core), lmin: 16 (over z_hi, y).
Axes of the slice: x: 4, y: 4, z: 8 (z_hi: 4, z_lo: 2; z = z_hi * 2 + z_lo), core: 2. Of those that a mesh axis runs over, the one named last changes fastest.
Arguments:
- resid_rows: bfloat16 [512, 3584], P('lmin'), may hold values from -6 to 6
- w_encode: bfloat16 [3584, 98304], P(None, ('lmaj', 'lmin')), may hold values from -0.09375 to 0.09375
- b_encode: float32 [98304], P(('lmaj', 'lmin')), may hold values from -3 to 3
- w_decode: bfloat16 [98304, 3584], P(('lmaj', 'lmin')), may hold values from -0.01953125 to 0.01953125
- b_decode: float32 [3584], replicated, may hold values from -3 to 3
Outputs:
- grad_encode: bfloat16 [3584, 98304], P(None, ('lmaj', 'lmin'))
- grad_b_encode: float32 [98304], P(('lmaj', 'lmin'))
- grad_decode: bfloat16 [98304, 3584], P(('lmaj', 'lmin'))
- grad_b_decode: float32 [3584], replicated
All inputs are finite; a program needn't handle non-finite values.
Results may differ from a plain program's by a relative error of at most 0.006.
Values may be sent and summed in bfloat16 or wider, within the bound.
No kernel may reach another device: no remote copies, remote signals or barrier semaphores. Data moves between devices by JAX's collectives and lax.ppermute only.
A program may use at most 128 MiB of HBM per device.

v0:
```python
import math

import jax
import jax.numpy as jnp
from jax import lax
from jax.sharding import PartitionSpec as P


def per_device(resid_rows, w_encode, b_encode, w_decode, b_decode):
    local_centered = (resid_rows.astype(jnp.float32) - b_decode).astype(jnp.bfloat16)
    centered = lax.all_gather(local_centered, "lmin", axis=0, tiled=True)
    total_rows = centered.shape[0]
    pre = jnp.dot(centered, w_encode, preferred_element_type=jnp.float32) + b_encode
    active = jnp.maximum(pre, 0.0)
    codes = (active * active).astype(jnp.bfloat16)
    partial_rows = lax.psum_scatter(
        jnp.dot(codes, w_decode, preferred_element_type=jnp.float32),
        "lmin",
        scatter_dimension=0,
        tiled=True,
    )
    summed = lax.psum(partial_rows, "lmaj")
    own = lax.dynamic_slice_in_dim(
        centered, lax.axis_index("lmin") * summed.shape[0], summed.shape[0], 0
    )
    error_part = (summed - own.astype(jnp.float32)).astype(jnp.bfloat16)
    error = lax.all_gather(error_part, "lmin", axis=0, tiled=True)
    factor = 1.0 / math.sqrt(total_rows)
    dec_float = w_decode.astype(jnp.float32)
    norms = jnp.sqrt(jnp.sum(dec_float * dec_float, axis=1) + 1e-06)
    code_sum = jnp.sum(codes.astype(jnp.float32), axis=0)
    grad_decode = (
        2.0 * factor * jnp.dot(codes.T, error, preferred_element_type=jnp.float32)
        + 0.5 * factor * (code_sum / norms)[:, None] * dec_float
    ).astype(jnp.bfloat16)
    back = (
        2.0 * factor * jnp.dot(error, w_decode.T, preferred_element_type=jnp.float32)
        + 0.5 * factor * norms
    )
    dpre = back * 2.0 * active
    dpre_round = dpre.astype(jnp.bfloat16)
    grad_encode = jnp.dot(centered.T, dpre_round, preferred_element_type=jnp.float32).astype(
        jnp.bfloat16
    )
    grad_b_encode = jnp.sum(dpre, axis=0)
    through_local = jnp.dot(
        w_encode.astype(jnp.float32), grad_b_encode, precision=lax.Precision.HIGHEST
    )
    through = lax.psum(through_local, ("lmaj", "lmin"))
    grad_b_decode = 2.0 * factor * jnp.sum(error.astype(jnp.float32), axis=0) - through
    return (grad_encode, grad_b_encode, grad_decode, grad_b_decode)


def solution(mesh):
    in_specs = (
        P("lmin", None),
        P(None, ("lmaj", "lmin")),
        P(("lmaj", "lmin")),
        P(("lmaj", "lmin"), None),
        P(),
    )
    out_specs = (P(None, ("lmaj", "lmin")), P(("lmaj", "lmin")), P(("lmaj", "lmin"), None), P())
    return jax.shard_map(
        per_device, mesh=mesh, in_specs=in_specs, out_specs=out_specs, check_vma=False
    )
```

profile of v0, /device:TPU:1, one launch (start us, length us, event | category | flops | bytes accessed | tf_op | source)
XLA Modules:
  0.0 510.2 jit_solution(5980601025028715552)
XLA Ops:
  7.2 0.0 copy-start
  7.2 0.0 all-gather.3.cloned.1.call-start
  7.2 1.8 subtract_convert_fusion.1
  9.0 0.0 all-gather.3.cloned.1.call-update
  9.1 0.0 reduce-scatter.2.cloned.1.call-start
  9.1 77.3 %all-gather.3.cloned.1.call-done = bf16[512,3584]{1,0:T(8,128)(2,1)} async-done(((bf16[32,3584]{1,0:T(8,128)(2,1)}), bf16[512,3584]{1,0:T(8,128)(2,1)}) %all-gather.3.cloned.1.call-update) | async-done | bytes 3670032 | tf_op jit(solution)/shard_map/all_gather | solution.py:11
  86.4 0.0 copy-done
  86.4 0.0 copy-start.1
  86.4 4.3 convert_reduce_fusion.1
  90.7 0.0 copy-done.1
  90.7 5.0 fusion.8
  95.8 0.0 reduce-scatter.2.cloned.1.call-update
  95.8 0.0 all-reduce.2.cloned.1.call-start
  95.8 112.2 %reduce-scatter.2.cloned.1.call-done = f32[32,3584]{1,0:T(8,128)} async-done(((f32[512,3584]{1,0:T(8,128)}), f32[32,3584]{1,0:T(8,128)}) %reduce-scatter.2.cloned.1.call-update) | async-done | bytes 458768 | tf_op jit(solution)/shard_map/reduce_scatter | solution.py:16
  208.0 0.0 all-reduce.2.cloned.1.call-update
  208.1 0.0 all-gather.5.cloned.1.call-start
  208.1 122.0 %all-reduce.2.cloned.1.call-done = f32[32,3584]{1,0:T(8,128)} async-done(((f32[32,3584]{1,0:T(8,128)}), f32[32,3584]{1,0:T(8,128)}) %all-reduce.2.cloned.1.call-update) | async-done | bytes 458768 | tf_op jit(solution)/shard_map/psum | solution.py:22
  330.2 1.8 subtract_convert_fusion
  332.0 0.0 all-gather.5.cloned.1.call-update
  332.0 2.4 fusion.2
  334.4 72.6 %all-gather.5.cloned.1.call-done = bf16[512,3584]{1,0:T(8,128)(2,1)} async-done(((bf16[32,3584]{1,0:T(8,128)(2,1)}), bf16[512,3584]{1,0:T(8,128)(2,1)}) %all-gather.5.cloned.1.call-update) | async-done | bytes 3670032 | tf_op jit(solution)/shard_map/all_gather | solution.py:27
  407.0 5.7 %fusion.9 = (f32[384]{0:T(512)S(1)}, bf16[512,384]{1,0:T(8,128)(2,1)}) fusion(f32[512,384]{1,0:T(8,128)S(1)} %get-tuple-element.7, f32[384]{0:T(512)S(1)} %get-tuple-element.5, bf16[512,3584]{1,0:T(8,128)(2,1)} %all-gather.5.cloned.1.call-done, bf16[384,3584]{1,0:T(8,128)(2,1)} %param.8), kind=kOutput, calls=%fused_computation.24 | convolution fusion | flops 1410465408 | bytes 7605248 | tf_op jit(solution)/shard_map/dot_general | solution.py:37
  412.7 0.0 copy-start.6
  412.7 2.9 convolution_reduce_fusion
  415.5 76.4 %psum.15 = f32[3584]{0:T(1024)} all-reduce(f32[3584]{0:T(1024)} %convolution_reduce_fusion), channel_id=1, replica_groups=mesh['lmaj'=16,'lmin'=16] {'lmaj','lmin'}, use_global_device_ids=true, to_apply=%region_6.0 | all-reduce | flops 3584 | bytes 28672 | tf_op jit(solution)/shard_map/psum | solution.py:49
  492.0 0.0 copy-start.4
  492.0 0.0 copy-start.5
  492.0 2.9 convert_reduce_fusion
  494.9 0.0 copy-done.4
  494.9 0.6 multiply_subtract_fusion
  495.5 0.0 copy-done.5
  495.5 0.0 copy-start.2
  495.5 0.0 copy-start.3
  495.5 4.8 convolution_convert_fusion
  500.3 0.0 copy-done.6
  500.3 0.0 copy-done.2
  500.3 0.0 copy-done.3
  500.3 3.4 fusion.1
  (2 shorter events, 0.0 us)
Async XLA Ops:
  7.2 79.3 %copy-start = (bf16[3584,384]{1,0:T(8,128)(2,1)S(1)}, bf16[3584,384]{1,0:T(8,128)(2,1)}, u32[]{:S(2)}) copy-start(bf16[3584,384]{1,0:T(8,128)(2,1)} %param.6) | copy-start | bytes 8257540
  7.2 79.2 %all-gather.3.cloned.1.call-start = ((), (), s32[]{:S(2)}) async-start(), calls=%async_computation.1 | async-start | bytes 3899392 | tf_op jit(solution)/shard_map/all_gather | solution.py:11
  9.1 199.0 %reduce-scatter.2.cloned.1.call-start = ((), (), s32[]{:S(2)}) async-start(), calls=%async_computation.2 | async-start | bytes 7798784 | tf_op jit(solution)/shard_map/reduce_scatter | solution.py:16
  86.4 4.3 copy-start.1
  95.8 234.4 %all-reduce.2.cloned.1.call-start = ((), (), s32[]{:S(2)}) async-start(), calls=%async_computation.3 | async-start | bytes 917504 | tf_op jit(solution)/shard_map/psum | solution.py:22
  208.1 198.9 %all-gather.5.cloned.1.call-start = ((), (), s32[]{:S(2)}) async-start(), calls=%async_computation.4 | async-start | bytes 3899392 | tf_op jit(solution)/shard_map/all_gather | solution.py:27
  412.7 87.6 %copy-start.6 = (f32[384]{0:T(512)}, f32[384]{0:T(512)S(1)}, u32[]{:S(2)}) copy-start(f32[384]{0:T(512)S(1)} %get-tuple-element.8) | copy-start | bytes 4612
  492.0 2.9 copy-start.4
  492.0 3.5 copy-start.5
  495.5 4.8 copy-start.2
  495.5 4.8 copy-start.3
Sparse Core Ops, SparseCore 0:
  11.0 75.3 all-gather.2
  95.9 112.0 reduce-scatter.1
  210.9 119.2 all-reduce.1
  333.0 73.8 all-gather.4
where the time goes:
time: 511 us; the launch traced here: 510 us
  waiting for transfers between devices  384 us (75%)
  blocking collectives  76.4 us (15%)
  matrix products  26.1 us (5%)
  between operations  13.8 us (3%)
  other arithmetic  9.52 us (2%)
    psum x1, waiting for transfers between devices, per_device(): summed = lax.psum(partial_rows, 'lmaj')  122 us
    reduce_scatter x1, waiting for transfers between devices, per_device(): lax.psum_scatter(jnp.dot(codes, w_decode, preferred_element_type=jnp.floa...  112 us
    all_gather x1, waiting for transfers between devices, per_device(): centered = lax.all_gather(local_centered, 'lmin', axis=0, tiled=True)  77.3 us
    psum x1, blocking collectives, per_device(): through = lax.psum(through_local, ('lmaj', 'lmin'))  76.4 us
    all_gather x1, waiting for transfers between devices, per_device(): error = lax.all_gather(error_part, 'lmin', axis=0, tiled=True)  72.6 us
  transfers between devices with their start and end apart: 4, of which 4 were waited for; matrix products, arithmetic and copies ran while one was open for 0% of the time, Pallas kernels for 0%

commit v1 on v0

v1 whole, which is shorter than its diff:
```python
import math

import jax
import jax.numpy as jnp
from jax import lax
from jax.sharding import Mesh, PartitionSpec as P

LMAJ = ("zl", "x", "c")
LMIN = ("zh", "y")
Z = ("zl", "zh")
XY = ("x", "y")


def spread(block, axes, n):
    return lax.all_to_all(
        jnp.broadcast_to(block[None], (n,) + block.shape), axes, 0, 0, tiled=True
    )


def swap(block):
    return lax.ppermute(block, "c", [(0, 1), (1, 0)])


def per_device(resid_rows, w_encode, b_encode, w_decode, b_decode):
    f32, bf16 = jnp.float32, jnp.bfloat16
    local_rows, width = resid_rows.shape
    nz, nxy, nx, nzh = 8, 16, 4, 4
    total_rows = local_rows * 16
    half = total_rows // 2
    factor = 1.0 / math.sqrt(total_rows)
    core = lax.axis_index("c")
    piece = local_rows // (2 * nx)
    mine = lax.dynamic_slice_in_dim(
        resid_rows, (core * nx + lax.axis_index("x")) * piece, piece, 0
    )
    mine = (mine.astype(f32) - b_decode).astype(bf16)
    block = spread(mine, ("zh",), nzh).reshape(piece * nzh, width)
    own = spread(block, XY, nxy).reshape(half, width)
    other = swap(own)

    def encode(rows):
        pre = jnp.dot(rows, w_encode, preferred_element_type=f32) + b_encode
        active = jnp.maximum(pre, 0.0)
        return active, (active * active).astype(bf16)

    active_own, codes_own = encode(own)
    active_other, codes_other = encode(other)
    to_other = jnp.dot(codes_other, w_decode, preferred_element_type=f32).astype(bf16)
    from_other = swap(to_other)
    part = jnp.dot(codes_own, w_decode, preferred_element_type=f32) + from_other.astype(f32)
    part = part.astype(bf16).reshape(nxy, half // nxy, width)
    part = lax.all_to_all(part, XY, 0, 0, tiled=True)
    part = jnp.sum(part.astype(f32), axis=0).astype(bf16)
    few = half // nxy // nz
    part = lax.all_to_all(part.reshape(nz, few, width), Z, 0, 0, tiled=True)
    summed = jnp.sum(part.astype(f32), axis=0)
    at = (lax.axis_index("zl") * nzh + lax.axis_index("zh")) * few
    few_rows = lax.dynamic_slice_in_dim(block, at, few, 0)
    error_part = (summed - few_rows.astype(f32)).astype(bf16)
    error_block = spread(error_part, Z, nz).reshape(half // nxy, width)
    error_own = spread(error_block, XY, nxy).reshape(half, width)
    error_other = swap(error_own)

    dec_float = w_decode.astype(f32)
    norms = jnp.sqrt(jnp.sum(dec_float * dec_float, axis=1) + 1e-06)

    def backward(error, active):
        back = (
            2.0 * factor * jnp.dot(error, w_decode.T, preferred_element_type=f32)
            + 0.5 * factor * norms
        )
        return back * 2.0 * active

    dpre_own = backward(error_own, active_own)
    dpre_other = backward(error_other, active_other)
    grad_b_encode = jnp.sum(dpre_own, axis=0) + jnp.sum(dpre_other, axis=0)
    through = jnp.dot(w_encode.astype(f32), grad_b_encode, precision=lax.Precision.HIGHEST)
    through = through.reshape(width // 128, 128)
    through = through + swap(through)
    through = jnp.sum(spread(through, Z, nz), axis=0)
    through = jnp.sum(spread(through, XY, nxy), axis=0).reshape(width)

    centered = jnp.concatenate([own, other], axis=0)
    error = jnp.concatenate([error_own, error_other], axis=0)
    codes = jnp.concatenate([codes_own, codes_other], axis=0)
    dpre_round = jnp.concatenate([dpre_own, dpre_other], axis=0).astype(bf16)
    code_sum = jnp.sum(codes.astype(f32), axis=0)
    grad_decode = (
        2.0 * factor * jnp.dot(codes.T, error, preferred_element_type=f32)
        + 0.5 * factor * (code_sum / norms)[:, None] * dec_float
    ).astype(bf16)
    grad_encode = jnp.dot(centered.T, dpre_round, preferred_element_type=f32).astype(bf16)
    grad_b_decode = 2.0 * factor * jnp.sum(error.astype(f32), axis=0) - through
    return (grad_encode, grad_b_encode, grad_decode, grad_b_decode)


def solution(mesh):
    fine = Mesh(mesh.devices.reshape(2, 4, 2, 4, 4), ("zl", "x", "c", "zh", "y"))
    latents = LMAJ + LMIN
    in_specs = (P(LMIN, None), P(None, latents), P(latents), P(latents, None), P())
    out_specs = (P(None, latents), P(latents), P(latents, None), P())
    return jax.shard_map(
        per_device, mesh=fine, in_specs=in_specs, out_specs=out_specs, check_vma=False
    )
```

time: 511 us -> 177 us (0.35)
  waiting for transfers between devices: 384 us -> 15.2 us
  blocking collectives: 76.4 us -> 107 us
  starting transfers between devices: 0.16 us -> 20.3 us
  between operations: 13.8 us -> 0.86 us
    all_gather x2 -> x0, waiting for transfers between devices: 150 us -> none  [the longest x1 77.3 us: per_device(): centered = lax.all_gather(local_centered, 'lmin', axis=0, tiled=True)]
    psum x1 -> x0, waiting for transfers between devices: 122 us -> none  [per_device(): summed = lax.psum(partial_rows, 'lmaj')]
    reduce_scatter x1 -> x0, waiting for transfers between devices: 112 us -> none  [per_device(): lax.psum_scatter(jnp.dot(codes, w_decode, preferred_element_type=jnp.floa...]
    all_to_all x0 -> x5, blocking collectives: none -> 107 us  [the longest x4 79.4 us: spread(): lax.all_to_all(jnp.broadcast_to(block[None], (n,) + block.shape), axes, 0...]
    psum x1 -> x0, blocking collectives: 76.4 us -> none  [per_device(): through = lax.psum(through_local, ('lmaj', 'lmin'))]
    all_to_all x0 -> x3, starting transfers between devices: none -> 10.4 us  [the longest x2 7.08 us: spread(): lax.all_to_all(jnp.broadcast_to(block[None], (n,) + block.shape), axes, 0...]
    ppermute x0 -> x4, starting transfers between devices: none -> 9.85 us  [swap(): return lax.ppermute(block, 'c', [(0, 1), (1, 0)])]
    all_to_all x0 -> x3, waiting for transfers between devices: none -> 7.91 us  [the longest x1 6.88 us: per_device(): part = lax.all_to_all(part.reshape(nz, few, width), Z, 0, 0, tiled=True)]
  transfers between devices with their start and end apart: 4 -> 7, of which waited for: 4 -> 7; matrix products, arithmetic and copies ran while one was open for 0% -> 9% of each run, Pallas kernels for 0% -> 0%
where the time goes in v1:
time: 177 us; the launch traced here: 174 us
  blocking collectives  107 us (60%)
  matrix products  23.3 us (13%)
  starting transfers between devices  20.3 us (11%)
  waiting for transfers between devices  15.2 us (9%)
  other arithmetic  4.99 us (3%)
  local copies, waits for them, and re-layouts  2.66 us (2%)
    all_to_all x4, blocking collectives, spread(): lax.all_to_all(jnp.broadcast_to(block[None], (n,) + block.shape), axes, 0...  79.4 us
    all_to_all x1, blocking collectives, per_device(): part = lax.all_to_all(part, XY, 0, 0, tiled=True)  27.8 us
    ppermute x4, starting transfers between devices, swap(): return lax.ppermute(block, 'c', [(0, 1), (1, 0)])  9.85 us
    ppermute x4, waiting for transfers between devices, swap(): return lax.ppermute(block, 'c', [(0, 1), (1, 0)])  7.3 us
    all_to_all x2, starting transfers between devices, spread(): lax.all_to_all(jnp.broadcast_to(block[None], (n,) + block.shape), axes, 0...  7.08 us
    all_to_all x1, waiting for transfers between devices, per_device(): part = lax.all_to_all(part.reshape(nz, few, width), Z, 0, 0, tiled=True)  6.88 us
    dot_general x1, matrix products, per_device(): jnp.dot(codes.T, error, preferred_element_type=f32)  6.26 us
    dot_general x1, matrix products, per_device(): jnp.dot(centered.T, dpre_round, preferred_element_type=f32).astype(bf16)  5.84 us
  transfers between devices with their start and end apart: 7, of which 7 were waited for; matrix products, arithmetic and copies ran while one was open for 9% of the time, Pallas kernels for 0%

profile of v1, /device:TPU:1, one launch (start us, length us, event | category | flops | bytes accessed | tf_op | source)
XLA Modules:
  0.0 174.5 jit_solution(5710328670895589488)
XLA Ops:
  0.6 0.0 copy-start
  0.7 1.0 subtract_convert_fusion
  1.7 16.0 %all_to_all.40 = bf16[4,4,3584]{2,1,0:T(4,128)(2,1)S(1)} all-to-all(bf16[4,4,3584]{2,1,0:T(4,128)(2,1)S(1)} %broadcast_in_dim.16), channel_id=1, replica_groups=mesh['zl'=2,'x'=4,'c'=2,'zh'=4,'y'=4] {'zh'}, dimensions={0} | all-to-all | bytes 229376 | tf_op jit(solution)/shard_map/all_to_all | solution.py:15
  17.7 0.0 copy-start.10
  17.7 0.2 broadcast_in_dim.18
  17.9 28.5 %all_to_all.41 = bf16[16,16,3584]{2,1,0:T(8,128)(2,1)S(1)} all-to-all(bf16[16,16,3584]{2,1,0:T(8,128)(2,1)S(1)} %broadcast_in_dim.18), channel_id=1, replica_groups=mesh['zl'=2,'x'=4,'c'=2,'zh'=4,'y'=4] {'x','y'}, dimensions={0} | all-to-all | bytes 3670016 | tf_op jit(solution)/shard_map/all_to_all | solution.py:15
  46.4 4.4 %collective-permute-start = (bf16[256,3584]{1,0:T(8,128)(2,1)S(1)}, bf16[256,3584]{1,0:T(8,128)(2,1)S(1)}, u32[]{:S(2)}, u32[]{:S(2)}) collective-permute-start(bf16[256,3584]{1,0:T(8,128)(2,1)S(1)} %bitcast.26), channel_id=1, source_target_pairs={{0,16},{16,0},{1,17},{17,1},{2,18},{18,2},{3,19},{19,3},{4,20},{20... | collective-permute-start | bytes 5505032 | tf_op jit(solution)/shard_map/ppermute | solution.py:21
  50.8 3.4 %collective-permute-done = bf16[256,3584]{1,0:T(8,128)(2,1)S(1)} collective-permute-done((bf16[256,3584]{1,0:T(8,128)(2,1)S(1)}, bf16[256,3584]{1,0:T(8,128)(2,1)S(1)}, u32[]{:S(2)}, u32[]{:S(2)}) %collective-permute-start) | collective-permute-done | bytes 1835040 | tf_op jit(solution)/shard_map/ppermute | solution.py:21
  54.2 0.0 copy-done
  54.2 1.9 %multiply_convert_fusion = (bf16[256,384]{1,0:T(8,128)(2,1)S(1)}, f32[256,384]{1,0:T(8,128)}) fusion(f32[384]{0:T(512)S(1)} %copy-done.10, bf16[256,3584]{1,0:T(8,128)(2,1)S(1)} %collective-permute-done, bf16[3584,384]{1,0:T(8,128)(2,1)S(1)} %copy-done), kind=kOutput, calls=%fused_computation.32 | convolution fusion | flops 705036288 | bytes 5178880 | tf_op jit(solution)/shard_map/dot_general | solution.py:42
  56.0 1.1 convolution_convert_fusion.1
  57.2 0.5 collective-permute-start.1
  57.6 1.9 %multiply_convert_fusion.1 = (bf16[256,384]{1,0:T(8,128)(2,1)S(1)}, f32[256,384]{1,0:T(8,128)}) fusion(f32[384]{0:T(512)S(1)} %copy-done.10, bf16[256,3584]{1,0:T(8,128)(2,1)S(1)} %bitcast.27, bf16[3584,384]{1,0:T(8,128)(2,1)S(1)} %copy-done), kind=kOutput, calls=%fused_computation.33 | convolution fusion | flops 705036288 | bytes 5178880 | tf_op jit(solution)/shard_map/dot_general | solution.py:42
  59.5 1.5 collective-permute-done.1
  61.0 1.1 add_convert_fusion
  62.2 27.8 %all_to_all.42 = bf16[16,16,3584]{2,1,0:T(8,128)(2,1)} all-to-all(bf16[16,16,3584]{2,1,0:T(8,128)(2,1)S(1)} %bitcast.25), channel_id=1, replica_groups=mesh['zl'=2,'x'=4,'c'=2,'zh'=4,'y'=4] {'x','y'}, dimensions={0} | all-to-all | bytes 3670016 | tf_op jit(solution)/shard_map/all_to_all | solution.py:52
  90.0 1.7 %reduce_sum.84 = bf16[16,3584]{1,0:T(8,128)(2,1)S(1)} reduce(bf16[16,16,3584]{2,1,0:T(8,128)(2,1)} %all_to_all.42, bf16[]{:T(256)} %constant.15.clone.1), dimensions={0}, to_apply=%region_0.0 | reduce | flops 860160 | bytes 1949698 | tf_op jit(solution)/shard_map/reduce_sum | solution.py:53
  91.8 0.7 reshape.51
  92.4 3.4 %all-to-all-start.3 = ((bf16[8,2,3584]{2,1,0:T(2,128)(2,1)}), bf16[8,2,3584]{2,1,0:T(2,128)(2,1)S(1)}, u32[]{:S(2)}, u32[]{:S(2)}) async-start(bf16[8,2,3584]{2,1,0:T(2,128)(2,1)} %reshape.51), calls=%async_computation.3 | async-start | bytes 229376 | tf_op jit(solution)/shard_map/all_to_all | solution.py:55
  95.8 6.9 %all-to-all-done.3 = bf16[8,2,3584]{2,1,0:T(2,128)(2,1)S(1)} async-done(((bf16[8,2,3584]{2,1,0:T(2,128)(2,1)}), bf16[8,2,3584]{2,1,0:T(2,128)(2,1)S(1)}, u32[]{:S(2)}, u32[]{:S(2)}) %all-to-all-start.3) | async-done | bytes 114720 | tf_op jit(solution)/shard_map/all_to_all | solution.py:55
  102.7 0.1 convert_reduce_fusion.2
  102.8 0.1 broadcast_in_dim.19
  102.9 9.4 %all_to_all.43 = bf16[8,2,3584]{2,1,0:T(2,128)(2,1)S(1)} all-to-all(bf16[8,2,3584]{2,1,0:T(2,128)(2,1)S(1)} %broadcast_in_dim.19), channel_id=1, replica_groups=mesh['zl'=2,'x'=4,'c'=2,'zh'=4,'y'=4] {'zl','zh'}, dimensions={0} | all-to-all | bytes 229376 | tf_op jit(solution)/shard_map/all_to_all | solution.py:15
  112.3 0.0 copy-start.2
  112.3 0.2 broadcast_in_dim.21
  112.5 0.0 copy-start.12
  112.5 25.5 %all_to_all.44 = bf16[16,16,3584]{2,1,0:T(8,128)(2,1)S(1)} all-to-all(bf16[16,16,3584]{2,1,0:T(8,128)(2,1)S(1)} %broadcast_in_dim.21), channel_id=1, replica_groups=mesh['zl'=2,'x'=4,'c'=2,'zh'=4,'y'=4] {'x','y'}, dimensions={0} | all-to-all | bytes 3670016 | tf_op jit(solution)/shard_map/all_to_all | solution.py:15
  138.1 4.5 %collective-permute-start.2 = (bf16[256,3584]{1,0:T(8,128)(2,1)S(1)}, bf16[256,3584]{1,0:T(8,128)(2,1)S(1)}, u32[]{:S(2)}, u32[]{:S(2)}) collective-permute-start(bf16[256,3584]{1,0:T(8,128)(2,1)S(1)} %bitcast.21), channel_id=1, source_target_pairs={{0,16},{16,0},{1,17},{17,1},{2,18},{18,2},{3,19},{19,3},{4,20},{20... | collective-permute-start | bytes 5505032 | tf_op jit(solution)/shard_map/ppermute | solution.py:21
  142.6 0.6 fusion.2
  143.2 0.1 convert_reduce_fusion.1
  143.4 0.0 copy-start.11
  143.4 1.1 fusion.20
  144.5 1.5 collective-permute-done.2
  146.0 0.0 copy-done.11
  146.0 1.8 %fusion.19 = (f32[384]{0:T(512)S(1)}, bf16[256,384]{1,0:T(8,128)(2,1)}) fusion(f32[256,384]{1,0:T(8,128)S(1)} %copy-done.11, f32[384]{0:T(512)S(1)} %get-tuple-element.9, bf16[256,3584]{1,0:T(8,128)(2,1)S(1)} %collective-permute-done.2, bf16[384,3584]{1,0:T(8,128)(2,1)S(1)} %copy-done.2), kind=kOutput, calls=%fused_computation.43 | convolution fusion | flops 705232512 | bytes 5180416 | tf_op jit(solution)/shard_map/dot_general | solution.py:69
  147.9 2.2 %convolution_reduce_fusion = f32[3584]{0:T(1024)S(1)} fusion(f32[384,1]{0,1:T(1,128)S(1)} %reshape.55, bf16[3584,384]{1,0:T(8,128)(2,1)S(1)} %copy-done), kind=kOutput, calls=%fused_computation.26 | convolution fusion | flops 16515072 | bytes 2768384 | tf_op jit(solution)/shard_map/dot_general | solution.py:77
  150.1 0.5 collective-permute-start.3
  150.6 0.8 collective-permute-done.3
  151.4 0.7 broadcast_in_dim.22
  152.1 3.6 %all-to-all-start.6 = ((f32[8,28,128]{2,1,0:T(8,128)}), f32[8,28,128]{2,1,0:T(8,128)S(1)}, u32[]{:S(2)}, u32[]{:S(2)}) async-start(f32[8,28,128]{2,1,0:T(8,128)} %broadcast_in_dim.22), calls=%async_computation.6 | async-start | bytes 262144 | tf_op jit(solution)/shard_map/all_to_all | solution.py:15
  155.7 6.3 %fusion.1 = bf16[384,3584]{1,0:T(8,128)(2,1)} fusion(bf16[384,3584]{1,0:T(8,128)(2,1)} %param.8, f32[384]{0:T(512)S(1)} %get-tuple-element.8, bf16[256,3584]{1,0:T(8,128)(2,1)} %copy-done.6, bf16[256,3584]{1,0:T(8,128)(2,1)} %bitcast.23, bf16[256,384]{1,0:T(8,128)(2,1)S(1)} %get-tuple-element.12, bf16[256,384]{1,0:T(8,128)(2,1)S(1)} %get-tuple-element.10), kind=kOutput, calls=%fused_computation.6 | convolution fusion | flops 1424293888 | bytes 9569792 | tf_op jit(solution)/shard_map/dot_general | solution.py:89
  161.9 0.3 all-to-all-done.6
  162.2 0.7 broadcast_in_dim.23
  163.0 3.5 %all-to-all-start.7 = ((f32[16,28,128]{2,1,0:T(8,128)}), f32[16,28,128]{2,1,0:T(8,128)S(1)}, u32[]{:S(2)}, u32[]{:S(2)}) async-start(f32[16,28,128]{2,1,0:T(8,128)} %broadcast_in_dim.23), calls=%async_computation.7 | async-start | bytes 524288 | tf_op jit(solution)/shard_map/all_to_all | solution.py:15
  166.5 5.8 %convolution_convert_fusion = bf16[3584,384]{1,0:T(8,128)(2,1)} fusion(bf16[256,3584]{1,0:T(8,128)(2,1)} %copy-done.9, bf16[256,3584]{1,0:T(8,128)(2,1)} %bitcast.28, bf16[256,384]{1,0:T(8,128)(2,1)} %get-tuple-element.5, bf16[256,384]{1,0:T(8,128)(2,1)S(1)} %get-tuple-element.7), kind=kOutput, calls=%fused_computation.5 | convolution fusion | flops 1418788864 | bytes 6815744 | tf_op jit(solution)/shard_map/dot_general | solution.py:92
  172.4 0.7 convert_reduce_fusion
  173.1 0.7 all-to-all-done.7
  173.9 0.6 bitcast_subtract_fusion
  (29 shorter events, 0.2 us)
Async XLA Ops:
  0.6 53.5 %copy-start = (bf16[3584,384]{1,0:T(8,128)(2,1)S(1)}, bf16[3584,384]{1,0:T(8,128)(2,1)}, u32[]{:S(2)}) copy-start(bf16[3584,384]{1,0:T(8,128)(2,1)} %param.6) | copy-start | bytes 8257540
  17.7 36.5 %copy-start.10 = (f32[384]{0:T(512)S(1)}, f32[384]{0:T(512)}, u32[]{:S(2)}) copy-start(f32[384]{0:T(512)} %param.7) | copy-start | bytes 4612
  46.4 11.3 %copy-start.5 = (bf16[16,16,3584]{2,1,0:T(8,128)(2,1)}, bf16[16,16,3584]{2,1,0:T(8,128)(2,1)S(1)}, u32[]{:S(2)}) copy-start(bf16[16,16,3584]{2,1,0:T(8,128)(2,1)S(1)} %all_to_all.41) | copy-start | bytes 5505028
  46.4 9.7 %copy-start.1 = (bf16[384,3584]{1,0:T(8,128)(2,1)S(1)}, bf16[384,3584]{1,0:T(8,128)(2,1)}, u32[]{:S(2)}) copy-start(bf16[384,3584]{1,0:T(8,128)(2,1)} %param.8) | copy-start | bytes 8257540
  46.4 7.8 %collective-permute-start = (bf16[256,3584]{1,0:T(8,128)(2,1)S(1)}, bf16[256,3584]{1,0:T(8,128)(2,1)S(1)}, u32[]{:S(2)}, u32[]{:S(2)}) collective-permute-start(bf16[256,3584]{1,0:T(8,128)(2,1)S(1)} %bitcast.26), channel_id=1, source_target_pairs={{0,16},{16,0},{1,17},{17,1},{2,18},{18,2},{3,19},{19,3},{4,20},{20... | collective-permute-start | bytes 5505032 | tf_op jit(solution)/shard_map/ppermute | solution.py:21
  54.2 1.9 %copy-start.9 = (bf16[256,3584]{1,0:T(8,128)(2,1)}, bf16[256,3584]{1,0:T(8,128)(2,1)S(1)}, u32[]{:S(2)}) copy-start(bf16[256,3584]{1,0:T(8,128)(2,1)S(1)} %collective-permute-done) | copy-start | bytes 5505028
  57.2 3.9 %collective-permute-start.1 = (bf16[256,3584]{1,0:T(8,128)(2,1)S(1)}, bf16[256,3584]{1,0:T(8,128)(2,1)S(1)}, u32[]{:S(2)}, u32[]{:S(2)}) collective-permute-start(bf16[256,3584]{1,0:T(8,128)(2,1)S(1)} %convolution_convert_fusion.1), channel_id=1, source_target_pairs={{0,16},{16,0},{1,17},{17,1},{2,18},{18,2},{3,19},{19,3},{4,20},{20... | collective-permute-start | bytes 5505032 | tf_op jit(solution)/shard_map/ppermute | solution.py:21
  92.4 10.3 %all-to-all-start.3 = ((bf16[8,2,3584]{2,1,0:T(2,128)(2,1)}), bf16[8,2,3584]{2,1,0:T(2,128)(2,1)S(1)}, u32[]{:S(2)}, u32[]{:S(2)}) async-start(bf16[8,2,3584]{2,1,0:T(2,128)(2,1)} %reshape.51), calls=%async_computation.3 | async-start | bytes 229376 | tf_op jit(solution)/shard_map/all_to_all | solution.py:55
  112.3 30.3 %copy-start.2 = (bf16[384,3584]{1,0:T(8,128)(2,1)S(1)}, bf16[384,3584]{1,0:T(8,128)(2,1)}, u32[]{:S(2)}) copy-start(bf16[384,3584]{1,0:T(8,128)(2,1)} %param.8) | copy-start | bytes 8257540
  112.5 30.8 %copy-start.12 = (f32[256,384]{1,0:T(8,128)S(1)}, f32[256,384]{1,0:T(8,128)}, u32[]{:S(2)}) copy-start(f32[256,384]{1,0:T(8,128)} %get-tuple-element.11) | copy-start | bytes 1179652
  138.1 6.5 %copy-start.3 = (bf16[16,16,3584]{2,1,0:T(8,128)(2,1)}, bf16[16,16,3584]{2,1,0:T(8,128)(2,1)S(1)}, u32[]{:S(2)}) copy-start(bf16[16,16,3584]{2,1,0:T(8,128)(2,1)S(1)} %all_to_all.44) | copy-start | bytes 5505028
  138.1 8.0 %collective-permute-start.2 = (bf16[256,3584]{1,0:T(8,128)(2,1)S(1)}, bf16[256,3584]{1,0:T(8,128)(2,1)S(1)}, u32[]{:S(2)}, u32[]{:S(2)}) collective-permute-start(bf16[256,3584]{1,0:T(8,128)(2,1)S(1)} %bitcast.21), channel_id=1, source_target_pairs={{0,16},{16,0},{1,17},{17,1},{2,18},{18,2},{3,19},{19,3},{4,20},{20... | collective-permute-start | bytes 5505032 | tf_op jit(solution)/shard_map/ppermute | solution.py:21
  143.4 2.7 %copy-start.11 = (f32[256,384]{1,0:T(8,128)S(1)}, f32[256,384]{1,0:T(8,128)}, u32[]{:S(2)}) copy-start(f32[256,384]{1,0:T(8,128)} %get-tuple-element.13) | copy-start | bytes 1179652
  146.0 1.8 %copy-start.6 = (bf16[256,3584]{1,0:T(8,128)(2,1)}, bf16[256,3584]{1,0:T(8,128)(2,1)S(1)}, u32[]{:S(2)}) copy-start(bf16[256,3584]{1,0:T(8,128)(2,1)S(1)} %collective-permute-done.2) | copy-start | bytes 5505028
  147.9 14.1 %copy-start.8 = (f32[384]{0:T(512)}, f32[384]{0:T(512)S(1)}, u32[]{:S(2)}) copy-start(f32[384]{0:T(512)S(1)} %add.79) | copy-start | bytes 4612
  150.1 1.3 collective-permute-start.3
  152.1 10.1 %all-to-all-start.6 = ((f32[8,28,128]{2,1,0:T(8,128)}), f32[8,28,128]{2,1,0:T(8,128)S(1)}, u32[]{:S(2)}, u32[]{:S(2)}) async-start(f32[8,28,128]{2,1,0:T(8,128)} %broadcast_in_dim.22), calls=%async_computation.6 | async-start | bytes 262144 | tf_op jit(solution)/shard_map/all_to_all | solution.py:15
  163.0 10.9 %all-to-all-start.7 = ((f32[16,28,128]{2,1,0:T(8,128)}), f32[16,28,128]{2,1,0:T(8,128)S(1)}, u32[]{:S(2)}, u32[]{:S(2)}) async-start(f32[16,28,128]{2,1,0:T(8,128)} %broadcast_in_dim.23), calls=%async_computation.7 | async-start | bytes 524288 | tf_op jit(solution)/shard_map/all_to_all | solution.py:15
  166.5 5.9 %copy-start.4 = (bf16[16,16,3584]{2,1,0:T(8,128)(2,1)S(1)}, bf16[16,16,3584]{2,1,0:T(8,128)(2,1)}, u32[]{:S(2)}) copy-start(bf16[16,16,3584]{2,1,0:T(8,128)(2,1)} %copy-done.3) | copy-start | bytes 5505028
  166.5 5.9 %copy-start.7 = (bf16[256,3584]{1,0:T(8,128)(2,1)S(1)}, bf16[256,3584]{1,0:T(8,128)(2,1)}, u32[]{:S(2)}) copy-start(bf16[256,3584]{1,0:T(8,128)(2,1)} %copy-done.6) | copy-start | bytes 5505028

commit v2 on v1

v2 whole, which is shorter than its diff:
```python
import math

import jax
import jax.numpy as jnp
from jax import lax
from jax.sharding import Mesh, PartitionSpec as P

LMAJ = ("zl", "x", "c")
LMIN = ("zh", "y")
WIDE = ("zl", "x", "y")
NWIDE, NZH, NC = 32, 4, 2


def spread(block, axes, n):
    return lax.all_to_all(
        jnp.broadcast_to(block[None], (n,) + block.shape), axes, 0, 0, tiled=True
    )


def swap(block):
    return lax.ppermute(block, "c", [(0, 1), (1, 0)])


def per_device(resid_rows, w_encode, b_encode, w_decode, b_decode):
    f32, bf16 = jnp.float32, jnp.bfloat16
    local_rows, width = resid_rows.shape
    total_rows = local_rows * 16
    half = total_rows // NC
    rows = half // NWIDE
    factor = 1.0 / math.sqrt(total_rows)

    enc = (w_encode, swap(w_encode))
    dec = (w_decode, swap(w_decode))
    bias = (b_encode, swap(b_encode))

    piece = rows // NZH
    at = (lax.axis_index("c") * 2 + lax.axis_index("zl")) * 4 + lax.axis_index("x")
    mine = lax.dynamic_slice_in_dim(resid_rows, at * piece, piece, 0)
    mine = (mine.astype(f32) - b_decode).astype(bf16)
    block = spread(mine, ("zh",), NZH).reshape(rows, width)
    centered = spread(block, WIDE, NWIDE).reshape(half, width)

    active, codes = [], []
    for w, b in zip(enc, bias):
        a = jnp.maximum(jnp.dot(centered, w, preferred_element_type=f32) + b, 0.0)
        active.append(a)
        codes.append((a * a).astype(bf16))
    part = jnp.dot(codes[0], dec[0], preferred_element_type=f32) + jnp.dot(
        codes[1], dec[1], preferred_element_type=f32
    )
    part = part.astype(bf16).reshape(NWIDE, rows, width)
    part = lax.all_to_all(part, WIDE, 0, 0, tiled=True)
    part = jnp.sum(part.astype(f32), axis=0).astype(bf16)
    summed = jnp.sum(spread(part, ("zh",), NZH).astype(f32), axis=0)
    error_block = (summed - block.astype(f32)).astype(bf16)
    error = spread(error_block, WIDE, NWIDE).reshape(half, width)

    dec_float = [w.astype(f32) for w in dec]
    norms = [jnp.sqrt(jnp.sum(w * w, axis=1) + 1e-06) for w in dec_float]
    dpre = []
    for w, n, a in zip(dec, norms, active):
        back = 2.0 * factor * jnp.dot(error, w.T, preferred_element_type=f32) + 0.5 * factor * n
        dpre.append(back * 2.0 * a)
    bias_grad = [jnp.sum(d, axis=0) for d in dpre]

    through = -2.0 * factor / NZH * jnp.sum(error_block.astype(f32), axis=0)
    for w, g in zip(enc, bias_grad):
        through = through + jnp.dot(w.astype(f32), g, precision=lax.Precision.HIGHEST)
    through = through.reshape(width // 128, 128)
    through = through + swap(through)
    codes[1], dpre[1], through = lax.optimization_barrier((codes[1], dpre[1], through))
    through = jnp.sum(spread(through, ("zh",), NZH), axis=0)
    codes[0], dpre[0], through = lax.optimization_barrier((codes[0], dpre[0], through))
    through = jnp.sum(spread(through, WIDE, NWIDE), axis=0).reshape(width)

    def decode_part(k):
        code_sum = jnp.sum(codes[k].astype(f32), axis=0)
        return (
            2.0 * factor * jnp.dot(codes[k].T, error, preferred_element_type=f32)
            + 0.5 * factor * (code_sum / norms[k])[:, None] * dec_float[k]
        )

    def encode_part(k):
        return jnp.dot(centered.T, dpre[k].astype(bf16), preferred_element_type=f32)

    from_decode = swap(decode_part(1).astype(bf16))
    from_encode = swap(encode_part(1).astype(bf16))
    grad_decode = (decode_part(0) + from_decode.astype(f32)).astype(bf16)
    grad_encode = (encode_part(0) + from_encode.astype(f32)).astype(bf16)
    grad_b_encode = bias_grad[0] + swap(bias_grad[1])
    return (grad_encode, grad_b_encode, grad_decode, -through)


def solution(mesh):
    fine = Mesh(mesh.devices.reshape(2, 4, 2, 4, 4), ("zl", "x", "c", "zh", "y"))
    latents = LMAJ + LMIN
    in_specs = (P(LMIN, None), P(None, latents), P(latents), P(latents, None), P())
    out_specs = (P(None, latents), P(latents), P(latents, None), P())
    return jax.shard_map(
        per_device, mesh=fine, in_specs=in_specs, out_specs=out_specs, check_vma=False
    )
```

time: 177 us -> 192 us (1.085)
  blocking collectives: 107 us -> 65.4 us
  waiting for transfers between devices: 15.2 us -> 34 us
  matrix products: 23.3 us -> 41.9 us
  starting transfers between devices: 20.3 us -> 30.2 us
  other arithmetic: 4.99 us -> 14.7 us
    all_to_all x4 -> x3, blocking collectives: 79.4 us -> 36.2 us  [spread(): lax.all_to_all(jnp.broadcast_to(block[None], (n,) + block.shape), axes, 0...]
    all_to_all x2 -> x3, waiting for transfers between devices: 1.03 us -> 32.3 us  [spread(): lax.all_to_all(jnp.broadcast_to(block[None], (n,) + block.shape), axes, 0...]
    dot_general x9 -> x12, matrix products: 23.3 us -> 41.9 us  [the longest x2 10.6 us: decode_part(): jnp.dot(codes[k].T, error, preferred_element_type=f32)]
    all_to_all x2 -> x3, starting transfers between devices: 7.08 us -> 17.3 us  [spread(): lax.all_to_all(jnp.broadcast_to(block[None], (n,) + block.shape), axes, 0...]
    all_to_all x1 -> x0, waiting for transfers between devices: 6.88 us -> none  [per_device(): part = lax.all_to_all(part.reshape(nz, few, width), Z, 0, 0, tiled=True)]
    convert_element_type x1 -> x2, other arithmetic: 0.03 us -> 5.72 us  [the longest x1 5.7 us: per_device(): grad_decode = (decode_part(0) + from_decode.astype(f32)).astype(bf16)]
    ppermute x4 -> x7, waiting for transfers between devices: 7.3 us -> 1.67 us  [swap(): return lax.ppermute(block, 'c', [(0, 1), (1, 0)])]
    reduce_sum x6 -> x8, other arithmetic: 1.57 us -> 5.08 us  [the longest x2 4.8 us: per_device(): norms = [jnp.sqrt(jnp.sum(w * w, axis=1) + 1e-06) for w in dec_float]]
  transfers between devices with their start and end apart: 7 -> 10, of which waited for: 7 -> 4; matrix products, arithmetic and copies ran while one was open for 9% -> 15% of each run, Pallas kernels for 0% -> 0%
where the time goes in v2:
time: 192 us; the launch traced here: 191 us
  blocking collectives  65.4 us (34%)
  matrix products  41.9 us (22%)
  waiting for transfers between devices  34 us (18%)
  starting transfers between devices  30.2 us (16%)
  other arithmetic  14.7 us (8%)
  local copies, waits for them, and re-layouts  3.77 us (2%)
    all_to_all x3, blocking collectives, spread(): lax.all_to_all(jnp.broadcast_to(block[None], (n,) + block.shape), axes, 0...  36.2 us
    all_to_all x3, waiting for transfers between devices, spread(): lax.all_to_all(jnp.broadcast_to(block[None], (n,) + block.shape), axes, 0...  32.3 us
    all_to_all x1, blocking collectives, per_device(): part = lax.all_to_all(part, WIDE, 0, 0, tiled=True)  29.2 us
    all_to_all x3, starting transfers between devices, spread(): lax.all_to_all(jnp.broadcast_to(block[None], (n,) + block.shape), axes, 0...  17.3 us
    ppermute x7, starting transfers between devices, swap(): return lax.ppermute(block, 'c', [(0, 1), (1, 0)])  12.9 us
    dot_general x2, matrix products, decode_part(): jnp.dot(codes[k].T, error, preferred_element_type=f32)  10.6 us
    dot_general x2, matrix products, encode_part(): return jnp.dot(centered.T, dpre[k].astype(bf16), preferred_element_type=f32)  7.14 us
    dot_general x2, matrix products, per_device(): jnp.dot(error, w.T, preferred_element_type=f32)  7.1 us
  transfers between devices with their start and end apart: 10, of which 4 were waited for; matrix products, arithmetic and copies ran while one was open for 15% of the time, Pallas kernels for 0%

profile of v2, /device:TPU:1, one launch (start us, length us, event | category | flops | bytes accessed | tf_op | source)
XLA Modules:
  0.0 190.8 jit_solution(15130690991031465328)
XLA Ops:
  0.6 0.9 subtract_convert_fusion.2
  1.5 15.8 %all_to_all.35 = bf16[4,2,3584]{2,1,0:T(2,128)(2,1)S(1)} all-to-all(bf16[4,2,3584]{2,1,0:T(2,128)(2,1)S(1)} %broadcast_in_dim.14), channel_id=1, replica_groups=mesh['zl'=2,'x'=4,'c'=2,'zh'=4,'y'=4] {'zh'}, dimensions={0} | all-to-all | bytes 114688 | tf_op jit(solution)/shard_map/all_to_all | solution.py:15
  17.4 0.0 copy-start.2
  17.4 1.3 broadcast_in_dim.16
  18.7 7.5 %all-to-all-start.1 = ((bf16[32,8,3584]{2,1,0:T(8,128)(2,1)}), bf16[32,8,3584]{2,1,0:T(8,128)(2,1)S(1)}, u32[]{:S(2)}, u32[]{:S(2)}) async-start(bf16[32,8,3584]{2,1,0:T(8,128)(2,1)} %broadcast_in_dim.16), calls=%async_computation.1 | async-start | bytes 3670016 | tf_op jit(solution)/shard_map/all_to_all | solution.py:15
  26.2 2.5 %collective-permute-start = (bf16[3584,384]{1,0:T(8,128)(2,1)}, bf16[3584,384]{1,0:T(8,128)(2,1)}, u32[]{:S(2)}, u32[]{:S(2)}) collective-permute-start(bf16[3584,384]{1,0:T(8,128)(2,1)} %param.6), channel_id=1, source_target_pairs={{0,16},{16,0},{1,17},{17,1},{2,18},{18,2},{3,19},{19,3},{4,20},{20... | collective-permute-start | bytes 8257544 | tf_op jit(solution)/shard_map/ppermute | solution.py:21
  28.7 0.1 collective-permute-start.2
  28.8 0.4 collective-permute-start.1
  29.2 18.3 %all-to-all-done.1 = bf16[32,8,3584]{2,1,0:T(8,128)(2,1)S(1)} async-done(((bf16[32,8,3584]{2,1,0:T(8,128)(2,1)}), bf16[32,8,3584]{2,1,0:T(8,128)(2,1)S(1)}, u32[]{:S(2)}, u32[]{:S(2)}) %all-to-all-start.1) | async-done | bytes 1835040 | tf_op jit(solution)/shard_map/all_to_all | solution.py:15
  47.6 2.9 %multiply_convert_fusion.1 = (bf16[256,384]{1,0:T(8,128)(2,1)S(1)}, f32[256,384]{1,0:T(8,128)S(1)}) fusion(f32[384]{0:T(512)S(1)} %copy-done.2, bf16[3584,384]{1,0:T(8,128)(2,1)} %param.6, bf16[32,8,3584]{2,1,0:T(8,128)(2,1)S(1)} %all-to-all-done.1), kind=kOutput, calls=%fused_computation.48 | convolution fusion | flops 705036288 | bytes 5178880 | tf_op jit(solution)/shard_map/dot_general | solution.py:45
  50.5 0.0 copy-start
  50.5 0.0 collective-permute-done
  50.5 3.8 %multiply_convert_fusion = (bf16[256,384]{1,0:T(8,128)(2,1)S(1)}, f32[256,384]{1,0:T(8,128)}) fusion(f32[384]{0:T(512)S(1)} %collective-permute-done.1, bf16[3584,384]{1,0:T(8,128)(2,1)} %collective-permute-done, bf16[32,8,3584]{2,1,0:T(8,128)(2,1)S(1)} %all-to-all-done.1), kind=kOutput, calls=%fused_computation.47 | convolution fusion | flops 705036288 | bytes 5178880 | tf_op jit(solution)/shard_map/dot_general | solution.py:45
  54.3 1.1 fusion.62
  55.5 2.9 %fusion.6 = bf16[32,8,3584]{2,1,0:T(8,128)(2,1)S(1)} fusion(f32[256,3584]{1,0:T(8,128)S(1)} %fusion.62, bf16[256,384]{1,0:T(8,128)(2,1)S(1)} %get-tuple-element.14, bf16[384,3584]{1,0:T(8,128)(2,1)} %collective-permute-done.2), kind=kOutput, calls=%fused_computation.16 | convolution fusion | flops 706478080 | bytes 8454144 | tf_op jit(solution)/shard_map/dot_general | solution.py:48
  58.4 29.2 %all_to_all.36 = bf16[32,8,3584]{2,1,0:T(8,128)(2,1)} all-to-all(bf16[32,8,3584]{2,1,0:T(8,128)(2,1)S(1)} %fusion.6), channel_id=1, replica_groups=mesh['zl'=2,'x'=4,'c'=2,'zh'=4,'y'=4] {'zl','x','y'}, dimensions={0} | all-to-all | bytes 3670016 | tf_op jit(solution)/shard_map/all_to_all | solution.py:52
  87.6 1.8 reduce_sum.104
  89.4 11.2 %all_to_all.37 = bf16[4,8,3584]{2,1,0:T(8,128)(2,1)S(1)} all-to-all(bf16[4,8,3584]{2,1,0:T(8,128)(2,1)S(1)} %broadcast_in_dim.17), channel_id=1, replica_groups=mesh['zl'=2,'x'=4,'c'=2,'zh'=4,'y'=4] {'zh'}, dimensions={0} | all-to-all | bytes 458752 | tf_op jit(solution)/shard_map/all_to_all | solution.py:15
  100.7 1.3 broadcast_in_dim.18
  102.0 5.4 %all-to-all-start.4 = ((bf16[32,8,3584]{2,1,0:T(8,128)(2,1)}), bf16[32,8,3584]{2,1,0:T(8,128)(2,1)}, u32[]{:S(2)}, u32[]{:S(2)}) async-start(bf16[32,8,3584]{2,1,0:T(8,128)(2,1)} %broadcast_in_dim.18), calls=%async_computation.4 | async-start | bytes 3670016 | tf_op jit(solution)/shard_map/all_to_all | solution.py:15
  107.4 2.4 %fusion.3 = f32[384]{0:T(512)S(1)} fusion(bf16[384,3584]{1,0:T(8,128)(2,1)} %param.8), kind=kLoop, calls=%fused_computation.11 | loop fusion | flops 4128384 | bytes 2754048 | tf_op jit(solution)/shard_map/reduce_sum | solution.py:59
  109.8 2.4 %fusion.4 = f32[384]{0:T(512)S(1)} fusion(bf16[384,3584]{1,0:T(8,128)(2,1)} %collective-permute-done.2), kind=kLoop, calls=%fused_computation.12 | loop fusion | flops 4128384 | bytes 2754048 | tf_op jit(solution)/shard_map/reduce_sum | solution.py:59
  112.2 0.1 reduce_sum.108
  112.3 0.1 convert_reduce_fusion.3
  112.4 14.0 %all-to-all-done.4 = bf16[32,8,3584]{2,1,0:T(8,128)(2,1)} async-done(((bf16[32,8,3584]{2,1,0:T(8,128)(2,1)}), bf16[32,8,3584]{2,1,0:T(8,128)(2,1)}, u32[]{:S(2)}, u32[]{:S(2)}) %all-to-all-start.4) | async-done | bytes 1835040 | tf_op jit(solution)/shard_map/all_to_all | solution.py:15
  126.4 3.6 %fusion.61 = (f32[384]{0:T(512)S(1)}, bf16[256,384]{1,0:T(8,128)(2,1)S(1)}) fusion(f32[256,384]{1,0:T(8,128)S(1)} %get-tuple-element.19, f32[384]{0:T(512)S(1)} %sqrt_multiply_fusion.1, bf16[384,3584]{1,0:T(8,128)(2,1)} %param.8, bf16[32,8,3584]{2,1,0:T(8,128)(2,1)} %all-to-all-done.4), kind=kOutput, calls=%fused_computation.62 | convolution fusion | flops 705232512 | bytes 5180416 | tf_op jit(solution)/shard_map/dot_general | solution.py:62
  130.0 0.0 copy-start.3
  130.1 2.2 %convolution_reduce_fusion.1 = f32[3584]{0:T(1024)S(1)} fusion(f32[384,1]{0,1:T(1,128)S(1)} %reshape.73, bf16[3584,384]{1,0:T(8,128)(2,1)S(1)} %copy-done.1), kind=kOutput, calls=%fused_computation.43 | convolution fusion | flops 16515072 | bytes 2768384 | tf_op jit(solution)/shard_map/dot_general | solution.py:68
  132.3 3.5 %fusion.60 = (f32[384]{0:T(512)S(1)}, bf16[256,384]{1,0:T(8,128)(2,1)S(1)}) fusion(f32[256,384]{1,0:T(8,128)S(1)} %copy-done.3, f32[384]{0:T(512)S(1)} %sqrt_multiply_fusion, bf16[384,3584]{1,0:T(8,128)(2,1)} %collective-permute-done.2, bf16[32,8,3584]{2,1,0:T(8,128)(2,1)} %all-to-all-done.4), kind=kOutput, calls=%fused_computation.61 | convolution fusion | flops 705232512 | bytes 5180416 | tf_op jit(solution)/shard_map/dot_general | solution.py:62
  135.8 4.0 %convolution_reduce_fusion = f32[3584]{0:T(1024)S(1)} fusion(f32[384,1]{0,1:T(1,128)S(1)} %reshape.75, bf16[3584,384]{1,0:T(8,128)(2,1)} %collective-permute-done), kind=kOutput, calls=%fused_computation.42 | convolution fusion | flops 16515072 | bytes 2768384 | tf_op jit(solution)/shard_map/dot_general | solution.py:68
  139.9 7.2 %collective-permute-start.3 = (f32[28,128]{1,0:T(8,128)S(1)}, f32[28,128]{1,0:T(8,128)S(1)}, u32[]{:S(2)}, u32[]{:S(2)}) collective-permute-start(f32[28,128]{1,0:T(8,128)S(1)} %add_bitcast_fusion), channel_id=1, source_target_pairs={{0,16},{16,0},{1,17},{17,1},{2,18},{18,2},{3,19},{19,3},{4,20},{20... | collective-permute-start | bytes 43016 | tf_op jit(solution)/shard_map/ppermute | solution.py:21
  147.1 0.8 collective-permute-done.3
  147.9 0.1 convert_reduce_fusion.1
  148.0 4.9 %fusion.2 = bf16[384,3584]{1,0:T(8,128)(2,1)} fusion(bf16[256,384]{1,0:T(8,128)(2,1)S(1)} %get-tuple-element.14, bf16[384,3584]{1,0:T(8,128)(2,1)} %collective-permute-done.2, f32[384]{0:T(512)S(1)} %multiply_multiply_fusion, bf16[32,8,3584]{2,1,0:T(8,128)(2,1)} %all-to-all-done.4), kind=kOutput, calls=%fused_computation.8 | convolution fusion | flops 711524352 | bytes 7538176 | tf_op jit(solution)/shard_map/dot_general | solution.py:79
  152.9 0.3 collective-permute-start.6
  153.2 2.7 %convolution_convert_fusion = bf16[3584,384]{1,0:T(8,128)(2,1)} fusion(bf16[32,8,3584]{2,1,0:T(8,128)(2,1)S(1)} %all-to-all-done.1, bf16[256,384]{1,0:T(8,128)(2,1)S(1)} %get-tuple-element.12), kind=kOutput, calls=%fused_computation.9 | convolution fusion | flops 706019328 | bytes 4784128 | tf_op jit(solution)/shard_map/dot_general | solution.py:84
  155.9 0.2 collective-permute-start.4
  156.1 9.2 %all_to_all.38 = f32[4,28,128]{2,1,0:T(8,128)S(1)} all-to-all(f32[4,28,128]{2,1,0:T(8,128)S(1)} %broadcast_in_dim.19), channel_id=1, replica_groups=mesh['zl'=2,'x'=4,'c'=2,'zh'=4,'y'=4] {'zh'}, dimensions={0} | all-to-all | bytes 114688 | tf_op jit(solution)/shard_map/all_to_all | solution.py:15
  165.3 0.9 broadcast_in_dim.20
  166.2 4.4 %all-to-all-start.6 = ((f32[32,28,128]{2,1,0:T(8,128)}), f32[32,28,128]{2,1,0:T(8,128)S(1)}, u32[]{:S(2)}, u32[]{:S(2)}) async-start(f32[32,28,128]{2,1,0:T(8,128)} %broadcast_in_dim.20), calls=%async_computation.6 | async-start | bytes 1048576 | tf_op jit(solution)/shard_map/all_to_all | solution.py:15
  170.6 2.2 %collective-permute-start.5 = (f32[384]{0:T(512)S(1)}, f32[384]{0:T(512)S(1)}, u32[]{:S(2)}, u32[]{:S(2)}) collective-permute-start(f32[384]{0:T(512)S(1)} %get-tuple-element.20), channel_id=1, source_target_pairs={{0,16},{16,0},{1,17},{17,1},{2,18},{18,2},{3,19},{19,3},{4,20},{20... | collective-permute-start | bytes 4616 | tf_op jit(solution)/shard_map/ppermute | solution.py:21
  172.8 0.8 collective-permute-done.5
  173.6 0.6 add.108
  174.2 0.1 convert_reduce_fusion.2
  174.2 5.7 %fusion.1 = f32[384,3584]{1,0:T(8,128)} fusion(bf16[256,384]{1,0:T(8,128)(2,1)S(1)} %get-tuple-element.13, bf16[384,3584]{1,0:T(8,128)(2,1)} %param.8, f32[384]{0:T(512)S(1)} %multiply_multiply_fusion.1, bf16[32,8,3584]{2,1,0:T(8,128)(2,1)} %all-to-all-done.4), kind=kOutput, calls=%fused_computation.7 | convolution fusion | flops 710148096 | bytes 10290688 | tf_op jit(solution)/shard_map/dot_general | solution.py:79
  180.0 0.6 negate_bitcast_fusion
  180.6 5.7 %add_convert_fusion = bf16[384,3584]{1,0:T(8,128)(2,1)} fusion(f32[384,3584]{1,0:T(8,128)} %fusion.1, bf16[384,3584]{1,0:T(8,128)(2,1)} %collective-permute-done.6), kind=kLoop, calls=%fused_computation.13 | loop fusion | flops 4128768 | bytes 11010048 | tf_op jit(solution)/shard_map/convert_element_type | solution.py:88
  186.3 4.5 %add_convert_fusion.1 = bf16[3584,384]{1,0:T(8,128)(2,1)} fusion(bf16[3584,384]{1,0:T(8,128)(2,1)} %collective-permute-done.4, bf16[32,8,3584]{2,1,0:T(8,128)(2,1)S(1)} %all-to-all-done.1, bf16[256,384]{1,0:T(8,128)(2,1)S(1)} %get-tuple-element.11), kind=kOutput, calls=%fused_computation.14 | convolution fusion | flops 708771840 | bytes 7536640 | tf_op jit(solution)/shard_map/dot_general | solution.py:84
  (26 shorter events, 0.3 us)
Async XLA Ops:
  17.4 11.4 %copy-start.2 = (f32[384]{0:T(512)S(1)}, f32[384]{0:T(512)}, u32[]{:S(2)}) copy-start(f32[384]{0:T(512)} %param.7) | copy-start | bytes 4612
  18.7 28.8 %all-to-all-start.1 = ((bf16[32,8,3584]{2,1,0:T(8,128)(2,1)}), bf16[32,8,3584]{2,1,0:T(8,128)(2,1)S(1)}, u32[]{:S(2)}, u32[]{:S(2)}) async-start(bf16[32,8,3584]{2,1,0:T(8,128)(2,1)} %broadcast_in_dim.16), calls=%async_computation.1 | async-start | bytes 3670016 | tf_op jit(solution)/shard_map/all_to_all | solution.py:15
  26.2 24.3 %collective-permute-start = (bf16[3584,384]{1,0:T(8,128)(2,1)}, bf16[3584,384]{1,0:T(8,128)(2,1)}, u32[]{:S(2)}, u32[]{:S(2)}) collective-permute-start(bf16[3584,384]{1,0:T(8,128)(2,1)} %param.6), channel_id=1, source_target_pairs={{0,16},{16,0},{1,17},{17,1},{2,18},{18,2},{3,19},{19,3},{4,20},{20... | collective-permute-start | bytes 8257544 | tf_op jit(solution)/shard_map/ppermute | solution.py:21
  28.7 26.8 %collective-permute-start.2 = (bf16[384,3584]{1,0:T(8,128)(2,1)}, bf16[384,3584]{1,0:T(8,128)(2,1)}, u32[]{:S(2)}, u32[]{:S(2)}) collective-permute-start(bf16[384,3584]{1,0:T(8,128)(2,1)} %param.8), channel_id=1, source_target_pairs={{0,16},{16,0},{1,17},{17,1},{2,18},{18,2},{3,19},{19,3},{4,20},{20... | collective-permute-start | bytes 8257544 | tf_op jit(solution)/shard_map/ppermute | solution.py:21
  28.8 21.7 %collective-permute-start.1 = (f32[384]{0:T(512)S(1)}, f32[384]{0:T(512)S(1)}, u32[]{:S(2)}, u32[]{:S(2)}) collective-permute-start(f32[384]{0:T(512)S(1)} %copy-done.2), channel_id=1, source_target_pairs={{0,16},{16,0},{1,17},{17,1},{2,18},{18,2},{3,19},{19,3},{4,20},{20... | collective-permute-start | bytes 4616 | tf_op jit(solution)/shard_map/ppermute | solution.py:21
  50.5 3.8 %copy-start = (bf16[384,3584]{1,0:T(8,128)(2,1)S(1)}, bf16[384,3584]{1,0:T(8,128)(2,1)}, u32[]{:S(2)}) copy-start(bf16[384,3584]{1,0:T(8,128)(2,1)} %param.8) | copy-start | bytes 8257540
  102.0 24.4 %all-to-all-start.4 = ((bf16[32,8,3584]{2,1,0:T(8,128)(2,1)}), bf16[32,8,3584]{2,1,0:T(8,128)(2,1)}, u32[]{:S(2)}, u32[]{:S(2)}) async-start(bf16[32,8,3584]{2,1,0:T(8,128)(2,1)} %broadcast_in_dim.18), calls=%async_computation.4 | async-start | bytes 3670016 | tf_op jit(solution)/shard_map/all_to_all | solution.py:15
  126.4 3.7 %copy-start.1 = (bf16[3584,384]{1,0:T(8,128)(2,1)S(1)}, bf16[3584,384]{1,0:T(8,128)(2,1)}, u32[]{:S(2)}) copy-start(bf16[3584,384]{1,0:T(8,128)(2,1)} %param.6) | copy-start | bytes 8257540
  130.0 2.3 %copy-start.3 = (f32[256,384]{1,0:T(8,128)S(1)}, f32[256,384]{1,0:T(8,128)}, u32[]{:S(2)}) copy-start(f32[256,384]{1,0:T(8,128)} %get-tuple-element.17) | copy-start | bytes 1179652
  139.9 8.1 %collective-permute-start.3 = (f32[28,128]{1,0:T(8,128)S(1)}, f32[28,128]{1,0:T(8,128)S(1)}, u32[]{:S(2)}, u32[]{:S(2)}) collective-permute-start(f32[28,128]{1,0:T(8,128)S(1)} %add_bitcast_fusion), channel_id=1, source_target_pairs={{0,16},{16,0},{1,17},{17,1},{2,18},{18,2},{3,19},{19,3},{4,20},{20... | collective-permute-start | bytes 43016 | tf_op jit(solution)/shard_map/ppermute | solution.py:21
  152.9 27.7 %collective-permute-start.6 = (bf16[384,3584]{1,0:T(8,128)(2,1)}, bf16[384,3584]{1,0:T(8,128)(2,1)}, u32[]{:S(2)}, u32[]{:S(2)}) collective-permute-start(bf16[384,3584]{1,0:T(8,128)(2,1)} %fusion.2), channel_id=1, source_target_pairs={{0,16},{16,0},{1,17},{17,1},{2,18},{18,2},{3,19},{19,3},{4,20},{20... | collective-permute-start | bytes 8257544 | tf_op jit(solution)/shard_map/ppermute | solution.py:21
  155.9 30.4 %collective-permute-start.4 = (bf16[3584,384]{1,0:T(8,128)(2,1)}, bf16[3584,384]{1,0:T(8,128)(2,1)}, u32[]{:S(2)}, u32[]{:S(2)}) collective-permute-start(bf16[3584,384]{1,0:T(8,128)(2,1)} %convolution_convert_fusion), channel_id=1, source_target_pairs={{0,16},{16,0},{1,17},{17,1},{2,18},{18,2},{3,19},{19,3},{4,20},{20... | collective-permute-start | bytes 8257544 | tf_op jit(solution)/shard_map/ppermute | solution.py:21
  166.2 13.7 %all-to-all-start.6 = ((f32[32,28,128]{2,1,0:T(8,128)}), f32[32,28,128]{2,1,0:T(8,128)S(1)}, u32[]{:S(2)}, u32[]{:S(2)}) async-start(f32[32,28,128]{2,1,0:T(8,128)} %broadcast_in_dim.20), calls=%async_computation.6 | async-start | bytes 1048576 | tf_op jit(solution)/shard_map/all_to_all | solution.py:15
  170.6 3.0 %collective-permute-start.5 = (f32[384]{0:T(512)S(1)}, f32[384]{0:T(512)S(1)}, u32[]{:S(2)}, u32[]{:S(2)}) collective-permute-start(f32[384]{0:T(512)S(1)} %get-tuple-element.20), channel_id=1, source_target_pairs={{0,16},{16,0},{1,17},{17,1},{2,18},{18,2},{3,19},{19,3},{4,20},{20... | collective-permute-start | bytes 4616 | tf_op jit(solution)/shard_map/ppermute | solution.py:21

commit v3 on v2

v3 whole, which is shorter than its diff:
```python
import functools
import math

import jax
import jax.numpy as jnp
from jax import lax
from jax.experimental import pallas as pl
from jax.experimental.pallas import tpu as pltpu
from jax.sharding import Mesh, PartitionSpec as P

LMAJ = ("zl", "x", "c")
LMIN = ("zh", "y")
WIDE = ("zl", "x", "y")
NWIDE, NZH, NC = 32, 4, 2
CHUNK = 512
VMEM_BYTES = 61 * 1024 * 1024
ANY = pl.BlockSpec(memory_space=pl.ANY)
VMEM = pl.BlockSpec(memory_space=pltpu.VMEM)
f32, bf16 = jnp.float32, jnp.bfloat16


def spread(block, axes, n):
    return lax.all_to_all(
        jnp.broadcast_to(block[None], (n,) + block.shape), axes, 0, 0, tiled=True
    )


def swap(block):
    return lax.ppermute(block, "c", [(0, 1), (1, 0)])


def forward_kernel(
    rows_hbm, enc0, enc1, dec0, dec1, bias0, bias1,
    active0, active1, codes0, codes1, part_hbm,
    rows, enc, dec, pre, codes, part, sem_in, sem_enc, sem_dec, sem_out,
):
    width, latents = enc.shape
    mine = latents // 2
    steps = width // CHUNK

    def at(k):
        return pl.ds(pl.multiple_of(k * CHUNK, CHUNK), CHUNK)

    def enc_copies(k):
        return (
            pltpu.make_async_copy(rows_hbm.at[:, at(k)], rows.at[:, at(k)], sem_in.at[k]),
            pltpu.make_async_copy(enc0.at[at(k)], enc.at[at(k), :mine], sem_enc.at[0, k]),
            pltpu.make_async_copy(enc1.at[at(k)], enc.at[at(k), mine:], sem_enc.at[1, k]),
        )

    def dec_copies(k):
        return (
            pltpu.make_async_copy(dec0.at[:, at(k)], dec.at[:mine, at(k)], sem_dec.at[0, k]),
            pltpu.make_async_copy(dec1.at[:, at(k)], dec.at[mine:, at(k)], sem_dec.at[1, k]),
        )

    for copies in (enc_copies, dec_copies):
        for k in range(steps):
            for copy in copies(k):
                copy.start()

    pre[:, :mine] = jnp.broadcast_to(bias0[...], (pre.shape[0], mine))
    pre[:, mine:] = jnp.broadcast_to(bias1[...], (pre.shape[0], mine))

    @pl.loop(0, steps)
    def _(k):
        for copy in enc_copies(k):
            copy.wait()
        pre[...] += jnp.dot(rows[:, at(k)], enc[at(k), :], preferred_element_type=f32)

    active = jnp.maximum(pre[...], 0.0)
    active0[...] = active[:, :mine]
    active1[...] = active[:, mine:]
    codes[...] = (active * active).astype(bf16)
    codes0[...] = codes[:, :mine]
    codes1[...] = codes[:, mine:]

    def out_copy(k):
        return pltpu.make_async_copy(part.at[:, at(k)], part_hbm.at[:, at(k)], sem_out.at[k])

    @pl.loop(0, steps)
    def _(k):
        for copy in dec_copies(k):
            copy.wait()
        part[:, at(k)] = jnp.dot(
            codes[...], dec[:, at(k)], preferred_element_type=f32
        ).astype(bf16)
        out_copy(k).start()

    for k in range(steps):
        out_copy(k).wait()


def forward(rows, enc, bias, dec):
    count, width = rows.shape
    mine = enc[0].shape[1]
    steps = width // CHUNK
    flat = jax.ShapeDtypeStruct((count, mine), f32)
    half = jax.ShapeDtypeStruct((count, mine), bf16)
    return pl.pallas_call(
        forward_kernel,
        out_shape=(flat, flat, half, half, jax.ShapeDtypeStruct((count, width), bf16)),
        in_specs=[ANY] * 5 + [VMEM] * 2,
        out_specs=(VMEM,) * 4 + (ANY,),
        scratch_shapes=[
            pltpu.VMEM((count, width), bf16),
            pltpu.VMEM((width, 2 * mine), bf16),
            pltpu.VMEM((2 * mine, width), bf16),
            pltpu.VMEM((count, 2 * mine), f32),
            pltpu.VMEM((count, 2 * mine), bf16),
            pltpu.VMEM((count, width), bf16),
            pltpu.SemaphoreType.DMA((steps,)),
            pltpu.SemaphoreType.DMA((2, steps)),
            pltpu.SemaphoreType.DMA((2, steps)),
            pltpu.SemaphoreType.DMA((steps,)),
        ],
        compiler_params=pltpu.CompilerParams(vmem_limit_bytes=VMEM_BYTES),
        cost_estimate=pl.CostEstimate(
            flops=8 * count * width * mine, bytes_accessed=13_000_000, transcendentals=0
        ),
        name="forward",
    )(rows, *enc, *dec, *(b.reshape(1, mine) for b in bias))


def backward_kernel(
    factor, error_hbm, dec0, dec1, enc0, enc1, active0, active1, norms0, norms1,
    dpre0, dpre1, sums, through,
    error, dec, enc, back, sem_in, sem_enc, sem_dec,
):
    width, latents = enc.shape
    mine = latents // 2
    steps = width // CHUNK

    def at(k):
        return pl.ds(pl.multiple_of(k * CHUNK, CHUNK), CHUNK)

    def dec_copies(k):
        return (
            pltpu.make_async_copy(error_hbm.at[:, at(k)], error.at[:, at(k)], sem_in.at[k]),
            pltpu.make_async_copy(dec0.at[:, at(k)], dec.at[:mine, at(k)], sem_dec.at[0, k]),
            pltpu.make_async_copy(dec1.at[:, at(k)], dec.at[mine:, at(k)], sem_dec.at[1, k]),
        )

    def enc_copies(k):
        return (
            pltpu.make_async_copy(enc0.at[at(k)], enc.at[at(k), :mine], sem_enc.at[0, k]),
            pltpu.make_async_copy(enc1.at[at(k)], enc.at[at(k), mine:], sem_enc.at[1, k]),
        )

    for copies in (dec_copies, enc_copies):
        for k in range(steps):
            for copy in copies(k):
                copy.start()

    back[...] = jnp.zeros_like(back)

    @pl.loop(0, steps)
    def _(k):
        for copy in dec_copies(k):
            copy.wait()
        back[...] += lax.dot_general(
            error[:, at(k)], dec[:, at(k)], (((1,), (1,)), ((), ())),
            preferred_element_type=f32,
        )

    def finish(columns, norms, active, dpre):
        value = (2.0 * factor * back[:, columns] + 0.5 * factor * norms[...]) * 2.0 * active[...]
        dpre[...] = value.astype(bf16)
        return jnp.sum(value, axis=0, keepdims=True)

    total = jnp.concatenate(
        [
            finish(slice(0, mine), norms0, active0, dpre0),
            finish(slice(mine, latents), norms1, active1, dpre1),
        ],
        axis=1,
    )
    sums[...] = total
    first = total.astype(bf16)
    rest = total - first.astype(f32)
    second = rest.astype(bf16)
    third = (rest - second.astype(f32)).astype(bf16)
    parts = jnp.concatenate(
        [first, second, third, jnp.zeros((13, latents), bf16)], axis=0
    )

    @pl.loop(0, steps)
    def _(k):
        for copy in enc_copies(k):
            copy.wait()
        product = lax.dot_general(
            parts, enc[at(k), :], (((1,), (1,)), ((), ())), preferred_element_type=f32
        )
        through[:, at(k)] = product[0:1] + product[1:2] + product[2:3]


def backward(error, dec, enc, active, norms, factor):
    count, width = error.shape
    mine = enc[0].shape[1]
    steps = width // CHUNK
    half = jax.ShapeDtypeStruct((count, mine), bf16)
    return pl.pallas_call(
        functools.partial(backward_kernel, factor),
        out_shape=(
            half,
            half,
            jax.ShapeDtypeStruct((1, 2 * mine), f32),
            jax.ShapeDtypeStruct((1, width), f32),
        ),
        in_specs=[ANY] * 5 + [VMEM] * 4,
        out_specs=(VMEM,) * 4,
        scratch_shapes=[
            pltpu.VMEM((count, width), bf16),
            pltpu.VMEM((2 * mine, width), bf16),
            pltpu.VMEM((width, 2 * mine), bf16),
            pltpu.VMEM((count, 2 * mine), f32),
            pltpu.SemaphoreType.DMA((steps,)),
            pltpu.SemaphoreType.DMA((2, steps)),
            pltpu.SemaphoreType.DMA((2, steps)),
        ],
        compiler_params=pltpu.CompilerParams(vmem_limit_bytes=VMEM_BYTES),
        cost_estimate=pl.CostEstimate(
            flops=6 * count * width * mine, bytes_accessed=13_000_000, transcendentals=0
        ),
        name="backward",
    )(error, *dec, *enc, *active, *(n.reshape(1, mine) for n in norms))


def per_device(resid_rows, w_encode, b_encode, w_decode, b_decode):
    local_rows, width = resid_rows.shape
    total_rows = local_rows * 16
    half = total_rows // NC
    rows = half // NWIDE
    factor = 1.0 / math.sqrt(total_rows)

    enc = (w_encode, swap(w_encode))
    dec = (w_decode, swap(w_decode))
    bias = (b_encode, swap(b_encode))

    piece = rows // NZH
    at = (lax.axis_index("c") * 2 + lax.axis_index("zl")) * 4 + lax.axis_index("x")
    mine = lax.dynamic_slice_in_dim(resid_rows, at * piece, piece, 0)
    mine = (mine.astype(f32) - b_decode).astype(bf16)
    block = spread(mine, ("zh",), NZH).reshape(rows, width)
    centered = spread(block, WIDE, NWIDE).reshape(half, width)
    dec_float = w_decode.astype(f32)
    norms = jnp.sqrt(jnp.sum(dec_float * dec_float, axis=1) + 1e-06)
    centered, norms, their_norms = lax.optimization_barrier((centered, norms, swap(norms)))

    active0, active1, codes0, codes1, part = forward(centered, enc, bias, dec)
    part = lax.all_to_all(part.reshape(NWIDE, rows, width), WIDE, 0, 0, tiled=True)
    all_codes = jnp.concatenate([codes0, swap(codes1)], axis=0)
    code_sum = jnp.sum(all_codes.astype(f32), axis=0)
    part, all_codes, code_sum, their_rows = lax.optimization_barrier(
        (part, all_codes, code_sum, swap(centered))
    )
    part = jnp.sum(part.astype(f32), axis=0).astype(bf16)
    summed = jnp.sum(spread(part, ("zh",), NZH).astype(f32), axis=0)
    error_block = (summed - block.astype(f32)).astype(bf16)
    error = spread(error_block, WIDE, NWIDE).reshape(half, width)
    block_sum = 2.0 * factor / NZH * jnp.sum(error_block.astype(f32), axis=0)
    error, block_sum = lax.optimization_barrier((error, block_sum))
    dpre0, dpre1, sums, through = backward(
        error, dec, enc, (active0, active1), (norms, their_norms), factor
    )

    mine = w_encode.shape[1]
    all_dpre = jnp.concatenate([dpre0, swap(dpre1)], axis=0)
    all_rows = jnp.concatenate([centered, their_rows], axis=0)
    all_error = jnp.concatenate([error, swap(error)], axis=0)

    through = (through.reshape(width) - block_sum).reshape(width // 128, 128)
    through = through + swap(through)
    through, all_codes = lax.optimization_barrier((through, all_codes))
    through = spread(through, ("zh",), NZH)
    grad_decode = (
        2.0 * factor * jnp.dot(all_codes.T, all_error, preferred_element_type=f32)
        + 0.5 * factor * (code_sum / norms)[:, None] * dec_float
    ).astype(bf16)
    through, grad_decode, all_dpre = lax.optimization_barrier((through, grad_decode, all_dpre))
    through = jnp.sum(spread(jnp.sum(through, axis=0), WIDE, NWIDE), axis=0).reshape(width)
    grad_encode = jnp.dot(all_rows.T, all_dpre, preferred_element_type=f32).astype(bf16)
    grad_b_encode = sums[0, :mine] + swap(sums[0, mine:])
    return (grad_encode, grad_b_encode, grad_decode, -through)


def solution(mesh):
    fine = Mesh(mesh.devices.reshape(2, 4, 2, 4, 4), ("zl", "x", "c", "zh", "y"))
    latents = LMAJ + LMIN
    in_specs = (P(LMIN, None), P(None, latents), P(latents), P(latents, None), P())
    out_specs = (P(None, latents), P(latents), P(latents, None), P())
    return jax.shard_map(
        per_device, mesh=fine, in_specs=in_specs, out_specs=out_specs, check_vma=False
    )
```

time: 192 us -> 175 us (0.911)
  blocking collectives: 65.4 us -> 27 us
  matrix products: 41.9 us -> 11.3 us
  waiting for transfers between devices: 34 us -> 55.8 us
  Pallas kernels: 0 us -> 21 us
  starting transfers between devices: 30.2 us -> 44.5 us
  other arithmetic: 14.7 us -> 5.75 us
  local copies, waits for them, and re-layouts: 3.77 us -> 7.37 us
    dot_general x12 -> x2, matrix products: 41.9 us -> 11.3 us  [the longest x1 5.74 us: per_device(): jnp.dot(all_rows.T, all_dpre, preferred_element_type=f32).astype(bf16)]
    all_to_all x1 -> x0, blocking collectives: 29.2 us -> none  [per_device(): part = lax.all_to_all(part, WIDE, 0, 0, tiled=True)]
    pallas_call x0 -> x2, Pallas kernels: none -> 21 us  [the longest x1 10.8 us: forward(): pl.pallas_call(forward_kernel, out_shape=(flat, flat, half, half, jax.Sha...]
    all_to_all x0 -> x1, waiting for transfers between devices: none -> 14.2 us  [per_device(): lax.all_to_all(part.reshape(NWIDE, rows, width), WIDE, 0, 0, tiled=True)]
    all_to_all x3 -> x2, blocking collectives: 36.2 us -> 27 us  [spread(): lax.all_to_all(jnp.broadcast_to(block[None], (n,) + block.shape), axes, 0...]
    ppermute x7 -> x10, waiting for transfers between devices: 1.67 us -> 10.6 us  [swap(): return lax.ppermute(block, 'c', [(0, 1), (1, 0)])]
    all_to_all x0 -> x1, starting transfers between devices: none -> 7.62 us  [per_device(): lax.all_to_all(part.reshape(NWIDE, rows, width), WIDE, 0, 0, tiled=True)]
    convert_element_type x1 -> x0, other arithmetic: 5.7 us -> none  [per_device(): grad_decode = (decode_part(0) + from_decode.astype(f32)).astype(bf16)]
  transfers between devices with their start and end apart: 10 -> 15, of which waited for: 4 -> 8; matrix products, arithmetic and copies ran while one was open for 15% -> 11% of each run, Pallas kernels for 0% -> 6%
where the time goes in v3:
time: 175 us; the launch traced here: 174 us
  waiting for transfers between devices  55.8 us (32%)
  starting transfers between devices  44.5 us (25%)
  blocking collectives  27 us (15%)
  Pallas kernels  21 us (12%)
  matrix products  11.3 us (6%)
  local copies, waits for them, and re-layouts  7.37 us (4%)
  other arithmetic  5.75 us (3%)
    all_to_all x4, waiting for transfers between devices, spread(): lax.all_to_all(jnp.broadcast_to(block[None], (n,) + block.shape), axes, 0...  31 us
    all_to_all x2, blocking collectives, spread(): lax.all_to_all(jnp.broadcast_to(block[None], (n,) + block.shape), axes, 0...  27 us
    all_to_all x4, starting transfers between devices, spread(): lax.all_to_all(jnp.broadcast_to(block[None], (n,) + block.shape), axes, 0...  22.6 us
    ppermute x10, starting transfers between devices, swap(): return lax.ppermute(block, 'c', [(0, 1), (1, 0)])  14.3 us
    all_to_all x1, waiting for transfers between devices, per_device(): lax.all_to_all(part.reshape(NWIDE, rows, width), WIDE, 0, 0, tiled=True)  14.2 us
    pallas_call x1, Pallas kernels, forward(): pl.pallas_call(forward_kernel, out_shape=(flat, flat, half, half, jax.Sha...  10.8 us
    ppermute x10, waiting for transfers between devices, swap(): return lax.ppermute(block, 'c', [(0, 1), (1, 0)])  10.6 us
    pallas_call x1, Pallas kernels, backward(): pl.pallas_call(functools.partial(backward_kernel, factor), out_shape=(hal...  10.1 us
  transfers between devices with their start and end apart: 15, of which 8 were waited for; matrix products, arithmetic and copies ran while one was open for 11% of the time, Pallas kernels for 6%

profile of v3, /device:TPU:1, one launch (start us, length us, event | category | flops | bytes accessed | tf_op | source)
XLA Modules:
  0.0 173.6 jit_solution(17024117019164585284)
XLA Ops:
  0.6 0.9 subtract_convert_fusion.2
  1.5 15.8 %all_to_all.35 = bf16[4,2,3584]{2,1,0:T(2,128)(2,1)S(1)} all-to-all(bf16[4,2,3584]{2,1,0:T(2,128)(2,1)S(1)} %broadcast_in_dim.14), channel_id=1, replica_groups=mesh['zl'=2,'x'=4,'c'=2,'zh'=4,'y'=4] {'zh'}, dimensions={0} | all-to-all | bytes 114688 | tf_op jit(solution)/shard_map/all_to_all | solution.py:23
  17.4 1.3 broadcast_in_dim.16
  18.7 7.7 %all-to-all-start.1 = ((bf16[32,8,3584]{2,1,0:T(8,128)(2,1)}), bf16[32,8,3584]{2,1,0:T(8,128)(2,1)}, u32[]{:S(2)}, u32[]{:S(2)}) async-start(bf16[32,8,3584]{2,1,0:T(8,128)(2,1)} %broadcast_in_dim.16), calls=%async_computation.1 | async-start | bytes 3670016 | tf_op jit(solution)/shard_map/all_to_all | solution.py:23
  26.5 2.5 %collective-permute-start.1 = (bf16[3584,384]{1,0:T(8,128)(2,1)}, bf16[3584,384]{1,0:T(8,128)(2,1)}, u32[]{:S(2)}, u32[]{:S(2)}) collective-permute-start(bf16[3584,384]{1,0:T(8,128)(2,1)} %enc0.3), channel_id=1, source_target_pairs={{0,16},{16,0},{1,17},{17,1},{2,18},{18,2},{3,19},{19,3},{4,20},{20... | collective-permute-start | bytes 8257544 | tf_op jit(solution)/shard_map/ppermute | solution.py:29
  29.0 0.1 collective-permute-start.2
  29.1 0.4 collective-permute-start.3
  29.5 0.6 fusion.2
  30.1 0.2 collective-permute-start
  30.3 0.6 reshape.57.bias0
  30.9 5.6 %collective-permute-done.3 = f32[384]{0:T(512)S(1)} collective-permute-done((f32[384]{0:T(512)S(1)}, f32[384]{0:T(512)S(1)}, u32[]{:S(2)}, u32[]{:S(2)}) %collective-permute-start.3) | collective-permute-done | bytes 1568 | tf_op jit(solution)/shard_map/ppermute | solution.py:29
  36.5 0.6 reshape.58.bias1
  37.1 10.8 %all-to-all-done.1 = bf16[32,8,3584]{2,1,0:T(8,128)(2,1)} async-done(((bf16[32,8,3584]{2,1,0:T(8,128)(2,1)}), bf16[32,8,3584]{2,1,0:T(8,128)(2,1)}, u32[]{:S(2)}, u32[]{:S(2)}) %all-to-all-start.1) | async-done | bytes 1835040 | tf_op jit(solution)/shard_map/all_to_all | solution.py:23
  47.8 10.8 %forward.1 = (f32[256,384]{1,0:T(8,128)}, f32[256,384]{1,0:T(8,128)}, bf16[256,384]{1,0:T(8,128)(2,1)}, bf16[256,384]{1,0:T(8,128)(2,1)}, bf16[256,3584]{1,0:T(8,128)(2,1)}) custom-call(bf16[256,3584]{1,0:T(8,128)(2,1)} %bitcast.rows_hbm, bf16[3584,384]{1,0:T(8,128)(2,1)} %enc0.3, bf16[3584,384]{1,0:T(8,128)(2,1)} %collective-permute-done.1.enc1, ...), custom_call_target="tpu_custom_call" | custom-call | flops 2818572288 | bytes 13000000 | tf_op jit(solution)/shard_map/forward/pallas_call | solution.py:100
  58.7 7.6 %all-to-all-start.2 = ((bf16[32,8,3584]{2,1,0:T(8,128)(2,1)}), bf16[32,8,3584]{2,1,0:T(8,128)(2,1)S(1)}, u32[]{:S(2)}, u32[]{:S(2)}) async-start(bf16[32,8,3584]{2,1,0:T(8,128)(2,1)} %bitcast.11), calls=%async_computation.2 | async-start | bytes 3670016 | tf_op jit(solution)/shard_map/all_to_all | solution.py:251
  66.3 2.6 %collective-permute-start.5 = (bf16[256,3584]{1,0:T(8,128)(2,1)}, bf16[256,3584]{1,0:T(8,128)(2,1)}, u32[]{:S(2)}, u32[]{:S(2)}) collective-permute-start(bf16[256,3584]{1,0:T(8,128)(2,1)} %bitcast.rows_hbm), channel_id=1, source_target_pairs={{0,16},{16,0},{1,17},{17,1},{2,18},{18,2},{3,19},{19,3},{4,20},{20... | collective-permute-start | bytes 5505032 | tf_op jit(solution)/shard_map/ppermute | solution.py:29
  68.9 0.1 collective-permute-start.4
  69.1 3.4 %collective-permute-done.4 = bf16[256,384]{1,0:T(8,128)(2,1)S(1)} collective-permute-done((bf16[256,384]{1,0:T(8,128)(2,1)S(1)}, bf16[256,384]{1,0:T(8,128)(2,1)S(1)}, u32[]{:S(2)}, u32[]{:S(2)}) %collective-permute-start.4) | collective-permute-done | bytes 196640 | tf_op jit(solution)/shard_map/ppermute | solution.py:29
  72.5 0.1 convert_reduce_fusion
  72.6 0.7 copy-done.2
  73.3 14.2 %all-to-all-done.2 = bf16[32,8,3584]{2,1,0:T(8,128)(2,1)S(1)} async-done(((bf16[32,8,3584]{2,1,0:T(8,128)(2,1)}), bf16[32,8,3584]{2,1,0:T(8,128)(2,1)S(1)}, u32[]{:S(2)}, u32[]{:S(2)}) %all-to-all-start.2) | async-done | bytes 1835040 | tf_op jit(solution)/shard_map/all_to_all | solution.py:251
  87.5 0.3 reduce_sum.70
  87.8 11.2 %all_to_all.36 = bf16[4,8,3584]{2,1,0:T(8,128)(2,1)S(1)} all-to-all(bf16[4,8,3584]{2,1,0:T(8,128)(2,1)S(1)} %broadcast_in_dim.17), channel_id=1, replica_groups=mesh['zl'=2,'x'=4,'c'=2,'zh'=4,'y'=4] {'zh'}, dimensions={0} | all-to-all | bytes 458752 | tf_op jit(solution)/shard_map/all_to_all | solution.py:23
  99.1 1.3 broadcast_in_dim.18
  100.4 6.7 %all-to-all-start.4 = ((bf16[32,8,3584]{2,1,0:T(8,128)(2,1)}), bf16[32,8,3584]{2,1,0:T(8,128)(2,1)}, u32[]{:S(2)}, u32[]{:S(2)}) async-start(bf16[32,8,3584]{2,1,0:T(8,128)(2,1)} %broadcast_in_dim.18), calls=%async_computation.4 | async-start | bytes 3670016 | tf_op jit(solution)/shard_map/all_to_all | solution.py:23
  107.1 0.1 reduce_sum.72
  107.2 0.1 convert_reduce_fusion.2
  107.3 19.9 %all-to-all-done.4 = bf16[32,8,3584]{2,1,0:T(8,128)(2,1)} async-done(((bf16[32,8,3584]{2,1,0:T(8,128)(2,1)}), bf16[32,8,3584]{2,1,0:T(8,128)(2,1)}, u32[]{:S(2)}, u32[]{:S(2)}) %all-to-all-start.4) | async-done | bytes 1835040 | tf_op jit(solution)/shard_map/all_to_all | solution.py:23
  127.2 6.1 %collective-permute-start.7 = (bf16[256,3584]{1,0:T(8,128)(2,1)}, bf16[256,3584]{1,0:T(8,128)(2,1)}, u32[]{:S(2)}, u32[]{:S(2)}) collective-permute-start(bf16[256,3584]{1,0:T(8,128)(2,1)} %bitcast.2.error_hbm), channel_id=1, source_target_pairs={{0,16},{16,0},{1,17},{17,1},{2,18},{18,2},{3,19},{19,3},{4,20},{20... | collective-permute-start | bytes 5505032 | tf_op jit(solution)/shard_map/ppermute | solution.py:29
  133.3 0.6 reshape.62.norms1
  133.9 0.6 reshape.61.norms0
  134.4 10.1 %backward.1 = (bf16[256,384]{1,0:T(8,128)(2,1)}, bf16[256,384]{1,0:T(8,128)(2,1)}, f32[1,768]{1,0:T(1,128)}, f32[1,3584]{1,0:T(1,128)}) custom-call(bf16[256,3584]{1,0:T(8,128)(2,1)} %bitcast.2.error_hbm, bf16[384,3584]{1,0:T(8,128)(2,1)} %dec0.3, bf16[384,3584]{1,0:T(8,128)(2,1)} %collective-permute-done.2.dec1, bf16[3584,384]{1,0:T(8,128)(2,1)} %enc0.3, ...), custom_call_target="tpu_custom_call" | custom-call | flops 2113929216 | bytes 13000000 | tf_op jit(solution)/shard_map/backward/pallas_call | solution.py:202
  144.6 0.8 reduce.2
  145.3 0.1 collective-permute-start.6
  145.5 0.5 collective-permute-start.8
  145.9 0.7 collective-permute-done.6
  146.6 0.6 broadcast_in_dim.19
  147.3 3.3 %all-to-all-start.5 = ((f32[4,28,128]{2,1,0:T(8,128)}), f32[4,28,128]{2,1,0:T(8,128)S(1)}, u32[]{:S(2)}, u32[]{:S(2)}) async-start(f32[4,28,128]{2,1,0:T(8,128)} %broadcast_in_dim.19), calls=%async_computation.5 | async-start | bytes 131072 | tf_op jit(solution)/shard_map/all_to_all | solution.py:23
  150.6 1.7 %pad_maximum_fusion = bf16[512,384]{1,0:T(8,128)(2,1)} fusion(bf16[256,384]{1,0:T(8,128)(2,1)S(1)} %collective-permute-done.8, bf16[256,384]{1,0:T(8,128)(2,1)} %get-tuple-element.44), kind=kLoop, calls=%fused_computation.15 | loop fusion | flops 786432 | bytes 786432 | tf_op jit(solution)/shard_map/concatenate | solution.py:268
  152.3 5.6 %fusion.1 = bf16[384,3584]{1,0:T(8,128)(2,1)} fusion(bf16[512,384]{1,0:T(8,128)(2,1)} %copy-done.2, bf16[384,3584]{1,0:T(8,128)(2,1)S(1)} %copy-done.1, bf16[256,3584]{1,0:T(8,128)(2,1)} %collective-permute-done.7, bf16[256,3584]{1,0:T(8,128)(2,1)} %bitcast.2.error_hbm, f32[384]{0:T(512)S(1)} %divide_multiply_fusion), kind=kOutput, calls=%fused_computation.5 | convolution fusion | flops 1423507456 | bytes 9569792 | tf_op jit(solution)/shard_map/dot_general | solution.py:277
  157.9 0.8 broadcast_in_dim.20
  158.7 4.9 %all-to-all-start.6 = ((f32[32,28,128]{2,1,0:T(8,128)}), f32[32,28,128]{2,1,0:T(8,128)S(1)}, u32[]{:S(2)}, u32[]{:S(2)}) async-start(f32[32,28,128]{2,1,0:T(8,128)} %broadcast_in_dim.20), calls=%async_computation.6 | async-start | bytes 1048576 | tf_op jit(solution)/shard_map/all_to_all | solution.py:23
  163.7 1.7 collective-permute-start.9
  165.4 0.8 collective-permute-done.9
  166.2 0.6 add.31
  166.8 5.7 %convolution_convert_fusion = bf16[3584,384]{1,0:T(8,128)(2,1)} fusion(bf16[512,384]{1,0:T(8,128)(2,1)} %pad_maximum_fusion, bf16[256,3584]{1,0:T(8,128)(2,1)} %collective-permute-done.5, bf16[256,3584]{1,0:T(8,128)(2,1)} %bitcast.rows_hbm), kind=kOutput, calls=%fused_computation.4 | convolution fusion | flops 1418002432 | bytes 6815744 | tf_op jit(solution)/shard_map/dot_general | solution.py:282
  172.5 0.4 all-to-all-done.6
  173.0 0.6 negate_bitcast_fusion
  (35 shorter events, 0.3 us)
Async XLA Ops:
  17.4 11.6 %copy-start = (bf16[384,3584]{1,0:T(8,128)(2,1)S(1)}, bf16[384,3584]{1,0:T(8,128)(2,1)}, u32[]{:S(2)}) copy-start(bf16[384,3584]{1,0:T(8,128)(2,1)} %dec0.3) | copy-start | bytes 8257540
  17.4 11.7 %copy-start.5 = (f32[384]{0:T(512)S(1)}, f32[384]{0:T(512)}, u32[]{:S(2)}) copy-start(f32[384]{0:T(512)} %param.7) | copy-start | bytes 4612
  18.7 29.1 %all-to-all-start.1 = ((bf16[32,8,3584]{2,1,0:T(8,128)(2,1)}), bf16[32,8,3584]{2,1,0:T(8,128)(2,1)}, u32[]{:S(2)}, u32[]{:S(2)}) async-start(bf16[32,8,3584]{2,1,0:T(8,128)(2,1)} %broadcast_in_dim.16), calls=%async_computation.1 | async-start | bytes 3670016 | tf_op jit(solution)/shard_map/all_to_all | solution.py:23
  26.5 21.3 %collective-permute-start.1 = (bf16[3584,384]{1,0:T(8,128)(2,1)}, bf16[3584,384]{1,0:T(8,128)(2,1)}, u32[]{:S(2)}, u32[]{:S(2)}) collective-permute-start(bf16[3584,384]{1,0:T(8,128)(2,1)} %enc0.3), channel_id=1, source_target_pairs={{0,16},{16,0},{1,17},{17,1},{2,18},{18,2},{3,19},{19,3},{4,20},{20... | collective-permute-start | bytes 8257544 | tf_op jit(solution)/shard_map/ppermute | solution.py:29
  29.0 18.9 %collective-permute-start.2 = (bf16[384,3584]{1,0:T(8,128)(2,1)S(1)}, bf16[384,3584]{1,0:T(8,128)(2,1)}, u32[]{:S(2)}, u32[]{:S(2)}) collective-permute-start(bf16[384,3584]{1,0:T(8,128)(2,1)S(1)} %copy-done), channel_id=1, source_target_pairs={{0,16},{16,0},{1,17},{17,1},{2,18},{18,2},{3,19},{19,3},{4,20},{20... | collective-permute-start | bytes 8257544 | tf_op jit(solution)/shard_map/ppermute | solution.py:29
  29.1 7.4 %collective-permute-start.3 = (f32[384]{0:T(512)S(1)}, f32[384]{0:T(512)S(1)}, u32[]{:S(2)}, u32[]{:S(2)}) collective-permute-start(f32[384]{0:T(512)S(1)} %copy-done.5), channel_id=1, source_target_pairs={{0,16},{16,0},{1,17},{17,1},{2,18},{18,2},{3,19},{19,3},{4,20},{20... | collective-permute-start | bytes 4616 | tf_op jit(solution)/shard_map/ppermute | solution.py:29
  30.1 7.0 %collective-permute-start = (f32[384]{0:T(512)S(1)}, f32[384]{0:T(512)S(1)}, u32[]{:S(2)}, u32[]{:S(2)}) collective-permute-start(f32[384]{0:T(512)S(1)} %add_sqrt_fusion), channel_id=1, source_target_pairs={{0,16},{16,0},{1,17},{17,1},{2,18},{18,2},{3,19},{19,3},{4,20},{20... | collective-permute-start | bytes 4616 | tf_op jit(solution)/shard_map/ppermute | solution.py:29
  58.7 10.2 %copy-start.6 = (bf16[256,384]{1,0:T(8,128)(2,1)S(1)}, bf16[256,384]{1,0:T(8,128)(2,1)}, u32[]{:S(2)}) copy-start(bf16[256,384]{1,0:T(8,128)(2,1)} %get-tuple-element.30) | copy-start | bytes 589828
  58.7 10.4 %copy-start.3 = (bf16[256,384]{1,0:T(8,128)(2,1)S(1)}, bf16[256,384]{1,0:T(8,128)(2,1)}, u32[]{:S(2)}) copy-start(bf16[256,384]{1,0:T(8,128)(2,1)} %get-tuple-element.29) | copy-start | bytes 589828
  58.7 28.8 %all-to-all-start.2 = ((bf16[32,8,3584]{2,1,0:T(8,128)(2,1)}), bf16[32,8,3584]{2,1,0:T(8,128)(2,1)S(1)}, u32[]{:S(2)}, u32[]{:S(2)}) async-start(bf16[32,8,3584]{2,1,0:T(8,128)(2,1)} %bitcast.11), calls=%async_computation.2 | async-start | bytes 3670016 | tf_op jit(solution)/shard_map/all_to_all | solution.py:251
  66.3 7.0 %collective-permute-start.5 = (bf16[256,3584]{1,0:T(8,128)(2,1)}, bf16[256,3584]{1,0:T(8,128)(2,1)}, u32[]{:S(2)}, u32[]{:S(2)}) collective-permute-start(bf16[256,3584]{1,0:T(8,128)(2,1)} %bitcast.rows_hbm), channel_id=1, source_target_pairs={{0,16},{16,0},{1,17},{17,1},{2,18},{18,2},{3,19},{19,3},{4,20},{20... | collective-permute-start | bytes 5505032 | tf_op jit(solution)/shard_map/ppermute | solution.py:29
  68.9 3.6 %collective-permute-start.4 = (bf16[256,384]{1,0:T(8,128)(2,1)S(1)}, bf16[256,384]{1,0:T(8,128)(2,1)S(1)}, u32[]{:S(2)}, u32[]{:S(2)}) collective-permute-start(bf16[256,384]{1,0:T(8,128)(2,1)S(1)} %copy-done.6), channel_id=1, source_target_pairs={{0,16},{16,0},{1,17},{17,1},{2,18},{18,2},{3,19},{19,3},{4,20},{20... | collective-permute-start | bytes 589832 | tf_op jit(solution)/shard_map/ppermute | solution.py:29
  72.5 0.8 copy-start.2
  100.4 26.8 %all-to-all-start.4 = ((bf16[32,8,3584]{2,1,0:T(8,128)(2,1)}), bf16[32,8,3584]{2,1,0:T(8,128)(2,1)}, u32[]{:S(2)}, u32[]{:S(2)}) async-start(bf16[32,8,3584]{2,1,0:T(8,128)(2,1)} %broadcast_in_dim.18), calls=%async_computation.4 | async-start | bytes 3670016 | tf_op jit(solution)/shard_map/all_to_all | solution.py:23
  127.2 25.1 %collective-permute-start.7 = (bf16[256,3584]{1,0:T(8,128)(2,1)}, bf16[256,3584]{1,0:T(8,128)(2,1)}, u32[]{:S(2)}, u32[]{:S(2)}) collective-permute-start(bf16[256,3584]{1,0:T(8,128)(2,1)} %bitcast.2.error_hbm), channel_id=1, source_target_pairs={{0,16},{16,0},{1,17},{17,1},{2,18},{18,2},{3,19},{19,3},{4,20},{20... | collective-permute-start | bytes 5505032 | tf_op jit(solution)/shard_map/ppermute | solution.py:29
  134.4 17.9 %copy-start.1 = (bf16[384,3584]{1,0:T(8,128)(2,1)S(1)}, bf16[384,3584]{1,0:T(8,128)(2,1)}, u32[]{:S(2)}) copy-start(bf16[384,3584]{1,0:T(8,128)(2,1)} %dec0.3) | copy-start | bytes 8257540
  145.3 1.3 collective-permute-start.6
  145.5 5.1 %collective-permute-start.8 = (bf16[256,384]{1,0:T(8,128)(2,1)}, bf16[256,384]{1,0:T(8,128)(2,1)S(1)}, u32[]{:S(2)}, u32[]{:S(2)}) collective-permute-start(bf16[256,384]{1,0:T(8,128)(2,1)} %get-tuple-element.45), channel_id=1, source_target_pairs={{0,16},{16,0},{1,17},{17,1},{2,18},{18,2},{3,19},{19,3},{4,20},{20... | collective-permute-start | bytes 589832 | tf_op jit(solution)/shard_map/ppermute | solution.py:29
  147.3 10.6 %all-to-all-start.5 = ((f32[4,28,128]{2,1,0:T(8,128)}), f32[4,28,128]{2,1,0:T(8,128)S(1)}, u32[]{:S(2)}, u32[]{:S(2)}) async-start(f32[4,28,128]{2,1,0:T(8,128)} %broadcast_in_dim.19), calls=%async_computation.5 | async-start | bytes 131072 | tf_op jit(solution)/shard_map/all_to_all | solution.py:23
  152.3 11.4 %copy-start.4 = (f32[1,768]{1,0:T(1,128)S(1)}, f32[1,768]{1,0:T(1,128)}, u32[]{:S(2)}) copy-start(f32[1,768]{1,0:T(1,128)} %get-tuple-element.47) | copy-start | bytes 9220
  158.7 14.2 %all-to-all-start.6 = ((f32[32,28,128]{2,1,0:T(8,128)}), f32[32,28,128]{2,1,0:T(8,128)S(1)}, u32[]{:S(2)}, u32[]{:S(2)}) async-start(f32[32,28,128]{2,1,0:T(8,128)} %broadcast_in_dim.20), calls=%async_computation.6 | async-start | bytes 1048576 | tf_op jit(solution)/shard_map/all_to_all | solution.py:23
  163.7 2.5 %collective-permute-start.9 = (f32[384]{0:T(512)S(1)}, f32[384]{0:T(512)S(1)}, u32[]{:S(2)}, u32[]{:S(2)}) collective-permute-start(f32[384]{0:T(512)S(1)} %get-tuple-element.50), channel_id=1, source_target_pairs={{0,16},{16,0},{1,17},{17,1},{2,18},{18,2},{3,19},{19,3},{4,20},{20... | collective-permute-start | bytes 4616 | tf_op jit(solution)/shard_map/ppermute | solution.py:29

commit v4 on v2

v4 whole, which is shorter than its diff:
```python
import math

import jax
import jax.numpy as jnp
from jax import lax
from jax.sharding import Mesh, PartitionSpec as P

LMAJ = ("zl", "x", "c")
LMIN = ("zh", "y")
WIDE, NWIDE = ("zl", "x", "y"), 32
XY, NXY = ("x", "y"), 16
Z, NZ = ("zl", "zh"), 8
ZH, NZH = ("zh",), 4
f32, bf16 = jnp.float32, jnp.bfloat16


def spread(block, axes, n):
    return lax.all_to_all(
        jnp.broadcast_to(block[None], (n,) + block.shape), axes, 0, 0, tiled=True
    )


def swap(block):
    return lax.ppermute(block, "c", [(0, 1), (1, 0)])


def tie(*values):
    return lax.optimization_barrier(values)


def per_device(resid_rows, w_encode, b_encode, w_decode, b_decode):
    local_rows, width = resid_rows.shape
    total_rows = local_rows * 16
    half = total_rows // 2
    rows = half // NWIDE
    factor = 1.0 / math.sqrt(total_rows)

    piece = rows // NZH
    at = (lax.axis_index("c") * 2 + lax.axis_index("zl")) * 4 + lax.axis_index("x")
    block = lax.dynamic_slice_in_dim(resid_rows, at * piece, piece, 0)
    block = (block.astype(f32) - b_decode).astype(bf16)
    block = spread(block, ZH, NZH).reshape(rows, width)
    dec_float = w_decode.astype(f32)
    norms = jnp.sqrt(jnp.sum(dec_float * dec_float, axis=1) + 1e-06)
    slope0 = 0.5 * factor * norms
    block, norms, slope0, slope1, bias1, enc1, dec1 = tie(
        block, norms, slope0, swap(slope0), swap(b_encode), swap(w_encode), swap(w_decode)
    )
    centered = spread(block, WIDE, NWIDE).reshape(half, width)

    def encode(w, b):
        active = jnp.maximum(jnp.dot(centered, w, preferred_element_type=f32) + b, 0.0)
        return active, (active * active).astype(bf16)

    active1, codes1 = encode(enc1, bias1)
    active0, codes0 = encode(w_encode, b_encode)
    part = jnp.dot(codes1, dec1, preferred_element_type=f32) + jnp.dot(
        codes0, w_decode, preferred_element_type=f32
    )
    part = part.astype(bf16).reshape(NWIDE, rows, width)
    part, their_rows, their_codes = tie(part, swap(centered), swap(codes1))
    part = lax.all_to_all(part, WIDE, 0, 0, tiled=True)
    part = jnp.sum(part.astype(f32), axis=0).astype(bf16)
    summed = jnp.sum(spread(part, ZH, NZH).astype(f32), axis=0)
    error_block = (summed - block.astype(f32)).astype(bf16)
    block_sum = 2.0 * factor / NZH * jnp.sum(error_block.astype(f32), axis=0)
    error_block, block_sum = tie(error_block, block_sum)
    error = spread(error_block, WIDE, NWIDE).reshape(half, width)

    def backward(w, slope, active):
        back = 2.0 * factor * jnp.dot(error, w.T, preferred_element_type=f32) + slope
        dpre = back * 2.0 * active
        return dpre.astype(bf16), jnp.sum(dpre, axis=0)

    def times(w, vector):
        first = lax.reduce_precision(vector, 8, 7)
        second = lax.reduce_precision(vector - first, 8, 7)
        third = vector - first - second
        parts = jnp.stack([first, second, third] + [jnp.zeros_like(vector)] * 5).astype(bf16)
        product = lax.dot_general(
            parts, w, (((1,), (1,)), ((), ())), preferred_element_type=f32
        )
        return product[0] + product[1] + product[2]

    dpre1, sums1 = backward(dec1, slope1, active1)
    dpre0, sums0 = backward(w_decode, slope0, active0)
    through = times(w_encode, sums0) + times(enc1, sums1) - block_sum
    through = through.reshape(width // 128, 128)
    through = through + swap(through)

    all_codes = jnp.concatenate([codes0, their_codes], axis=0)
    all_dpre = jnp.concatenate([dpre0, swap(dpre1)], axis=0)
    all_rows = jnp.concatenate([centered, their_rows], axis=0)
    all_error = jnp.concatenate([error, swap(error)], axis=0)
    through, all_codes, all_dpre = tie(through, all_codes, all_dpre)
    code_sum = jnp.sum(all_codes.astype(f32), axis=0)
    through = spread(through, Z, NZ)
    grad_decode = (
        2.0 * factor * jnp.dot(all_codes.T, all_error, preferred_element_type=f32)
        + 0.5 * factor * (code_sum / norms)[:, None] * dec_float
    ).astype(bf16)
    through, grad_decode, all_dpre = tie(through, grad_decode, all_dpre)
    through = jnp.sum(spread(jnp.sum(through, axis=0), XY, NXY), axis=0).reshape(width)
    grad_encode = jnp.dot(all_rows.T, all_dpre, preferred_element_type=f32).astype(bf16)
    grad_b_encode = sums0 + swap(sums1)
    return (grad_encode, grad_b_encode, grad_decode, -through)


def solution(mesh):
    fine = Mesh(mesh.devices.reshape(2, 4, 2, 4, 4), ("zl", "x", "c", "zh", "y"))
    latents = LMAJ + LMIN
    in_specs = (P(LMIN, None), P(None, latents), P(latents), P(latents, None), P())
    out_specs = (P(None, latents), P(latents), P(latents, None), P())
    return jax.shard_map(
        per_device, mesh=fine, in_specs=in_specs, out_specs=out_specs, check_vma=False
    )
```

time: 192 us -> 178 us (0.927)
  blocking collectives: 65.4 us -> 96.4 us
  waiting for transfers between devices: 34 us -> 5.51 us
  matrix products: 41.9 us -> 30.7 us
  other arithmetic: 14.7 us -> 10 us
  starting transfers between devices: 30.2 us -> 27.9 us
    all_to_all x3, blocking collectives: 36.2 us -> 68.8 us  [spread(): lax.all_to_all(jnp.broadcast_to(block[None], (n,) + block.shape), axes, 0...]
    all_to_all x3, waiting for transfers between devices: 32.3 us -> 5.49 us  [spread(): lax.all_to_all(jnp.broadcast_to(block[None], (n,) + block.shape), axes, 0...]
    dot_general x12 -> x10, matrix products: 41.9 us -> 30.7 us  [the longest x2 8.07 us: backward(): jnp.dot(error, w.T, preferred_element_type=f32)]
    convert_element_type x3 -> x1, other arithmetic: 6.58 us -> 0.86 us  [per_device(): block = (block.astype(f32) - b_decode).astype(bf16)]
    all_to_all x3, starting transfers between devices: 17.3 us -> 13.5 us  [spread(): lax.all_to_all(jnp.broadcast_to(block[None], (n,) + block.shape), axes, 0...]
    reduce_sum x8 -> x6, other arithmetic: 5.08 us -> 2.61 us  [the longest x1 2.39 us: per_device(): norms = jnp.sqrt(jnp.sum(dec_float * dec_float, axis=1) + 1e-06)]
    ppermute x7 -> x10, starting transfers between devices: 12.9 us -> 14.4 us  [swap(): return lax.ppermute(block, 'c', [(0, 1), (1, 0)])]
  transfers between devices with their start and end apart: 10 -> 13, of which waited for: 4 -> 3; matrix products, arithmetic and copies ran while one was open for 15% -> 20% of each run, Pallas kernels for 0% -> 0%
where the time goes in v4:
time: 178 us; the launch traced here: 176 us
  blocking collectives  96.4 us (54%)
  matrix products  30.7 us (17%)
  starting transfers between devices  27.9 us (16%)
  other arithmetic  10 us (6%)
  waiting for transfers between devices  5.51 us (3%)
  local copies, waits for them, and re-layouts  4.28 us (2%)
    all_to_all x3, blocking collectives, spread(): lax.all_to_all(jnp.broadcast_to(block[None], (n,) + block.shape), axes, 0...  68.8 us
    all_to_all x1, blocking collectives, per_device(): part = lax.all_to_all(part, WIDE, 0, 0, tiled=True)  27.6 us
    ppermute x10, starting transfers between devices, swap(): return lax.ppermute(block, 'c', [(0, 1), (1, 0)])  14.4 us
    all_to_all x3, starting transfers between devices, spread(): lax.all_to_all(jnp.broadcast_to(block[None], (n,) + block.shape), axes, 0...  13.5 us
    dot_general x2, matrix products, backward(): jnp.dot(error, w.T, preferred_element_type=f32)  8.07 us
    dot_general x1, matrix products, per_device(): jnp.dot(all_rows.T, all_dpre, preferred_element_type=f32).astype(bf16)  5.74 us
    all_to_all x3, waiting for transfers between devices, spread(): lax.all_to_all(jnp.broadcast_to(block[None], (n,) + block.shape), axes, 0...  5.49 us
    dot_general x1, matrix products, per_device(): jnp.dot(all_codes.T, all_error, preferred_element_type=f32)  5.43 us
  transfers between devices with their start and end apart: 13, of which 3 were waited for; matrix products, arithmetic and copies ran while one was open for 20% of the time, Pallas kernels for 0%

profile of v4, /device:TPU:1, one launch (start us, length us, event | category | flops | bytes accessed | tf_op | source)
XLA Modules:
  0.0 175.7 jit_solution(11713536185187111712)
XLA Ops:
  0.6 3.3 %collective-permute-start.2 = (bf16[3584,384]{1,0:T(8,128)(2,1)}, bf16[3584,384]{1,0:T(8,128)(2,1)S(1)}, u32[]{:S(2)}, u32[]{:S(2)}) collective-permute-start(bf16[3584,384]{1,0:T(8,128)(2,1)} %param.6), channel_id=1, source_target_pairs={{0,16},{16,0},{1,17},{17,1},{2,18},{18,2},{3,19},{19,3},{4,20},{20... | collective-permute-start | bytes 8257544 | tf_op jit(solution)/shard_map/ppermute | solution.py:24
  4.0 0.1 collective-permute-start.3
  4.1 0.9 subtract_convert_fusion.1
  4.9 0.7 broadcast_in_dim.12
  5.6 6.4 %all-to-all-start = ((bf16[4,2,3584]{2,1,0:T(2,128)(2,1)}), bf16[4,2,3584]{2,1,0:T(2,128)(2,1)S(1)}, u32[]{:S(2)}, u32[]{:S(2)}) async-start(bf16[4,2,3584]{2,1,0:T(2,128)(2,1)} %broadcast_in_dim.12), calls=%async_computation | async-start | bytes 114688 | tf_op jit(solution)/shard_map/all_to_all | solution.py:18
  12.0 2.4 %fusion.2 = f32[384]{0:T(512)S(1)} fusion(bf16[384,3584]{1,0:T(8,128)(2,1)} %param.8), kind=kLoop, calls=%fused_computation.7 | loop fusion | flops 4128384 | bytes 2754048 | tf_op jit(solution)/shard_map/reduce_sum | solution.py:44
  14.4 0.6 broadcast_multiply_fusion.1
  15.0 0.7 collective-permute-start
  15.7 3.2 %all-to-all-done = bf16[4,2,3584]{2,1,0:T(2,128)(2,1)S(1)} async-done(((bf16[4,2,3584]{2,1,0:T(2,128)(2,1)}), bf16[4,2,3584]{2,1,0:T(2,128)(2,1)S(1)}, u32[]{:S(2)}, u32[]{:S(2)}) %all-to-all-start) | async-done | bytes 57376 | tf_op jit(solution)/shard_map/all_to_all | solution.py:18
  19.0 0.1 broadcast_in_dim.13
  19.1 29.3 %all_to_all.35 = bf16[32,8,3584]{2,1,0:T(8,128)(2,1)S(1)} all-to-all(bf16[32,8,3584]{2,1,0:T(8,128)(2,1)S(1)} %broadcast_in_dim.13), channel_id=1, replica_groups=mesh['zl'=2,'x'=4,'c'=2,'zh'=4,'y'=4] {'zl','x','y'}, dimensions={0} | all-to-all | bytes 3670016 | tf_op jit(solution)/shard_map/all_to_all | solution.py:18
  48.4 4.1 %collective-permute-start.4 = (bf16[256,3584]{1,0:T(8,128)(2,1)S(1)}, bf16[256,3584]{1,0:T(8,128)(2,1)S(1)}, u32[]{:S(2)}, u32[]{:S(2)}) collective-permute-start(bf16[256,3584]{1,0:T(8,128)(2,1)S(1)} %bitcast.40), channel_id=1, source_target_pairs={{0,16},{16,0},{1,17},{17,1},{2,18},{18,2},{3,19},{19,3},{4,20},{20... | collective-permute-start | bytes 5505032 | tf_op jit(solution)/shard_map/ppermute | solution.py:24
  52.5 1.9 %multiply_convert_fusion.1 = (bf16[256,384]{1,0:T(8,128)(2,1)S(1)}, f32[256,384]{1,0:T(8,128)}) fusion(f32[384]{0:T(512)S(1)} %collective-permute-done.1, bf16[3584,384]{1,0:T(8,128)(2,1)S(1)} %collective-permute-done.2, bf16[32,8,3584]{2,1,0:T(8,128)(2,1)S(1)} %all_to_all.35), kind=kOutput, calls=%fused_computation.31 | convolution fusion | flops 705036288 | bytes 5178880 | tf_op jit(solution)/shard_map/dot_general | solution.py:52
  54.5 0.0 collective-permute-start.5
  54.5 2.0 %multiply_convert_fusion = (bf16[256,384]{1,0:T(8,128)(2,1)S(1)}, f32[256,384]{1,0:T(8,128)}) fusion(f32[384]{0:T(512)S(1)} %copy-done.10, bf16[3584,384]{1,0:T(8,128)(2,1)S(1)} %copy-done.1, bf16[32,8,3584]{2,1,0:T(8,128)(2,1)S(1)} %all_to_all.35), kind=kOutput, calls=%fused_computation.30 | convolution fusion | flops 705036288 | bytes 5178880 | tf_op jit(solution)/shard_map/dot_general | solution.py:52
  56.4 1.1 fusion.28
  57.6 2.9 %fusion.4 = bf16[32,8,3584]{2,1,0:T(8,128)(2,1)S(1)} fusion(f32[256,3584]{1,0:T(8,128)S(1)} %fusion.28, bf16[256,384]{1,0:T(8,128)(2,1)S(1)} %get-tuple-element.56, bf16[384,3584]{1,0:T(8,128)(2,1)} %collective-permute-done.3), kind=kOutput, calls=%fused_computation.9 | convolution fusion | flops 706478080 | bytes 8454144 | tf_op jit(solution)/shard_map/dot_general | solution.py:57
  60.5 1.2 copy-done.8
  61.8 27.6 %all_to_all.36 = bf16[32,8,3584]{2,1,0:T(8,128)(2,1)} all-to-all(bf16[32,8,3584]{2,1,0:T(8,128)(2,1)S(1)} %fusion.4), channel_id=1, replica_groups=mesh['zl'=2,'x'=4,'c'=2,'zh'=4,'y'=4] {'zl','x','y'}, dimensions={0} | all-to-all | bytes 3670016 | tf_op jit(solution)/shard_map/all_to_all | solution.py:62
  89.4 1.8 reduce_sum.89
  91.2 13.3 %all_to_all.37 = bf16[4,8,3584]{2,1,0:T(8,128)(2,1)S(1)} all-to-all(bf16[4,8,3584]{2,1,0:T(8,128)(2,1)S(1)} %broadcast_in_dim.14), channel_id=1, replica_groups=mesh['zl'=2,'x'=4,'c'=2,'zh'=4,'y'=4] {'zh'}, dimensions={0} | all-to-all | bytes 458752 | tf_op jit(solution)/shard_map/all_to_all | solution.py:18
  104.6 0.0 copy-start.11
  104.7 0.1 broadcast_in_dim.15
  104.8 26.1 %all_to_all.38 = bf16[32,8,3584]{2,1,0:T(8,128)(2,1)} all-to-all(bf16[32,8,3584]{2,1,0:T(8,128)(2,1)S(1)} %broadcast_in_dim.15), channel_id=1, replica_groups=mesh['zl'=2,'x'=4,'c'=2,'zh'=4,'y'=4] {'zl','x','y'}, dimensions={0} | all-to-all | bytes 3670016 | tf_op jit(solution)/shard_map/all_to_all | solution.py:18
  130.9 4.7 %fusion.27 = (bf16[256,384]{1,0:T(8,128)(2,1)}, f32[384]{0:T(512)}) fusion(f32[256,384]{1,0:T(8,128)S(1)} %copy-done.11, f32[384]{0:T(512)S(1)} %collective-permute-done, bf16[384,3584]{1,0:T(8,128)(2,1)} %collective-permute-done.3, bf16[32,8,3584]{2,1,0:T(8,128)(2,1)} %all_to_all.38), kind=kOutput, calls=%fused_computation.64 | convolution fusion | flops 705232512 | bytes 5180416 | tf_op jit(solution)/shard_map/dot_general | solution.py:71
  135.6 0.7 fusion.19
  136.3 5.2 %collective-permute-start.9 = (f32[384]{0:T(512)}, f32[384]{0:T(512)}, u32[]{:S(2)}, u32[]{:S(2)}) collective-permute-start(f32[384]{0:T(512)} %get-tuple-element.45), channel_id=1, source_target_pairs={{0,16},{16,0},{1,17},{17,1},{2,18},{18,2},{3,19},{19,3},{4,20},{20... | collective-permute-start | bytes 4616 | tf_op jit(solution)/shard_map/ppermute | solution.py:24
  141.5 0.3 collective-permute-start.8
  141.8 3.4 %fusion.26 = (bf16[256,384]{1,0:T(8,128)(2,1)}, f32[384]{0:T(512)S(1)}) fusion(f32[256,384]{1,0:T(8,128)} %get-tuple-element.55, f32[384]{0:T(512)S(1)} %get-tuple-element.29, bf16[384,3584]{1,0:T(8,128)(2,1)S(1)} %copy-done, bf16[32,8,3584]{2,1,0:T(8,128)(2,1)} %all_to_all.38), kind=kOutput, calls=%fused_computation.63 | convolution fusion | flops 705232512 | bytes 5180416 | tf_op jit(solution)/shard_map/dot_general | solution.py:71
  145.2 0.6 copy-done.6
  145.8 2.7 %fusion.30 = f32[8,3584]{1,0:T(8,128)S(1)} fusion(bf16[8,384]{1,0:T(8,128)(2,1)S(1)} %stack.7, bf16[3584,384]{1,0:T(8,128)(2,1)} %copy-done.3), kind=kOutput, calls=%fused_computation.67 | convolution fusion | flops 22020096 | bytes 2873344 | tf_op jit(solution)/shard_map/dot_general | solution.py:80
  148.5 0.8 fusion.29
  149.3 0.1 fusion.17
  149.5 0.3 collective-permute-start.6
  149.8 0.4 collective-permute-start.7
  150.2 1.3 add.103
  151.5 0.8 pad_maximum_fusion.1
  152.3 0.7 broadcast_in_dim.16
  153.0 3.4 %all-to-all-start.5 = ((f32[8,28,128]{2,1,0:T(8,128)}), f32[8,28,128]{2,1,0:T(8,128)S(1)}, u32[]{:S(2)}, u32[]{:S(2)}) async-start(f32[8,28,128]{2,1,0:T(8,128)} %broadcast_in_dim.16), calls=%async_computation.5 | async-start | bytes 262144 | tf_op jit(solution)/shard_map/all_to_all | solution.py:18
  156.3 0.1 convert_reduce_fusion
  156.4 0.7 divide_multiply_fusion
  157.1 5.4 %fusion.1 = bf16[384,3584]{1,0:T(8,128)(2,1)} fusion(bf16[512,384]{1,0:T(8,128)(2,1)S(1)} %pad_maximum_fusion, bf16[384,3584]{1,0:T(8,128)(2,1)S(1)} %copy-done, bf16[256,3584]{1,0:T(8,128)(2,1)} %collective-permute-done.8, bf16[256,3584]{1,0:T(8,128)(2,1)} %bitcast.2, f32[384]{0:T(512)S(1)} %divide_multiply_fusion), kind=kOutput, calls=%fused_computation.5 | convolution fusion | flops 1423507456 | bytes 9569792 | tf_op jit(solution)/shard_map/dot_general | solution.py:99
  162.6 0.8 all-to-all-done.5
  163.3 0.7 broadcast_in_dim.17
  164.1 3.7 %all-to-all-start.6 = ((f32[16,28,128]{2,1,0:T(8,128)}), f32[16,28,128]{2,1,0:T(8,128)S(1)}, u32[]{:S(2)}, u32[]{:S(2)}) async-start(f32[16,28,128]{2,1,0:T(8,128)} %broadcast_in_dim.17), calls=%async_computation.6 | async-start | bytes 524288 | tf_op jit(solution)/shard_map/all_to_all | solution.py:18
  167.7 5.7 %convolution_convert_fusion = bf16[3584,384]{1,0:T(8,128)(2,1)} fusion(bf16[512,384]{1,0:T(8,128)(2,1)} %pad_maximum_fusion.1, bf16[256,3584]{1,0:T(8,128)(2,1)} %copy-done.8, bf16[256,3584]{1,0:T(8,128)(2,1)} %bitcast.41), kind=kOutput, calls=%fused_computation.4 | convolution fusion | flops 1418002432 | bytes 6815744 | tf_op jit(solution)/shard_map/dot_general | solution.py:104
  173.5 1.6 all-to-all-done.6
  175.1 0.6 negate_bitcast_fusion
  (47 shorter events, 0.4 us)
Async XLA Ops:
  0.6 15.1 %copy-start.10 = (f32[384]{0:T(512)S(1)}, f32[384]{0:T(512)}, u32[]{:S(2)}) copy-start(f32[384]{0:T(512)} %param.7) | copy-start | bytes 4612
  0.6 18.3 %collective-permute-start.2 = (bf16[3584,384]{1,0:T(8,128)(2,1)}, bf16[3584,384]{1,0:T(8,128)(2,1)S(1)}, u32[]{:S(2)}, u32[]{:S(2)}) collective-permute-start(bf16[3584,384]{1,0:T(8,128)(2,1)} %param.6), channel_id=1, source_target_pairs={{0,16},{16,0},{1,17},{17,1},{2,18},{18,2},{3,19},{19,3},{4,20},{20... | collective-permute-start | bytes 8257544 | tf_op jit(solution)/shard_map/ppermute | solution.py:24
  4.0 15.0 %collective-permute-start.3 = (bf16[384,3584]{1,0:T(8,128)(2,1)}, bf16[384,3584]{1,0:T(8,128)(2,1)}, u32[]{:S(2)}, u32[]{:S(2)}) collective-permute-start(bf16[384,3584]{1,0:T(8,128)(2,1)} %param.8), channel_id=1, source_target_pairs={{0,16},{16,0},{1,17},{17,1},{2,18},{18,2},{3,19},{19,3},{4,20},{20... | collective-permute-start | bytes 8257544 | tf_op jit(solution)/shard_map/ppermute | solution.py:24
  5.6 13.3 %all-to-all-start = ((bf16[4,2,3584]{2,1,0:T(2,128)(2,1)}), bf16[4,2,3584]{2,1,0:T(2,128)(2,1)S(1)}, u32[]{:S(2)}, u32[]{:S(2)}) async-start(bf16[4,2,3584]{2,1,0:T(2,128)(2,1)} %broadcast_in_dim.12), calls=%async_computation | async-start | bytes 114688 | tf_op jit(solution)/shard_map/all_to_all | solution.py:18
  15.0 3.9 %collective-permute-start = (f32[384]{0:T(512)S(1)}, f32[384]{0:T(512)S(1)}, u32[]{:S(2)}, u32[]{:S(2)}) collective-permute-start(f32[384]{0:T(512)S(1)} %get-tuple-element.29), channel_id=1, source_target_pairs={{0,16},{16,0},{1,17},{17,1},{2,18},{18,2},{3,19},{19,3},{4,20},{20... | collective-permute-start | bytes 4616 | tf_op jit(solution)/shard_map/ppermute | solution.py:24
  15.7 3.2 %collective-permute-start.1 = (f32[384]{0:T(512)S(1)}, f32[384]{0:T(512)S(1)}, u32[]{:S(2)}, u32[]{:S(2)}) collective-permute-start(f32[384]{0:T(512)S(1)} %copy-done.10), channel_id=1, source_target_pairs={{0,16},{16,0},{1,17},{17,1},{2,18},{18,2},{3,19},{19,3},{4,20},{20... | collective-permute-start | bytes 4616 | tf_op jit(solution)/shard_map/ppermute | solution.py:24
  18.9 33.6 %copy-start.3 = (bf16[3584,384]{1,0:T(8,128)(2,1)}, bf16[3584,384]{1,0:T(8,128)(2,1)S(1)}, u32[]{:S(2)}) copy-start(bf16[3584,384]{1,0:T(8,128)(2,1)S(1)} %collective-permute-done.2) | copy-start | bytes 8257540
  48.4 8.0 %copy-start.4 = (bf16[32,8,3584]{2,1,0:T(8,128)(2,1)}, bf16[32,8,3584]{2,1,0:T(8,128)(2,1)S(1)}, u32[]{:S(2)}) copy-start(bf16[32,8,3584]{2,1,0:T(8,128)(2,1)S(1)} %all_to_all.35) | copy-start | bytes 5505028
  48.4 6.1 %copy-start.1 = (bf16[3584,384]{1,0:T(8,128)(2,1)S(1)}, bf16[3584,384]{1,0:T(8,128)(2,1)}, u32[]{:S(2)}) copy-start(bf16[3584,384]{1,0:T(8,128)(2,1)} %param.6) | copy-start | bytes 8257540
  48.4 12.1 %collective-permute-start.4 = (bf16[256,3584]{1,0:T(8,128)(2,1)S(1)}, bf16[256,3584]{1,0:T(8,128)(2,1)S(1)}, u32[]{:S(2)}, u32[]{:S(2)}) collective-permute-start(bf16[256,3584]{1,0:T(8,128)(2,1)S(1)} %bitcast.40), channel_id=1, source_target_pairs={{0,16},{16,0},{1,17},{17,1},{2,18},{18,2},{3,19},{19,3},{4,20},{20... | collective-permute-start | bytes 5505032 | tf_op jit(solution)/shard_map/ppermute | solution.py:24
  54.5 2.0 %copy-start = (bf16[384,3584]{1,0:T(8,128)(2,1)S(1)}, bf16[384,3584]{1,0:T(8,128)(2,1)}, u32[]{:S(2)}) copy-start(bf16[384,3584]{1,0:T(8,128)(2,1)} %param.8) | copy-start | bytes 8257540
  54.5 6.0 %collective-permute-start.5 = (bf16[256,384]{1,0:T(8,128)(2,1)S(1)}, bf16[256,384]{1,0:T(8,128)(2,1)S(1)}, u32[]{:S(2)}, u32[]{:S(2)}) collective-permute-start(bf16[256,384]{1,0:T(8,128)(2,1)S(1)} %get-tuple-element.56), channel_id=1, source_target_pairs={{0,16},{16,0},{1,17},{17,1},{2,18},{18,2},{3,19},{19,3},{4,20},{20... | collective-permute-start | bytes 589832 | tf_op jit(solution)/shard_map/ppermute | solution.py:24
  60.5 1.3 copy-start.8
  104.6 26.2 %copy-start.11 = (f32[256,384]{1,0:T(8,128)S(1)}, f32[256,384]{1,0:T(8,128)}, u32[]{:S(2)}) copy-start(f32[256,384]{1,0:T(8,128)} %get-tuple-element.57) | copy-start | bytes 1179652
  136.3 13.9 %collective-permute-start.9 = (f32[384]{0:T(512)}, f32[384]{0:T(512)}, u32[]{:S(2)}, u32[]{:S(2)}) collective-permute-start(f32[384]{0:T(512)} %get-tuple-element.45), channel_id=1, source_target_pairs={{0,16},{16,0},{1,17},{17,1},{2,18},{18,2},{3,19},{19,3},{4,20},{20... | collective-permute-start | bytes 4616 | tf_op jit(solution)/shard_map/ppermute | solution.py:24
  141.5 15.7 %collective-permute-start.8 = (bf16[256,3584]{1,0:T(8,128)(2,1)}, bf16[256,3584]{1,0:T(8,128)(2,1)}, u32[]{:S(2)}, u32[]{:S(2)}) collective-permute-start(bf16[256,3584]{1,0:T(8,128)(2,1)} %bitcast.2), channel_id=1, source_target_pairs={{0,16},{16,0},{1,17},{17,1},{2,18},{18,2},{3,19},{19,3},{4,20},{20... | collective-permute-start | bytes 5505032 | tf_op jit(solution)/shard_map/ppermute | solution.py:24
  145.1 0.6 copy-start.6
  145.8 2.8 %copy-start.2 = (bf16[3584,384]{1,0:T(8,128)(2,1)S(1)}, bf16[3584,384]{1,0:T(8,128)(2,1)}, u32[]{:S(2)}) copy-start(bf16[3584,384]{1,0:T(8,128)(2,1)} %param.6) | copy-start | bytes 8257540
  145.8 4.1 %copy-start.9 = (bf16[256,384]{1,0:T(8,128)(2,1)S(1)}, bf16[256,384]{1,0:T(8,128)(2,1)}, u32[]{:S(2)}) copy-start(bf16[256,384]{1,0:T(8,128)(2,1)} %get-tuple-element.44) | copy-start | bytes 589828
  145.8 4.4 %copy-start.7 = (f32[384]{0:T(512)S(1)}, f32[384]{0:T(512)}, u32[]{:S(2)}) copy-start(f32[384]{0:T(512)} %copy-done.6) | copy-start | bytes 4612
  145.8 5.7 %copy-start.5 = (bf16[256,384]{1,0:T(8,128)(2,1)S(1)}, bf16[256,384]{1,0:T(8,128)(2,1)}, u32[]{:S(2)}) copy-start(bf16[256,384]{1,0:T(8,128)(2,1)} %get-tuple-element.42) | copy-start | bytes 589828
  149.5 2.0 %collective-permute-start.6 = (f32[28,128]{1,0:T(8,128)S(1)}, f32[28,128]{1,0:T(8,128)S(1)}, u32[]{:S(2)}, u32[]{:S(2)}) collective-permute-start(f32[28,128]{1,0:T(8,128)S(1)} %subtract_bitcast_fusion), channel_id=1, source_target_pairs={{0,16},{16,0},{1,17},{17,1},{2,18},{18,2},{3,19},{19,3},{4,20},{20... | collective-permute-start | bytes 43016 | tf_op jit(solution)/shard_map/ppermute | solution.py:24
  149.8 1.6 collective-permute-start.7
  153.0 10.3 %all-to-all-start.5 = ((f32[8,28,128]{2,1,0:T(8,128)}), f32[8,28,128]{2,1,0:T(8,128)S(1)}, u32[]{:S(2)}, u32[]{:S(2)}) async-start(f32[8,28,128]{2,1,0:T(8,128)} %broadcast_in_dim.16), calls=%async_computation.5 | async-start | bytes 262144 | tf_op jit(solution)/shard_map/all_to_all | solution.py:18
  164.1 11.0 %all-to-all-start.6 = ((f32[16,28,128]{2,1,0:T(8,128)}), f32[16,28,128]{2,1,0:T(8,128)S(1)}, u32[]{:S(2)}, u32[]{:S(2)}) async-start(f32[16,28,128]{2,1,0:T(8,128)} %broadcast_in_dim.17), calls=%async_computation.6 | async-start | bytes 524288 | tf_op jit(solution)/shard_map/all_to_all | solution.py:18

commit v5 on v4

v5 whole, which is shorter than its diff:
```python
import functools
import math

import jax
import jax.numpy as jnp
from jax import lax
from jax.experimental import pallas as pl
from jax.experimental.pallas import tpu as pltpu
from jax.sharding import Mesh, PartitionSpec as P

LMAJ = ("zl", "x", "c")
LMIN = ("zh", "y")
WIDE, NWIDE = ("zl", "x", "y"), 32
XY, NXY = ("x", "y"), 16
Z, NZ = ("zl", "zh"), 8
ZH, NZH = ("zh",), 4
f32, bf16 = jnp.float32, jnp.bfloat16
VMEM = pl.BlockSpec(memory_space=pltpu.VMEM)
VMEM_BYTES = 16 * 1024 * 1024
NT = (((1,), (1,)), ((), ()))


def spread(block, axes, n):
    return lax.all_to_all(
        jnp.broadcast_to(block[None], (n,) + block.shape), axes, 0, 0, tiled=True
    )


def swap(block):
    return lax.ppermute(block, "c", [(0, 1), (1, 0)])


def tie(*values):
    return lax.optimization_barrier(values)


def forward_kernel(
    rows, enc0, enc1, dec0, dec1, bias0, bias1, active0, active1, codes0, codes1, part
):
    for enc, bias, active, codes in (
        (enc0, bias0, active0, codes0),
        (enc1, bias1, active1, codes1),
    ):
        pre = jnp.dot(rows[...], enc[...], preferred_element_type=f32) + bias[...]
        value = jnp.maximum(pre, 0.0)
        active[...] = value
        codes[...] = (value * value).astype(bf16)
    total = jnp.dot(codes0[...], dec0[...], preferred_element_type=f32)
    total += jnp.dot(codes1[...], dec1[...], preferred_element_type=f32)
    part[...] = total.astype(bf16)


def forward(rows, enc, dec, bias):
    count, width = rows.shape
    mine = enc[0].shape[1]
    flat = jax.ShapeDtypeStruct((count, mine), f32)
    half = jax.ShapeDtypeStruct((count, mine), bf16)
    return pl.pallas_call(
        forward_kernel,
        out_shape=(flat, flat, half, half, jax.ShapeDtypeStruct((count, width), bf16)),
        in_specs=[VMEM] * 7,
        out_specs=(VMEM,) * 5,
        compiler_params=pltpu.CompilerParams(vmem_limit_bytes=VMEM_BYTES),
        cost_estimate=pl.CostEstimate(
            flops=8 * count * width * mine, bytes_accessed=16_000_000, transcendentals=0
        ),
        name="forward",
    )(rows, *enc, *dec, *bias)


def backward_kernel(
    factor, error, dec0, dec1, enc0, enc1, active0, active1, slope0, slope1, block_sum,
    dpre0, dpre1, sums0, sums1, through,
):
    product = None
    for dec, enc, active, slope, dpre, sums in (
        (dec0, enc0, active0, slope0, dpre0, sums0),
        (dec1, enc1, active1, slope1, dpre1, sums1),
    ):
        back = lax.dot_general(error[...], dec[...], NT, preferred_element_type=f32)
        value = (2.0 * factor * back + slope[...]) * 2.0 * active[...]
        dpre[...] = value.astype(bf16)
        total = jnp.sum(value, axis=0, keepdims=True)
        sums[...] = total
        first = total.astype(bf16)
        rest = total - first.astype(f32)
        second = rest.astype(bf16)
        third = (rest - second.astype(f32)).astype(bf16)
        parts = jnp.concatenate(
            [first, second, third, jnp.zeros((13, total.shape[1]), bf16)], axis=0
        )
        term = lax.dot_general(parts, enc[...], NT, preferred_element_type=f32)
        product = term if product is None else product + term
    row = product[0:1] + product[1:2] + product[2:3]
    for k in range(through.shape[0]):
        through[k : k + 1, :] = row[:, 128 * k : 128 * (k + 1)] - block_sum[k : k + 1, :]


def backward(error, dec, enc, active, slope, block_sum, factor):
    count, width = error.shape
    mine = enc[0].shape[1]
    half = jax.ShapeDtypeStruct((count, mine), bf16)
    line = jax.ShapeDtypeStruct((1, mine), f32)
    return pl.pallas_call(
        functools.partial(backward_kernel, factor),
        out_shape=(half, half, line, line, jax.ShapeDtypeStruct(block_sum.shape, f32)),
        in_specs=[VMEM] * 10,
        out_specs=(VMEM,) * 5,
        compiler_params=pltpu.CompilerParams(vmem_limit_bytes=VMEM_BYTES),
        cost_estimate=pl.CostEstimate(
            flops=6 * count * width * mine, bytes_accessed=15_000_000, transcendentals=0
        ),
        name="backward",
    )(error, *dec, *enc, *active, *slope, block_sum)


def per_device(resid_rows, w_encode, b_encode, w_decode, b_decode):
    local_rows, width = resid_rows.shape
    total_rows = local_rows * 16
    half = total_rows // 2
    rows = half // NWIDE
    factor = 1.0 / math.sqrt(total_rows)

    piece = rows // NZH
    at = (lax.axis_index("c") * 2 + lax.axis_index("zl")) * 4 + lax.axis_index("x")
    block = lax.dynamic_slice_in_dim(resid_rows, at * piece, piece, 0)
    block = (block.astype(f32) - b_decode).astype(bf16)
    block = spread(block, ZH, NZH).reshape(rows, width)
    dec_float = w_decode.astype(f32)
    norms = jnp.sqrt(jnp.sum(dec_float * dec_float, axis=1) + 1e-06)
    slope0 = (0.5 * factor * norms).reshape(1, -1)
    bias0 = b_encode.reshape(1, -1)
    block, norms, slope0, slope1, bias0, bias1, enc1, dec1 = tie(
        block, norms, slope0, swap(slope0), bias0, swap(bias0), swap(w_encode), swap(w_decode)
    )
    centered = spread(block, WIDE, NWIDE).reshape(half, width)

    active0, active1, codes0, codes1, part = forward(
        centered, (w_encode, enc1), (w_decode, dec1), (bias0, bias1)
    )
    part = part.reshape(NWIDE, rows, width)
    part = lax.all_to_all(part, WIDE, 0, 0, tiled=True)
    part = jnp.sum(part.astype(f32), axis=0).astype(bf16)
    summed = jnp.sum(spread(part, ZH, NZH).astype(f32), axis=0)
    error_block = (summed - block.astype(f32)).astype(bf16)
    block_sum = 2.0 * factor / NZH * jnp.sum(error_block.astype(f32), axis=0)
    block_sum = block_sum.reshape(width // 128, 128)
    error_block, block_sum = tie(error_block, block_sum)
    error = spread(error_block, WIDE, NWIDE).reshape(half, width)
    error, centered, codes1 = tie(error, centered, codes1)

    dpre0, dpre1, sums0, sums1, through = backward(
        error, (w_decode, dec1), (w_encode, enc1), (active0, active1), (slope0, slope1),
        block_sum, factor,
    )
    through = through + swap(through)

    all_codes = jnp.concatenate([codes0, swap(codes1)], axis=0)
    all_dpre = jnp.concatenate([dpre0, swap(dpre1)], axis=0)
    all_rows = jnp.concatenate([centered, swap(centered)], axis=0)
    all_error = jnp.concatenate([error, swap(error)], axis=0)
    through, all_codes, all_dpre = tie(through, all_codes, all_dpre)
    code_sum = jnp.sum(all_codes.astype(f32), axis=0)
    through = spread(through, Z, NZ)
    grad_decode = (
        2.0 * factor * jnp.dot(all_codes.T, all_error, preferred_element_type=f32)
        + 0.5 * factor * (code_sum / norms)[:, None] * dec_float
    ).astype(bf16)
    through, grad_decode, all_dpre = tie(through, grad_decode, all_dpre)
    through = jnp.sum(spread(jnp.sum(through, axis=0), XY, NXY), axis=0).reshape(width)
    grad_encode = jnp.dot(all_rows.T, all_dpre, preferred_element_type=f32).astype(bf16)
    grad_b_encode = (sums0 + swap(sums1)).reshape(-1)
    return (grad_encode, grad_b_encode, grad_decode, -through)


def solution(mesh):
    fine = Mesh(mesh.devices.reshape(2, 4, 2, 4, 4), ("zl", "x", "c", "zh", "y"))
    latents = LMAJ + LMIN
    in_specs = (P(LMIN, None), P(None, latents), P(latents), P(latents, None), P())
    out_specs = (P(None, latents), P(latents), P(latents, None), P())
    return jax.shard_map(
        per_device, mesh=fine, in_specs=in_specs, out_specs=out_specs, check_vma=False
    )
```

time: 178 us -> 174 us (0.978)
  matrix products: 30.7 us -> 11.2 us
  Pallas kernels: 0 us -> 11.7 us
  local copies, waits for them, and re-layouts: 4.28 us -> 8.51 us
  starting transfers between devices: 27.9 us -> 24.2 us
  blocking collectives: 96.4 us -> 99.5 us
    dot_general x8 -> x0, matrix products: 19.6 us -> none  [the longest x2 8.07 us: backward(): jnp.dot(error, w.T, preferred_element_type=f32)]
    pallas_call x0 -> x2, Pallas kernels: none -> 11.7 us  [the longest x1 5.9 us: backward(): pl.pallas_call(functools.partial(backward_kernel, factor), out_shape=(hal...]
    all_to_all x3, blocking collectives: 68.8 us -> 72.7 us  [spread(): lax.all_to_all(jnp.broadcast_to(block[None], (n,) + block.shape), axes, 0...]
    ppermute x10, starting transfers between devices: 14.4 us -> 10.7 us  [swap(): return lax.ppermute(block, 'c', [(0, 1), (1, 0)])]
    unnamed x24 -> x28, local copies, waits for them, and re-layouts: 1.86 us -> 5.37 us
  transfers between devices with their start and end apart: 13 -> 13, of which waited for: 3 -> 4; matrix products, arithmetic and copies ran while one was open for 20% -> 11% of each run, Pallas kernels for 0% -> 3%
where the time goes in v5:
time: 174 us; the launch traced here: 172 us
  blocking collectives  99.5 us (57%)
  starting transfers between devices  24.2 us (14%)
  Pallas kernels  11.7 us (7%)
  matrix products  11.2 us (6%)
  other arithmetic  9.31 us (5%)
  local copies, waits for them, and re-layouts  8.51 us (5%)
  waiting for transfers between devices  6.69 us (4%)
    all_to_all x3, blocking collectives, spread(): lax.all_to_all(jnp.broadcast_to(block[None], (n,) + block.shape), axes, 0...  72.7 us
    all_to_all x1, blocking collectives, per_device(): part = lax.all_to_all(part, WIDE, 0, 0, tiled=True)  26.8 us
    all_to_all x3, starting transfers between devices, spread(): lax.all_to_all(jnp.broadcast_to(block[None], (n,) + block.shape), axes, 0...  13.5 us
    ppermute x10, starting transfers between devices, swap(): return lax.ppermute(block, 'c', [(0, 1), (1, 0)])  10.7 us
    all_to_all x3, waiting for transfers between devices, spread(): lax.all_to_all(jnp.broadcast_to(block[None], (n,) + block.shape), axes, 0...  6.02 us
    pallas_call x1, Pallas kernels, backward(): pl.pallas_call(functools.partial(backward_kernel, factor), out_shape=(hal...  5.9 us
    pallas_call x1, Pallas kernels, forward(): pl.pallas_call(forward_kernel, out_shape=(flat, flat, half, half, jax.Sha...  5.83 us
    dot_general x1, matrix products, per_device(): jnp.dot(all_rows.T, all_dpre, preferred_element_type=f32).astype(bf16)  5.74 us
  transfers between devices with their start and end apart: 13, of which 4 were waited for; matrix products, arithmetic and copies ran while one was open for 11% of the time, Pallas kernels for 3%

profile of v5, /device:TPU:1, one launch (start us, length us, event | category | flops | bytes accessed | tf_op | source)
XLA Modules:
  0.0 172.0 jit_solution(16260142602695983259)
XLA Ops:
  0.6 3.3 %collective-permute-start.2 = (bf16[3584,384]{1,0:T(8,128)(2,1)}, bf16[3584,384]{1,0:T(8,128)(2,1)S(1)}, u32[]{:S(2)}, u32[]{:S(2)}) collective-permute-start(bf16[3584,384]{1,0:T(8,128)(2,1)} %enc0.3), channel_id=1, source_target_pairs={{0,16},{16,0},{1,17},{17,1},{2,18},{18,2},{3,19},{19,3},{4,20},{20... | collective-permute-start | bytes 8257544 | tf_op jit(solution)/shard_map/ppermute | solution.py:30
  4.0 0.1 collective-permute-start.3
  4.1 0.9 subtract_convert_fusion.1
  4.9 0.7 broadcast_in_dim.12
  5.6 6.4 %all-to-all-start = ((bf16[4,2,3584]{2,1,0:T(2,128)(2,1)}), bf16[4,2,3584]{2,1,0:T(2,128)(2,1)S(1)}, u32[]{:S(2)}, u32[]{:S(2)}) async-start(bf16[4,2,3584]{2,1,0:T(2,128)(2,1)} %broadcast_in_dim.12), calls=%async_computation | async-start | bytes 114688 | tf_op jit(solution)/shard_map/all_to_all | solution.py:24
  12.0 2.4 %fusion.2 = f32[384]{0:T(512)S(1)} fusion(bf16[384,3584]{1,0:T(8,128)(2,1)} %dec0.3), kind=kLoop, calls=%fused_computation.6 | loop fusion | flops 4128384 | bytes 2754048 | tf_op jit(solution)/shard_map/reduce_sum | solution.py:130
  14.4 0.6 broadcast_multiply_fusion
  15.0 0.7 collective-permute-start
  15.7 0.1 collective-permute-start.1
  15.8 3.1 %all-to-all-done = bf16[4,2,3584]{2,1,0:T(2,128)(2,1)S(1)} async-done(((bf16[4,2,3584]{2,1,0:T(2,128)(2,1)}), bf16[4,2,3584]{2,1,0:T(2,128)(2,1)S(1)}, u32[]{:S(2)}, u32[]{:S(2)}) %all-to-all-start) | async-done | bytes 57376 | tf_op jit(solution)/shard_map/all_to_all | solution.py:24
  18.9 0.0 copy-start.3
  18.9 1.5 copy-done.3
  20.5 0.1 broadcast_in_dim.13
  20.6 29.6 %all_to_all.35 = bf16[32,8,3584]{2,1,0:T(8,128)(2,1)S(1)} all-to-all(bf16[32,8,3584]{2,1,0:T(8,128)(2,1)S(1)} %broadcast_in_dim.13), channel_id=1, replica_groups=mesh['zl'=2,'x'=4,'c'=2,'zh'=4,'y'=4] {'zl','x','y'}, dimensions={0} | all-to-all | bytes 3670016 | tf_op jit(solution)/shard_map/all_to_all | solution.py:24
  50.2 0.0 copy-start.4
  50.2 2.4 %copy-done.4 = bf16[3584,384]{1,0:T(8,128)(2,1)S(1)} copy-done((bf16[3584,384]{1,0:T(8,128)(2,1)S(1)}, bf16[3584,384]{1,0:T(8,128)(2,1)}, u32[]{:S(2)}) %copy-start.4) | copy-done | bytes 2752536
  52.7 5.8 %forward.1 = (f32[256,384]{1,0:T(8,128)S(1)}, f32[256,384]{1,0:T(8,128)S(1)}, bf16[256,384]{1,0:T(8,128)(2,1)S(1)}, bf16[256,384]{1,0:T(8,128)(2,1)S(1)}, bf16[256,3584]{1,0:T(8,128)(2,1)S(1)}) custom-call(bf16[256,3584]{1,0:T(8,128)(2,1)S(1)} %bitcast.9, bf16[3584,384]{1,0:T(8,128)(2,1)S(1)} %copy-done.1, bf16[3584,384]{1,0:T(8,128)(2,1)S(1)} %copy-done.4, ...), custom_call_target="tpu_custom_call" | custom-call | flops 2818572288 | bytes 16000000 | tf_op jit(solution)/shard_map/forward/pallas_call | solution.py:58
  58.5 0.7 copy-done.7
  59.2 0.7 copy-done.9
  59.9 26.8 %all_to_all.36 = bf16[32,8,3584]{2,1,0:T(8,128)(2,1)} all-to-all(bf16[32,8,3584]{2,1,0:T(8,128)(2,1)S(1)} %bitcast.12), channel_id=1, replica_groups=mesh['zl'=2,'x'=4,'c'=2,'zh'=4,'y'=4] {'zl','x','y'}, dimensions={0} | all-to-all | bytes 3670016 | tf_op jit(solution)/shard_map/all_to_all | solution.py:142
  86.7 2.4 %reduce_sum.67 = bf16[8,3584]{1,0:T(8,128)(2,1)} reduce(bf16[32,8,3584]{2,1,0:T(8,128)(2,1)} %all_to_all.36, bf16[]{:T(256)} %constant.34.clone.1), dimensions={0}, to_apply=%region_1.0 | reduce | flops 888832 | bytes 1892354 | tf_op jit(solution)/shard_map/reduce_sum | solution.py:143
  89.1 0.8 broadcast_in_dim.14
  89.9 16.7 %all_to_all.37 = bf16[4,8,3584]{2,1,0:T(8,128)(2,1)S(1)} all-to-all(bf16[4,8,3584]{2,1,0:T(8,128)(2,1)S(1)} %broadcast_in_dim.14), channel_id=1, replica_groups=mesh['zl'=2,'x'=4,'c'=2,'zh'=4,'y'=4] {'zh'}, dimensions={0} | all-to-all | bytes 458752 | tf_op jit(solution)/shard_map/all_to_all | solution.py:24
  106.7 0.9 convert_reduce_fusion.2
  107.6 0.0 copy-start.2
  107.6 0.0 copy-start.5
  107.6 0.1 broadcast_in_dim.15
  107.7 26.4 %all_to_all.38 = bf16[32,8,3584]{2,1,0:T(8,128)(2,1)} all-to-all(bf16[32,8,3584]{2,1,0:T(8,128)(2,1)S(1)} %broadcast_in_dim.15), channel_id=1, replica_groups=mesh['zl'=2,'x'=4,'c'=2,'zh'=4,'y'=4] {'zl','x','y'}, dimensions={0} | all-to-all | bytes 3670016 | tf_op jit(solution)/shard_map/all_to_all | solution.py:24
  134.1 5.2 %collective-permute-start.8 = (bf16[256,3584]{1,0:T(8,128)(2,1)}, bf16[256,3584]{1,0:T(8,128)(2,1)}, u32[]{:S(2)}, u32[]{:S(2)}) collective-permute-start(bf16[256,3584]{1,0:T(8,128)(2,1)} %bitcast.3.error), channel_id=1, source_target_pairs={{0,16},{16,0},{1,17},{17,1},{2,18},{18,2},{3,19},{19,3},{4,20},{20... | collective-permute-start | bytes 5505032 | tf_op jit(solution)/shard_map/ppermute | solution.py:30
  139.3 0.0 copy-start.12
  139.4 5.9 %backward.1 = (bf16[256,384]{1,0:T(8,128)(2,1)S(1)}, bf16[256,384]{1,0:T(8,128)(2,1)S(1)}, f32[1,384]{1,0:T(1,128)S(1)}, f32[1,384]{1,0:T(1,128)S(1)}, f32[28,128]{1,0:T(8,128)S(1)}) custom-call(bf16[256,3584]{1,0:T(8,128)(2,1)} %bitcast.3.error, bf16[384,3584]{1,0:T(8,128)(2,1)S(1)} %copy-done, bf16[384,3584]{1,0:T(8,128)(2,1)} %collective-permute-done.3.dec1, ...), custom_call_target="tpu_custom_call" | custom-call | flops 2113929216 | bytes 15000000 | tf_op jit(solution)/shard_map/backward/pallas_call | solution.py:104
  145.3 0.5 collective-permute-start.7
  145.8 0.1 collective-permute-start.9
  145.9 0.4 collective-permute-start.5
  146.3 0.6 collective-permute-done.9
  146.9 0.3 collective-permute-start.6
  147.2 0.6 add_reduce_fusion
  147.8 0.8 pad_maximum_fusion.1
  148.7 0.7 broadcast_in_dim.16
  149.3 3.4 %all-to-all-start.5 = ((f32[8,28,128]{2,1,0:T(8,128)}), f32[8,28,128]{2,1,0:T(8,128)S(1)}, u32[]{:S(2)}, u32[]{:S(2)}) async-start(f32[8,28,128]{2,1,0:T(8,128)} %broadcast_in_dim.16), calls=%async_computation.5 | async-start | bytes 262144 | tf_op jit(solution)/shard_map/all_to_all | solution.py:24
  152.7 0.1 convert_reduce_fusion
  152.8 5.4 %fusion.1 = bf16[384,3584]{1,0:T(8,128)(2,1)} fusion(bf16[512,384]{1,0:T(8,128)(2,1)S(1)} %pad_maximum_fusion, bf16[384,3584]{1,0:T(8,128)(2,1)S(1)} %copy-done, bf16[256,3584]{1,0:T(8,128)(2,1)} %collective-permute-done.8, bf16[256,3584]{1,0:T(8,128)(2,1)} %bitcast.3.error, f32[384]{0:T(512)S(1)} %divide_multiply_fusion), kind=kOutput, calls=%fused_computation.5 | convolution fusion | flops 1423507456 | bytes 9569792 | tf_op jit(solution)/shard_map/dot_general | solution.py:166
  158.3 1.4 all-to-all-done.5
  159.7 0.7 broadcast_in_dim.17
  160.4 3.7 %all-to-all-start.6 = ((f32[16,28,128]{2,1,0:T(8,128)}), f32[16,28,128]{2,1,0:T(8,128)S(1)}, u32[]{:S(2)}, u32[]{:S(2)}) async-start(f32[16,28,128]{2,1,0:T(8,128)} %broadcast_in_dim.17), calls=%async_computation.6 | async-start | bytes 524288 | tf_op jit(solution)/shard_map/all_to_all | solution.py:24
  164.1 5.7 %convolution_convert_fusion = bf16[3584,384]{1,0:T(8,128)(2,1)} fusion(bf16[512,384]{1,0:T(8,128)(2,1)} %pad_maximum_fusion.1, bf16[256,3584]{1,0:T(8,128)(2,1)} %collective-permute-done.4, bf16[256,3584]{1,0:T(8,128)(2,1)} %bitcast.11), kind=kOutput, calls=%fused_computation.4 | convolution fusion | flops 1418002432 | bytes 6815744 | tf_op jit(solution)/shard_map/dot_general | solution.py:171
  169.8 1.6 all-to-all-done.6
  171.4 0.6 negate_bitcast_fusion
  (39 shorter events, 0.2 us)
Async XLA Ops:
  0.6 15.1 %copy-start.13 = (f32[384]{0:T(512)S(1)}, f32[384]{0:T(512)}, u32[]{:S(2)}) copy-start(f32[384]{0:T(512)} %param.7) | copy-start | bytes 4612
  0.6 18.3 %collective-permute-start.2 = (bf16[3584,384]{1,0:T(8,128)(2,1)}, bf16[3584,384]{1,0:T(8,128)(2,1)S(1)}, u32[]{:S(2)}, u32[]{:S(2)}) collective-permute-start(bf16[3584,384]{1,0:T(8,128)(2,1)} %enc0.3), channel_id=1, source_target_pairs={{0,16},{16,0},{1,17},{17,1},{2,18},{18,2},{3,19},{19,3},{4,20},{20... | collective-permute-start | bytes 8257544 | tf_op jit(solution)/shard_map/ppermute | solution.py:30
  4.0 16.5 %collective-permute-start.3 = (bf16[384,3584]{1,0:T(8,128)(2,1)}, bf16[384,3584]{1,0:T(8,128)(2,1)}, u32[]{:S(2)}, u32[]{:S(2)}) collective-permute-start(bf16[384,3584]{1,0:T(8,128)(2,1)} %dec0.3), channel_id=1, source_target_pairs={{0,16},{16,0},{1,17},{17,1},{2,18},{18,2},{3,19},{19,3},{4,20},{20... | collective-permute-start | bytes 8257544 | tf_op jit(solution)/shard_map/ppermute | solution.py:30
  5.6 13.3 %all-to-all-start = ((bf16[4,2,3584]{2,1,0:T(2,128)(2,1)}), bf16[4,2,3584]{2,1,0:T(2,128)(2,1)S(1)}, u32[]{:S(2)}, u32[]{:S(2)}) async-start(bf16[4,2,3584]{2,1,0:T(2,128)(2,1)} %broadcast_in_dim.12), calls=%async_computation | async-start | bytes 114688 | tf_op jit(solution)/shard_map/all_to_all | solution.py:24
  15.0 3.9 %collective-permute-start = (f32[1,384]{1,0:T(1,128)S(1)}, f32[1,384]{1,0:T(1,128)S(1)}, u32[]{:S(2)}, u32[]{:S(2)}) collective-permute-start(f32[1,384]{1,0:T(1,128)S(1)} %mul.63.slope0), channel_id=1, source_target_pairs={{0,16},{16,0},{1,17},{17,1},{2,18},{18,2},{3,19},{19,3},{4,20},{20... | collective-permute-start | bytes 4616 | tf_op jit(solution)/shard_map/ppermute | solution.py:30
  15.7 3.2 %collective-permute-start.1 = (f32[1,384]{1,0:T(1,128)S(1)}, f32[1,384]{1,0:T(1,128)S(1)}, u32[]{:S(2)}, u32[]{:S(2)}) collective-permute-start(f32[1,384]{1,0:T(1,128)S(1)} %reshape.61.bias0), channel_id=1, source_target_pairs={{0,16},{16,0},{1,17},{17,1},{2,18},{18,2},{3,19},{19,3},{4,20},{20... | collective-permute-start | bytes 4616 | tf_op jit(solution)/shard_map/ppermute | solution.py:30
  18.9 31.3 %copy-start.11 = (bf16[8,3584]{1,0:T(8,128)(2,1)}, bf16[8,3584]{1,0:T(8,128)(2,1)S(1)}, u32[]{:S(2)}) copy-start(bf16[8,3584]{1,0:T(8,128)(2,1)S(1)} %reshape.60) | copy-start | bytes 172036
  18.9 1.5 copy-start.3
  20.5 29.7 %copy-start = (bf16[384,3584]{1,0:T(8,128)(2,1)S(1)}, bf16[384,3584]{1,0:T(8,128)(2,1)}, u32[]{:S(2)}) copy-start(bf16[384,3584]{1,0:T(8,128)(2,1)} %dec0.3) | copy-start | bytes 8257540
  20.5 29.7 %copy-start.1 = (bf16[3584,384]{1,0:T(8,128)(2,1)S(1)}, bf16[3584,384]{1,0:T(8,128)(2,1)}, u32[]{:S(2)}) copy-start(bf16[3584,384]{1,0:T(8,128)(2,1)} %enc0.3) | copy-start | bytes 8257540
  50.2 8.3 %copy-start.6 = (bf16[32,8,3584]{2,1,0:T(8,128)(2,1)}, bf16[32,8,3584]{2,1,0:T(8,128)(2,1)S(1)}, u32[]{:S(2)}) copy-start(bf16[32,8,3584]{2,1,0:T(8,128)(2,1)S(1)} %all_to_all.35) | copy-start | bytes 5505028
  50.2 2.4 %copy-start.4 = (bf16[3584,384]{1,0:T(8,128)(2,1)S(1)}, bf16[3584,384]{1,0:T(8,128)(2,1)}, u32[]{:S(2)}) copy-start(bf16[3584,384]{1,0:T(8,128)(2,1)} %copy-done.3) | copy-start | bytes 8257540
  58.5 0.7 copy-start.7
  59.2 0.7 copy-start.9
  107.6 31.7 %copy-start.2 = (bf16[3584,384]{1,0:T(8,128)(2,1)S(1)}, bf16[3584,384]{1,0:T(8,128)(2,1)}, u32[]{:S(2)}) copy-start(bf16[3584,384]{1,0:T(8,128)(2,1)} %enc0.3) | copy-start | bytes 8257540
  107.6 31.7 %copy-start.5 = (bf16[3584,384]{1,0:T(8,128)(2,1)S(1)}, bf16[3584,384]{1,0:T(8,128)(2,1)}, u32[]{:S(2)}) copy-start(bf16[3584,384]{1,0:T(8,128)(2,1)} %copy-done.3) | copy-start | bytes 8257540
  134.1 18.7 %collective-permute-start.8 = (bf16[256,3584]{1,0:T(8,128)(2,1)}, bf16[256,3584]{1,0:T(8,128)(2,1)}, u32[]{:S(2)}, u32[]{:S(2)}) collective-permute-start(bf16[256,3584]{1,0:T(8,128)(2,1)} %bitcast.3.error), channel_id=1, source_target_pairs={{0,16},{16,0},{1,17},{17,1},{2,18},{18,2},{3,19},{19,3},{4,20},{20... | collective-permute-start | bytes 5505032 | tf_op jit(solution)/shard_map/ppermute | solution.py:30
  139.3 24.8 %collective-permute-start.4 = (bf16[256,3584]{1,0:T(8,128)(2,1)}, bf16[256,3584]{1,0:T(8,128)(2,1)}, u32[]{:S(2)}, u32[]{:S(2)}) collective-permute-start(bf16[256,3584]{1,0:T(8,128)(2,1)} %bitcast.10), channel_id=1, source_target_pairs={{0,16},{16,0},{1,17},{17,1},{2,18},{18,2},{3,19},{19,3},{4,20},{20... | collective-permute-start | bytes 5505032 | tf_op jit(solution)/shard_map/ppermute | solution.py:30
  139.3 7.6 %copy-start.10 = (bf16[256,384]{1,0:T(8,128)(2,1)S(1)}, bf16[256,384]{1,0:T(8,128)(2,1)}, u32[]{:S(2)}) copy-start(bf16[256,384]{1,0:T(8,128)(2,1)} %copy-done.9) | copy-start | bytes 589828
  139.3 9.3 %copy-start.8 = (bf16[256,384]{1,0:T(8,128)(2,1)S(1)}, bf16[256,384]{1,0:T(8,128)(2,1)}, u32[]{:S(2)}) copy-start(bf16[256,384]{1,0:T(8,128)(2,1)} %copy-done.7) | copy-start | bytes 589828
  139.3 13.5 %copy-start.12 = (f32[384]{0:T(512)S(1)}, f32[384]{0:T(512)}, u32[]{:S(2)}) copy-start(f32[384]{0:T(512)} %get-tuple-element.55) | copy-start | bytes 4612
  145.3 2.6 %collective-permute-start.7 = (bf16[256,384]{1,0:T(8,128)(2,1)S(1)}, bf16[256,384]{1,0:T(8,128)(2,1)S(1)}, u32[]{:S(2)}, u32[]{:S(2)}) collective-permute-start(bf16[256,384]{1,0:T(8,128)(2,1)S(1)} %get-tuple-element.52), channel_id=1, source_target_pairs={{0,16},{16,0},{1,17},{17,1},{2,18},{18,2},{3,19},{19,3},{4,20},{20... | collective-permute-start | bytes 589832 | tf_op jit(solution)/shard_map/ppermute | solution.py:30
  145.8 1.2 collective-permute-start.9
  145.9 1.9 %collective-permute-start.5 = (f32[28,128]{1,0:T(8,128)S(1)}, f32[28,128]{1,0:T(8,128)S(1)}, u32[]{:S(2)}, u32[]{:S(2)}) collective-permute-start(f32[28,128]{1,0:T(8,128)S(1)} %get-tuple-element.48), channel_id=1, source_target_pairs={{0,16},{16,0},{1,17},{17,1},{2,18},{18,2},{3,19},{19,3},{4,20},{20... | collective-permute-start | bytes 43016 | tf_op jit(solution)/shard_map/ppermute | solution.py:30
  146.9 1.7 collective-permute-start.6
  149.3 10.3 %all-to-all-start.5 = ((f32[8,28,128]{2,1,0:T(8,128)}), f32[8,28,128]{2,1,0:T(8,128)S(1)}, u32[]{:S(2)}, u32[]{:S(2)}) async-start(f32[8,28,128]{2,1,0:T(8,128)} %broadcast_in_dim.16), calls=%async_computation.5 | async-start | bytes 262144 | tf_op jit(solution)/shard_map/all_to_all | solution.py:24
  160.4 11.0 %all-to-all-start.6 = ((f32[16,28,128]{2,1,0:T(8,128)}), f32[16,28,128]{2,1,0:T(8,128)S(1)}, u32[]{:S(2)}, u32[]{:S(2)}) async-start(f32[16,28,128]{2,1,0:T(8,128)} %broadcast_in_dim.17), calls=%async_computation.6 | async-start | bytes 524288 | tf_op jit(solution)/shard_map/all_to_all | solution.py:24

commit v6 on v5

--- a/solution.py
+++ b/solution.py
@@ -16,7 +16,9 @@
 ZH, NZH = ("zh",), 4
 f32, bf16 = jnp.float32, jnp.bfloat16
 VMEM = pl.BlockSpec(memory_space=pltpu.VMEM)
+ANY = pl.BlockSpec(memory_space=pl.ANY)
 VMEM_BYTES = 16 * 1024 * 1024
+SMALL_BYTES = 6 * 1024 * 1024
 NT = (((1,), (1,)), ((), ()))
 
 
@@ -34,9 +36,78 @@
     return lax.optimization_barrier(values)
 
 
+def small_kernel(body, out_shape, *args, name):
+    return pl.pallas_call(
+        body,
+        out_shape=out_shape,
+        in_specs=[VMEM] * len(args),
+        out_specs=jax.tree.map(lambda _: VMEM, out_shape),
+        compiler_params=pltpu.CompilerParams(vmem_limit_bytes=SMALL_BYTES),
+        name=name,
+    )(*args)
+
+
+def repeat_into(out, value):
+    for k in range(out.shape[0]):
+        out[k] = value
+
+
+def collect_kernel(pieces, enc_hbm, dec_hbm, block, out, enc, dec, sem):
+    copies = (
+        pltpu.make_async_copy(enc_hbm, enc, sem.at[0]),
+        pltpu.make_async_copy(dec_hbm, dec, sem.at[1]),
+    )
+    for copy in copies:
+        copy.start()
+    value = jnp.concatenate([pieces[k] for k in range(pieces.shape[0])], axis=0)
+    block[...] = value
+    repeat_into(out, value)
+    for copy in copies:
+        copy.wait()
+
+
+def collect(pieces, enc, dec, wide):
+    count, rows, width = pieces.shape
+    return pl.pallas_call(
+        collect_kernel,
+        out_shape=(
+            jax.ShapeDtypeStruct((count * rows, width), bf16),
+            jax.ShapeDtypeStruct((wide, count * rows, width), bf16),
+            jax.ShapeDtypeStruct(enc.shape, bf16),
+            jax.ShapeDtypeStruct(dec.shape, bf16),
+        ),
+        in_specs=[VMEM, ANY, ANY],
+        out_specs=(VMEM,) * 4,
+        scratch_shapes=[pltpu.SemaphoreType.DMA((2,))],
+        compiler_params=pltpu.CompilerParams(vmem_limit_bytes=SMALL_BYTES),
+        name="collect",
+    )(pieces, enc, dec)
+
+
+def reduce_kernel(parts, out):
+    total = parts[0].astype(f32)
+    for k in range(1, parts.shape[0]):
+        total += parts[k].astype(f32)
+    repeat_into(out, total.astype(bf16))
+
+
+def error_kernel(factor, parts, block, out, block_sum):
+    total = parts[0].astype(f32)
+    for k in range(1, parts.shape[0]):
+        total += parts[k].astype(f32)
+    error = (total - block[...].astype(f32)).astype(bf16)
+    repeat_into(out, error)
+    row = (2.0 * factor / parts.shape[0]) * jnp.sum(error.astype(f32), axis=0, keepdims=True)
+    for k in range(block_sum.shape[0]):
+        block_sum[k : k + 1, :] = row[:, 128 * k : 128 * (k + 1)]
+
+
 def forward_kernel(
-    rows, enc0, enc1, dec0, dec1, bias0, bias1, active0, active1, codes0, codes1, part
+    rows, enc0, enc1, dec0, dec1, bias0, bias1,
+    active0, active1, codes0, codes1, part, rows_out, sem,
 ):
+    copy = pltpu.make_async_copy(rows, rows_out, sem)
+    copy.start()
     for enc, bias, active, codes in (
         (enc0, bias0, active0, codes0),
         (enc1, bias1, active1, codes1),
@@ -48,6 +119,7 @@
     total = jnp.dot(codes0[...], dec0[...], preferred_element_type=f32)
     total += jnp.dot(codes1[...], dec1[...], preferred_element_type=f32)
     part[...] = total.astype(bf16)
+    copy.wait()
 
 
 def forward(rows, enc, dec, bias):
@@ -55,11 +127,13 @@
     mine = enc[0].shape[1]
     flat = jax.ShapeDtypeStruct((count, mine), f32)
     half = jax.ShapeDtypeStruct((count, mine), bf16)
+    full = jax.ShapeDtypeStruct((count, width), bf16)
     return pl.pallas_call(
         forward_kernel,
-        out_shape=(flat, flat, half, half, jax.ShapeDtypeStruct((count, width), bf16)),
+        out_shape=(flat, flat, half, half, full, full),
         in_specs=[VMEM] * 7,
-        out_specs=(VMEM,) * 5,
+        out_specs=(VMEM,) * 5 + (ANY,),
+        scratch_shapes=[pltpu.SemaphoreType.DMA],
         compiler_params=pltpu.CompilerParams(vmem_limit_bytes=VMEM_BYTES),
         cost_estimate=pl.CostEstimate(
             flops=8 * count * width * mine, bytes_accessed=16_000_000, transcendentals=0
@@ -70,8 +144,10 @@
 
 def backward_kernel(
     factor, error, dec0, dec1, enc0, enc1, active0, active1, slope0, slope1, block_sum,
-    dpre0, dpre1, sums0, sums1, through,
+    dpre0, dpre1, sums0, sums1, through, error_out, sem,
 ):
+    copy = pltpu.make_async_copy(error, error_out, sem)
+    copy.start()
     product = None
     for dec, enc, active, slope, dpre, sums in (
         (dec0, enc0, active0, slope0, dpre0, sums0),
@@ -94,6 +170,7 @@
     row = product[0:1] + product[1:2] + product[2:3]
     for k in range(through.shape[0]):
         through[k : k + 1, :] = row[:, 128 * k : 128 * (k + 1)] - block_sum[k : k + 1, :]
+    copy.wait()
 
 
 def backward(error, dec, enc, active, slope, block_sum, factor):
@@ -103,9 +180,13 @@
     line = jax.ShapeDtypeStruct((1, mine), f32)
     return pl.pallas_call(
         functools.partial(backward_kernel, factor),
-        out_shape=(half, half, line, line, jax.ShapeDtypeStruct(block_sum.shape, f32)),
+        out_shape=(
+            half, half, line, line, jax.ShapeDtypeStruct(block_sum.shape, f32),
+            jax.ShapeDtypeStruct((count, width), bf16),
+        ),
         in_specs=[VMEM] * 10,
-        out_specs=(VMEM,) * 5,
+        out_specs=(VMEM,) * 5 + (ANY,),
+        scratch_shapes=[pltpu.SemaphoreType.DMA],
         compiler_params=pltpu.CompilerParams(vmem_limit_bytes=VMEM_BYTES),
         cost_estimate=pl.CostEstimate(
             flops=6 * count * width * mine, bytes_accessed=15_000_000, transcendentals=0
@@ -125,31 +206,36 @@
     at = (lax.axis_index("c") * 2 + lax.axis_index("zl")) * 4 + lax.axis_index("x")
     block = lax.dynamic_slice_in_dim(resid_rows, at * piece, piece, 0)
     block = (block.astype(f32) - b_decode).astype(bf16)
-    block = spread(block, ZH, NZH).reshape(rows, width)
+    pieces = spread(block, ZH, NZH)
     dec_float = w_decode.astype(f32)
     norms = jnp.sqrt(jnp.sum(dec_float * dec_float, axis=1) + 1e-06)
     slope0 = (0.5 * factor * norms).reshape(1, -1)
     bias0 = b_encode.reshape(1, -1)
-    block, norms, slope0, slope1, bias0, bias1, enc1, dec1 = tie(
-        block, norms, slope0, swap(slope0), bias0, swap(bias0), swap(w_encode), swap(w_decode)
-    )
-    centered = spread(block, WIDE, NWIDE).reshape(half, width)
-
-    active0, active1, codes0, codes1, part = forward(
+    pieces, norms, slope0, slope1, bias0, bias1, enc1, dec1 = tie(
+        pieces, norms, slope0, swap(slope0), bias0, swap(bias0), swap(w_encode), swap(w_decode)
+    )
+    wide_shape = jax.ShapeDtypeStruct((NWIDE, rows, width), bf16)
+    block, centered, enc1, dec1 = collect(pieces, enc1, dec1, NWIDE)
+    centered = lax.all_to_all(centered, WIDE, 0, 0, tiled=True).reshape(half, width)
+
+    active0, active1, codes0, codes1, part, centered = forward(
         centered, (w_encode, enc1), (w_decode, dec1), (bias0, bias1)
     )
     part = part.reshape(NWIDE, rows, width)
     part = lax.all_to_all(part, WIDE, 0, 0, tiled=True)
-    part = jnp.sum(part.astype(f32), axis=0).astype(bf16)
-    summed = jnp.sum(spread(part, ZH, NZH).astype(f32), axis=0)
-    error_block = (summed - block.astype(f32)).astype(bf16)
-    block_sum = 2.0 * factor / NZH * jnp.sum(error_block.astype(f32), axis=0)
-    block_sum = block_sum.reshape(width // 128, 128)
-    error_block, block_sum = tie(error_block, block_sum)
-    error = spread(error_block, WIDE, NWIDE).reshape(half, width)
+    part = small_kernel(
+        reduce_kernel, jax.ShapeDtypeStruct((NZH, rows, width), bf16), part, name="reduce"
+    )
+    part = lax.all_to_all(part, ZH, 0, 0, tiled=True)
+    error, block_sum = small_kernel(
+        functools.partial(error_kernel, factor),
+        (wide_shape, jax.ShapeDtypeStruct((width // 128, 128), f32)),
+        part, block, name="error",
+    )
+    error = lax.all_to_all(error, WIDE, 0, 0, tiled=True).reshape(half, width)
     error, centered, codes1 = tie(error, centered, codes1)
 
-    dpre0, dpre1, sums0, sums1, through = backward(
+    dpre0, dpre1, sums0, sums1, through, error = backward(
         error, (w_decode, dec1), (w_encode, enc1), (active0, active1), (slope0, slope1),
         block_sum, factor,
     )

time: 174 us -> 166 us (0.954)
  local copies, waits for them, and re-layouts: 8.51 us -> 2.08 us
  waiting for transfers between devices: 6.69 us -> 11 us
  other arithmetic: 9.31 us -> 5.46 us
    unnamed x28 -> x6, local copies, waits for them, and re-layouts: 5.37 us -> 0.01 us
    ppermute x10, waiting for transfers between devices: 0.66 us -> 5.4 us  [swap(): return lax.ppermute(block, 'c', [(0, 1), (1, 0)])]
    reduce_sum x3 -> x0, other arithmetic: 3.28 us -> none  [the longest x1 2.39 us: per_device(): part = jnp.sum(part.astype(f32), axis=0).astype(bf16)]
    pallas_call x1, Pallas kernels: 5.9 us -> 3.55 us  [backward(): pl.pallas_call(functools.partial(backward_kernel, factor), out_shape=(hal...]
    pallas_call x1 -> x4, Pallas kernels: 5.83 us -> 6.79 us  [the longest x1 4.07 us: forward(): pl.pallas_call(forward_kernel, out_shape=(flat, flat, half, half, full, f...]
  transfers between devices with their start and end apart: 13 -> 13, of which waited for: 4 -> 7; matrix products, arithmetic and copies ran while one was open for 11% -> 11% of each run, Pallas kernels for 3% -> 0%
where the time goes in v6:
time: 166 us; the launch traced here: 164 us
  blocking collectives  98.8 us (60%)
  starting transfers between devices  24.4 us (15%)
  matrix products  11.2 us (7%)
  waiting for transfers between devices  11 us (7%)
  Pallas kernels  10.3 us (6%)
  other arithmetic  5.46 us (3%)
  local copies, waits for them, and re-layouts  2.08 us (1%)
    all_to_all x1, blocking collectives, per_device(): lax.all_to_all(centered, WIDE, 0, 0, tiled=True).reshape(half, width)  29.6 us
    all_to_all x1, blocking collectives, per_device(): part = lax.all_to_all(part, WIDE, 0, 0, tiled=True)  26.7 us
    all_to_all x1, blocking collectives, per_device(): error = lax.all_to_all(error, WIDE, 0, 0, tiled=True).reshape(half, width)  26.1 us
    all_to_all x1, blocking collectives, per_device(): part = lax.all_to_all(part, ZH, 0, 0, tiled=True)  16.3 us
    all_to_all x3, starting transfers between devices, spread(): lax.all_to_all(jnp.broadcast_to(block[None], (n,) + block.shape), axes, 0...  13.5 us
    ppermute x10, starting transfers between devices, swap(): return lax.ppermute(block, 'c', [(0, 1), (1, 0)])  10.9 us
    dot_general x1, matrix products, per_device(): jnp.dot(all_rows.T, all_dpre, preferred_element_type=f32).astype(bf16)  5.74 us
    all_to_all x3, waiting for transfers between devices, spread(): lax.all_to_all(jnp.broadcast_to(block[None], (n,) + block.shape), axes, 0...  5.6 us
  transfers between devices with their start and end apart: 13, of which 7 were waited for; matrix products, arithmetic and copies ran while one was open for 11% of the time, Pallas kernels for 0%

profile of v6, /device:TPU:1, one launch (start us, length us, event | category | flops | bytes accessed | tf_op | source)
XLA Modules:
  0.0 163.9 jit_solution(12638760532003050352)
XLA Ops:
  0.6 0.0 copy-start.2
  0.6 3.3 %collective-permute-start.2 = (bf16[3584,384]{1,0:T(8,128)(2,1)}, bf16[3584,384]{1,0:T(8,128)(2,1)S(1)}, u32[]{:S(2)}, u32[]{:S(2)}) collective-permute-start(bf16[3584,384]{1,0:T(8,128)(2,1)} %enc0.3), channel_id=1, source_target_pairs={{0,16},{16,0},{1,17},{17,1},{2,18},{18,2},{3,19},{19,3},{4,20},{20... | collective-permute-start | bytes 8257544 | tf_op jit(solution)/shard_map/ppermute | solution.py:32
  4.0 0.1 collective-permute-start.3
  4.1 0.9 subtract_convert_fusion
  4.9 0.7 broadcast_in_dim.6
  5.6 6.4 %all-to-all-start = ((bf16[4,2,3584]{2,1,0:T(2,128)(2,1)}), bf16[4,2,3584]{2,1,0:T(2,128)(2,1)S(1)}, u32[]{:S(2)}, u32[]{:S(2)}) async-start(bf16[4,2,3584]{2,1,0:T(2,128)(2,1)} %broadcast_in_dim.6), calls=%async_computation | async-start | bytes 114688 | tf_op jit(solution)/shard_map/all_to_all | solution.py:26
  12.0 2.4 %fusion.2 = f32[384]{0:T(512)S(1)} fusion(bf16[384,3584]{1,0:T(8,128)(2,1)} %dec0.3), kind=kLoop, calls=%fused_computation.6 | loop fusion | flops 4128384 | bytes 2754048 | tf_op jit(solution)/shard_map/reduce_sum | solution.py:211
  14.4 0.8 collective-permute-start
  15.2 0.1 collective-permute-start.1
  15.3 0.7 collective-permute-done.slope1
  16.0 0.3 collective-permute-done.1.bias1
  16.4 2.5 %all-to-all-done.pieces = bf16[4,2,3584]{2,1,0:T(2,128)(2,1)S(1)} async-done(((bf16[4,2,3584]{2,1,0:T(2,128)(2,1)}), bf16[4,2,3584]{2,1,0:T(2,128)(2,1)S(1)}, u32[]{:S(2)}, u32[]{:S(2)}) %all-to-all-start) | async-done | bytes 57376 | tf_op jit(solution)/shard_map/all_to_all | solution.py:26
  18.9 0.0 collective-permute-done.2.enc_hbm
  18.9 0.0 collective-permute-done.3.dec_hbm
  18.9 2.3 %collect.1 = (bf16[8,3584]{1,0:T(8,128)(2,1)S(1)}, bf16[32,8,3584]{2,1,0:T(8,128)(2,1)S(1)}, bf16[3584,384]{1,0:T(8,128)(2,1)S(1)}, bf16[384,3584]{1,0:T(8,128)(2,1)S(1)}) custom-call(bf16[4,2,3584]{2,1,0:T(2,128)(2,1)S(1)} %all-to-all-done.pieces, bf16[3584,384]{1,0:T(8,128)(2,1)S(1)} %collective-permute-done.2.enc_hbm, ...), custom_call_target="tpu_custom_call" | custom-call | tf_op jit(solution)/shard_map/collect/pallas_call | solution.py:71
  21.2 0.0 copy-start
  21.2 29.6 %all_to_all.35 = bf16[32,8,3584]{2,1,0:T(8,128)(2,1)S(1)} all-to-all(bf16[32,8,3584]{2,1,0:T(8,128)(2,1)S(1)} %get-tuple-element.42), channel_id=1, replica_groups=mesh['zl'=2,'x'=4,'c'=2,'zh'=4,'y'=4] {'zl','x','y'}, dimensions={0} | all-to-all | bytes 3670016 | tf_op jit(solution)/shard_map/all_to_all | solution.py:219
  50.8 4.1 %forward.1 = (f32[256,384]{1,0:T(8,128)S(1)}, f32[256,384]{1,0:T(8,128)S(1)}, bf16[256,384]{1,0:T(8,128)(2,1)S(1)}, bf16[256,384]{1,0:T(8,128)(2,1)S(1)}, bf16[2...) custom-call(bf16[256,3584]{1,0:T(8,128)(2,1)S(1)} %bitcast.8, bf16[3584,384]{1,0:T(8,128)(2,1)S(1)} %copy-done.1, ...), custom_call_target="tpu_custom_call" | custom-call | flops 2818572288 | bytes 16000000 | tf_op jit(solution)/shard_map/forward/pallas_call | solution.py:131
  54.9 26.7 %all_to_all.36.parts = bf16[32,8,3584]{2,1,0:T(8,128)(2,1)S(1)} all-to-all(bf16[32,8,3584]{2,1,0:T(8,128)(2,1)S(1)} %bitcast.9), channel_id=1, replica_groups=mesh['zl'=2,'x'=4,'c'=2,'zh'=4,'y'=4] {'zl','x','y'}, dimensions={0} | all-to-all | bytes 3670016 | tf_op jit(solution)/shard_map/all_to_all | solution.py:225
  81.6 0.2 reduce.3
  81.9 16.3 %all_to_all.37.parts = bf16[4,8,3584]{2,1,0:T(8,128)(2,1)S(1)} all-to-all(bf16[4,8,3584]{2,1,0:T(8,128)(2,1)S(1)} %reduce.3), channel_id=1, replica_groups=mesh['zl'=2,'x'=4,'c'=2,'zh'=4,'y'=4] {'zh'}, dimensions={0} | all-to-all | bytes 458752 | tf_op jit(solution)/shard_map/all_to_all | solution.py:229
  98.2 0.1 error.1
  98.4 26.1 %all_to_all.38 = bf16[32,8,3584]{2,1,0:T(8,128)(2,1)S(1)} all-to-all(bf16[32,8,3584]{2,1,0:T(8,128)(2,1)S(1)} %get-tuple-element.49), channel_id=1, replica_groups=mesh['zl'=2,'x'=4,'c'=2,'zh'=4,'y'=4] {'zl','x','y'}, dimensions={0} | all-to-all | bytes 3670016 | tf_op jit(solution)/shard_map/all_to_all | solution.py:235
  124.5 3.5 %backward.1 = (bf16[256,384]{1,0:T(8,128)(2,1)S(1)}, bf16[256,384]{1,0:T(8,128)(2,1)S(1)}, f32[1,384]{1,0:T(1,128)S(1)}, f32[1,384]{1,0:T(1,128)S(1)}, f32[28,128]{1,0:T(8,128)S(1)}, /*index=5*/bf16[256,3584]{1,0:T(8,128)(2,1)}) custom-call(bf16[256,3584]{1,0:T(8,128)(2,1)S(1)} %bitcast.7, bf16[384,3584]{1,0:T(8,128)(2,1)S(1)} %copy-done, ...), custom_call_target="tpu_custom_call" | custom-call | flops 2113929216 | bytes 15000000 | tf_op jit(solution)/shard_map/backward/pallas_call | solution.py:181
  128.0 5.2 %collective-permute-start.8 = (bf16[256,3584]{1,0:T(8,128)(2,1)}, bf16[256,3584]{1,0:T(8,128)(2,1)}, u32[]{:S(2)}, u32[]{:S(2)}) collective-permute-start(bf16[256,3584]{1,0:T(8,128)(2,1)} %get-tuple-element.66), channel_id=1, source_target_pairs={{0,16},{16,0},{1,17},{17,1},{2,18},{18,2},{3,19},{19,3},{4,20},{20... | collective-permute-start | bytes 5505032 | tf_op jit(solution)/shard_map/ppermute | solution.py:32
  133.2 0.1 collective-permute-start.4
  133.3 0.4 collective-permute-start.7
  133.7 0.1 collective-permute-start.9
  133.8 0.4 collective-permute-start.5
  134.2 3.0 %collective-permute-done.9 = f32[1,384]{1,0:T(1,128)S(1)} collective-permute-done((f32[1,384]{1,0:T(1,128)S(1)}, f32[1,384]{1,0:T(1,128)S(1)}, u32[]{:S(2)}, u32[]{:S(2)}) %collective-permute-start.9) | collective-permute-done | bytes 1568 | tf_op jit(solution)/shard_map/ppermute | solution.py:32
  137.2 0.4 collective-permute-start.6
  137.6 0.6 add_reduce_fusion
  138.2 1.4 collective-permute-done.5
  139.6 0.0 collective-permute-done.7
  139.6 0.8 pad_maximum_fusion.1
  140.4 0.0 collective-permute-done.6
  140.4 0.7 broadcast_in_dim.7
  141.1 3.4 %all-to-all-start.5 = ((f32[8,28,128]{2,1,0:T(8,128)}), f32[8,28,128]{2,1,0:T(8,128)S(1)}, u32[]{:S(2)}, u32[]{:S(2)}) async-start(f32[8,28,128]{2,1,0:T(8,128)} %broadcast_in_dim.7), calls=%async_computation.5 | async-start | bytes 262144 | tf_op jit(solution)/shard_map/all_to_all | solution.py:26
  144.5 0.1 convert_reduce_fusion
  144.6 0.0 collective-permute-done.8
  144.6 5.4 %fusion.1 = bf16[384,3584]{1,0:T(8,128)(2,1)} fusion(bf16[512,384]{1,0:T(8,128)(2,1)S(1)} %pad_maximum_fusion, bf16[384,3584]{1,0:T(8,128)(2,1)S(1)} %copy-done, bf16[256,3584]{1,0:T(8,128)(2,1)} %collective-permute-done.8, bf16[256,3584]{1,0:T(8,128)(2,1)} %get-tuple-element.66, f32[384]{0:T(512)S(1)} %divide_multiply_fusion), kind=kOutput, calls=%fused_computation.5 | convolution fusion | flops 1423507456 | bytes 9569792 | tf_op jit(solution)/shard_map/dot_general | solution.py:252
  150.0 1.5 all-to-all-done.5
  151.5 0.7 broadcast_in_dim.8
  152.3 3.7 %all-to-all-start.6 = ((f32[16,28,128]{2,1,0:T(8,128)}), f32[16,28,128]{2,1,0:T(8,128)S(1)}, u32[]{:S(2)}, u32[]{:S(2)}) async-start(f32[16,28,128]{2,1,0:T(8,128)} %broadcast_in_dim.8), calls=%async_computation.6 | async-start | bytes 524288 | tf_op jit(solution)/shard_map/all_to_all | solution.py:26
  155.9 0.0 collective-permute-done.4
  155.9 5.7 %convolution_convert_fusion = bf16[3584,384]{1,0:T(8,128)(2,1)} fusion(bf16[512,384]{1,0:T(8,128)(2,1)} %pad_maximum_fusion.1, bf16[256,3584]{1,0:T(8,128)(2,1)} %collective-permute-done.4, bf16[256,3584]{1,0:T(8,128)(2,1)} %get-tuple-element.52), kind=kOutput, calls=%fused_computation.4 | convolution fusion | flops 1418002432 | bytes 6815744 | tf_op jit(solution)/shard_map/dot_general | solution.py:257
  161.7 1.6 all-to-all-done.6
  163.3 0.6 negate_bitcast_fusion
  (12 shorter events, 0.1 us)
Async XLA Ops:
  0.6 14.6 %copy-start.2 = (f32[384]{0:T(512)S(1)}, f32[384]{0:T(512)}, u32[]{:S(2)}) copy-start(f32[384]{0:T(512)} %param.7) | copy-start | bytes 4612
  0.6 18.2 %collective-permute-start.2 = (bf16[3584,384]{1,0:T(8,128)(2,1)}, bf16[3584,384]{1,0:T(8,128)(2,1)S(1)}, u32[]{:S(2)}, u32[]{:S(2)}) collective-permute-start(bf16[3584,384]{1,0:T(8,128)(2,1)} %enc0.3), channel_id=1, source_target_pairs={{0,16},{16,0},{1,17},{17,1},{2,18},{18,2},{3,19},{19,3},{4,20},{20... | collective-permute-start | bytes 8257544 | tf_op jit(solution)/shard_map/ppermute | solution.py:32
  4.0 14.9 %collective-permute-start.3 = (bf16[384,3584]{1,0:T(8,128)(2,1)}, bf16[384,3584]{1,0:T(8,128)(2,1)}, u32[]{:S(2)}, u32[]{:S(2)}) collective-permute-start(bf16[384,3584]{1,0:T(8,128)(2,1)} %dec0.3), channel_id=1, source_target_pairs={{0,16},{16,0},{1,17},{17,1},{2,18},{18,2},{3,19},{19,3},{4,20},{20... | collective-permute-start | bytes 8257544 | tf_op jit(solution)/shard_map/ppermute | solution.py:32
  5.6 13.3 %all-to-all-start = ((bf16[4,2,3584]{2,1,0:T(2,128)(2,1)}), bf16[4,2,3584]{2,1,0:T(2,128)(2,1)S(1)}, u32[]{:S(2)}, u32[]{:S(2)}) async-start(bf16[4,2,3584]{2,1,0:T(2,128)(2,1)} %broadcast_in_dim.6), calls=%async_computation | async-start | bytes 114688 | tf_op jit(solution)/shard_map/all_to_all | solution.py:26
  14.4 1.6 collective-permute-start
  15.2 1.2 collective-permute-start.1
  18.9 31.9 %copy-start.1 = (bf16[3584,384]{1,0:T(8,128)(2,1)S(1)}, bf16[3584,384]{1,0:T(8,128)(2,1)}, u32[]{:S(2)}) copy-start(bf16[3584,384]{1,0:T(8,128)(2,1)} %enc0.3) | copy-start | bytes 8257540
  21.2 29.6 %copy-start = (bf16[384,3584]{1,0:T(8,128)(2,1)S(1)}, bf16[384,3584]{1,0:T(8,128)(2,1)}, u32[]{:S(2)}) copy-start(bf16[384,3584]{1,0:T(8,128)(2,1)} %dec0.3) | copy-start | bytes 8257540
  128.0 16.6 %collective-permute-start.8 = (bf16[256,3584]{1,0:T(8,128)(2,1)}, bf16[256,3584]{1,0:T(8,128)(2,1)}, u32[]{:S(2)}, u32[]{:S(2)}) collective-permute-start(bf16[256,3584]{1,0:T(8,128)(2,1)} %get-tuple-element.66), channel_id=1, source_target_pairs={{0,16},{16,0},{1,17},{17,1},{2,18},{18,2},{3,19},{19,3},{4,20},{20... | collective-permute-start | bytes 5505032 | tf_op jit(solution)/shard_map/ppermute | solution.py:32
  133.2 22.7 %collective-permute-start.4 = (bf16[256,3584]{1,0:T(8,128)(2,1)}, bf16[256,3584]{1,0:T(8,128)(2,1)}, u32[]{:S(2)}, u32[]{:S(2)}) collective-permute-start(bf16[256,3584]{1,0:T(8,128)(2,1)} %get-tuple-element.52), channel_id=1, source_target_pairs={{0,16},{16,0},{1,17},{17,1},{2,18},{18,2},{3,19},{19,3},{4,20},{20... | collective-permute-start | bytes 5505032 | tf_op jit(solution)/shard_map/ppermute | solution.py:32
  133.3 6.2 %collective-permute-start.7 = (bf16[256,384]{1,0:T(8,128)(2,1)S(1)}, bf16[256,384]{1,0:T(8,128)(2,1)S(1)}, u32[]{:S(2)}, u32[]{:S(2)}) collective-permute-start(bf16[256,384]{1,0:T(8,128)(2,1)S(1)} %get-tuple-element.63), channel_id=1, source_target_pairs={{0,16},{16,0},{1,17},{17,1},{2,18},{18,2},{3,19},{19,3},{4,20},{20... | collective-permute-start | bytes 589832 | tf_op jit(solution)/shard_map/ppermute | solution.py:32
  133.7 3.5 %collective-permute-start.9 = (f32[1,384]{1,0:T(1,128)S(1)}, f32[1,384]{1,0:T(1,128)S(1)}, u32[]{:S(2)}, u32[]{:S(2)}) collective-permute-start(f32[1,384]{1,0:T(1,128)S(1)} %get-tuple-element.71), channel_id=1, source_target_pairs={{0,16},{16,0},{1,17},{17,1},{2,18},{18,2},{3,19},{19,3},{4,20},{20... | collective-permute-start | bytes 4616 | tf_op jit(solution)/shard_map/ppermute | solution.py:32
  133.8 5.7 %collective-permute-start.5 = (f32[28,128]{1,0:T(8,128)S(1)}, f32[28,128]{1,0:T(8,128)S(1)}, u32[]{:S(2)}, u32[]{:S(2)}) collective-permute-start(f32[28,128]{1,0:T(8,128)S(1)} %get-tuple-element.59), channel_id=1, source_target_pairs={{0,16},{16,0},{1,17},{17,1},{2,18},{18,2},{3,19},{19,3},{4,20},{20... | collective-permute-start | bytes 43016 | tf_op jit(solution)/shard_map/ppermute | solution.py:32
  137.2 3.2 %collective-permute-start.6 = (bf16[256,384]{1,0:T(8,128)(2,1)S(1)}, bf16[256,384]{1,0:T(8,128)(2,1)S(1)}, u32[]{:S(2)}, u32[]{:S(2)}) collective-permute-start(bf16[256,384]{1,0:T(8,128)(2,1)S(1)} %get-tuple-element.61), channel_id=1, source_target_pairs={{0,16},{16,0},{1,17},{17,1},{2,18},{18,2},{3,19},{19,3},{4,20},{20... | collective-permute-start | bytes 589832 | tf_op jit(solution)/shard_map/ppermute | solution.py:32
  141.1 10.4 %all-to-all-start.5 = ((f32[8,28,128]{2,1,0:T(8,128)}), f32[8,28,128]{2,1,0:T(8,128)S(1)}, u32[]{:S(2)}, u32[]{:S(2)}) async-start(f32[8,28,128]{2,1,0:T(8,128)} %broadcast_in_dim.7), calls=%async_computation.5 | async-start | bytes 262144 | tf_op jit(solution)/shard_map/all_to_all | solution.py:26
  152.3 11.0 %all-to-all-start.6 = ((f32[16,28,128]{2,1,0:T(8,128)}), f32[16,28,128]{2,1,0:T(8,128)S(1)}, u32[]{:S(2)}, u32[]{:S(2)}) async-start(f32[16,28,128]{2,1,0:T(8,128)} %broadcast_in_dim.8), calls=%async_computation.6 | async-start | bytes 524288 | tf_op jit(solution)/shard_map/all_to_all | solution.py:26

commit v7 on v6

v7 whole, which is shorter than its diff:
```python
import functools
import math

import jax
import jax.numpy as jnp
from jax import lax
from jax.experimental import pallas as pl
from jax.experimental.pallas import tpu as pltpu
from jax.sharding import Mesh, PartitionSpec as P

LMAJ = ("zl", "x", "c")
LMIN = ("zh", "y")
WIDE, NWIDE = ("zl", "x", "y"), 32
XY, NXY = ("x", "y"), 16
Z, NZ = ("zl", "zh"), 8
ZH, NZH = ("zh",), 4
f32, bf16 = jnp.float32, jnp.bfloat16
VMEM = pl.BlockSpec(memory_space=pltpu.VMEM)
ANY = pl.BlockSpec(memory_space=pl.ANY)
VMEM_BYTES = 16 * 1024 * 1024
SMALL_BYTES = 6 * 1024 * 1024
GRAD_BYTES = 24 * 1024 * 1024
PART = 896
NT = (((1,), (1,)), ((), ()))


def spread(block, axes, n):
    return lax.all_to_all(
        jnp.broadcast_to(block[None], (n,) + block.shape), axes, 0, 0, tiled=True
    )


def swap(block):
    return lax.ppermute(block, "c", [(0, 1), (1, 0)])


def tie(*values):
    return lax.optimization_barrier(values)


def small_kernel(body, out_shape, *args, name):
    return pl.pallas_call(
        body,
        out_shape=out_shape,
        in_specs=[VMEM] * len(args),
        out_specs=jax.tree.map(lambda _: VMEM, out_shape),
        compiler_params=pltpu.CompilerParams(vmem_limit_bytes=SMALL_BYTES),
        name=name,
    )(*args)


def repeat_into(out, value):
    for k in range(out.shape[0]):
        out[k] = value


def collect_kernel(pieces, bias, block, out):
    value = jnp.concatenate([pieces[k] for k in range(pieces.shape[0])], axis=0)
    value = (value.astype(f32) - bias[...]).astype(bf16)
    block[...] = value
    repeat_into(out, value)


def reduce_kernel(parts, out):
    total = parts[0].astype(f32)
    for k in range(1, parts.shape[0]):
        total += parts[k].astype(f32)
    repeat_into(out, total.astype(bf16))


def error_kernel(factor, parts, block, out, block_sum):
    total = parts[0].astype(f32)
    for k in range(1, parts.shape[0]):
        total += parts[k].astype(f32)
    error = (total - block[...].astype(f32)).astype(bf16)
    repeat_into(out, error)
    row = (2.0 * factor / parts.shape[0]) * jnp.sum(error.astype(f32), axis=0, keepdims=True)
    for k in range(block_sum.shape[0]):
        block_sum[k : k + 1, :] = row[:, 128 * k : 128 * (k + 1)]


def forward_kernel(
    rows, enc0, enc1_hbm, dec0, dec1_hbm, bias0, bias1,
    active0, active1, codes0, codes1, part, rows_out, enc1, dec1, sem,
):
    load_enc = pltpu.make_async_copy(enc1_hbm, enc1, sem.at[0])
    load_dec = pltpu.make_async_copy(dec1_hbm, dec1, sem.at[1])
    copy = pltpu.make_async_copy(rows, rows_out, sem.at[2])
    load_enc.start()
    load_dec.start()

    def encode(enc, bias, active, codes):
        pre = jnp.dot(rows[...], enc[...], preferred_element_type=f32) + bias[...]
        value = jnp.maximum(pre, 0.0)
        active[...] = value
        codes[...] = (value * value).astype(bf16)

    encode(enc0, bias0, active0, codes0)
    load_enc.wait()
    encode(enc1, bias1, active1, codes1)
    copy.start()
    load_dec.wait()
    total = jnp.dot(codes0[...], dec0[...], preferred_element_type=f32)
    total += jnp.dot(codes1[...], dec1[...], preferred_element_type=f32)
    part[...] = total.astype(bf16)
    copy.wait()


def forward(rows, enc, dec, bias):
    count, width = rows.shape
    mine = enc[0].shape[1]
    flat = jax.ShapeDtypeStruct((count, mine), f32)
    half = jax.ShapeDtypeStruct((count, mine), bf16)
    full = jax.ShapeDtypeStruct((count, width), bf16)
    weights = (jax.ShapeDtypeStruct(w.shape, bf16) for w in (enc[1], dec[1]))
    return pl.pallas_call(
        forward_kernel,
        out_shape=(flat, flat, half, half, full, full, *weights),
        in_specs=[VMEM, VMEM, ANY, VMEM, ANY, VMEM, VMEM],
        out_specs=(VMEM,) * 5 + (ANY,) + (VMEM,) * 2,
        scratch_shapes=[pltpu.SemaphoreType.DMA((3,))],
        compiler_params=pltpu.CompilerParams(vmem_limit_bytes=VMEM_BYTES),
        cost_estimate=pl.CostEstimate(
            flops=8 * count * width * mine, bytes_accessed=16_000_000, transcendentals=0
        ),
        name="forward",
    )(rows, enc[0], enc[1], dec[0], dec[1], *bias)


def backward_kernel(
    factor, error, dec0, dec1, enc0, enc1, active0, active1, slope0, slope1, block_sum,
    dpre0, dpre1, sums0, sums1, through, error_out, rounded, sem,
):
    copies = [
        pltpu.make_async_copy(rounded.at[0], dpre0, sem.at[0]),
        pltpu.make_async_copy(rounded.at[1], dpre1, sem.at[1]),
        pltpu.make_async_copy(error, error_out, sem.at[2]),
    ]
    product = None
    for k, (dec, enc, active, slope, sums) in enumerate((
        (dec0, enc0, active0, slope0, sums0),
        (dec1, enc1, active1, slope1, sums1),
    )):
        back = lax.dot_general(error[...], dec[...], NT, preferred_element_type=f32)
        value = (2.0 * factor * back + slope[...]) * 2.0 * active[...]
        rounded[k] = value.astype(bf16)
        copies[k].start()
        total = jnp.sum(value, axis=0, keepdims=True)
        sums[...] = total
        first = total.astype(bf16)
        rest = total - first.astype(f32)
        second = rest.astype(bf16)
        third = (rest - second.astype(f32)).astype(bf16)
        parts = jnp.concatenate(
            [first, second, third, jnp.zeros((13, total.shape[1]), bf16)], axis=0
        )
        term = lax.dot_general(parts, enc[...], NT, preferred_element_type=f32)
        product = term if product is None else product + term
    copies[2].start()
    row = product[0:1] + product[1:2] + product[2:3]
    for k in range(through.shape[0]):
        through[k : k + 1, :] = row[:, 128 * k : 128 * (k + 1)] - block_sum[k : k + 1, :]
    for copy in copies:
        copy.wait()


def backward(error, dec, enc, active, slope, block_sum, factor):
    count, width = error.shape
    mine = enc[0].shape[1]
    half = jax.ShapeDtypeStruct((count, mine), bf16)
    line = jax.ShapeDtypeStruct((1, mine), f32)
    return pl.pallas_call(
        functools.partial(backward_kernel, factor),
        out_shape=(
            half, half, line, line, jax.ShapeDtypeStruct(block_sum.shape, f32),
            jax.ShapeDtypeStruct((count, width), bf16),
        ),
        in_specs=[VMEM] * 10,
        out_specs=(ANY,) * 2 + (VMEM,) * 3 + (ANY,),
        scratch_shapes=[pltpu.VMEM((2, count, mine), bf16), pltpu.SemaphoreType.DMA((3,))],
        compiler_params=pltpu.CompilerParams(vmem_limit_bytes=VMEM_BYTES),
        cost_estimate=pl.CostEstimate(
            flops=6 * count * width * mine, bytes_accessed=15_000_000, transcendentals=0
        ),
        name="backward",
    )(error, *dec, *enc, *active, *slope, block_sum)


def decode_grad_kernel(
    factor, codes0, codes1, error0, error1, dec, norms, out,
    codes_in, error_in, dec_in, out_buf, sem_codes, sem_in, sem_out,
):
    half, width = error0.shape
    first = [
        pltpu.make_async_copy(codes0, codes_in.at[:half], sem_codes.at[0]),
        pltpu.make_async_copy(codes1, codes_in.at[half:], sem_codes.at[1]),
    ]
    loads, stores = [], []
    for k in range(width // PART):
        at = slice(k * PART, (k + 1) * PART)
        loads.append((
            pltpu.make_async_copy(error0.at[:, at], error_in.at[:half, at], sem_in.at[0, k]),
            pltpu.make_async_copy(error1.at[:, at], error_in.at[half:, at], sem_in.at[1, k]),
            pltpu.make_async_copy(dec.at[:, at], dec_in.at[:, at], sem_in.at[2, k]),
        ))
        stores.append(pltpu.make_async_copy(out_buf.at[:, at], out.at[:, at], sem_out.at[k]))
    for group in (first, *loads):
        for copy in group:
            copy.start()
    for copy in first:
        copy.wait()
    codes = codes_in[...].T
    norm = jnp.broadcast_to(norms[...], (8, norms.shape[1])).T[:, :1]
    scale = 0.5 * factor * (jnp.sum(codes.astype(f32), axis=1, keepdims=True) / norm)
    for k in range(width // PART):
        at = slice(k * PART, (k + 1) * PART)
        for copy in loads[k]:
            copy.wait()
        grad = 2.0 * factor * jnp.dot(codes, error_in[:, at], preferred_element_type=f32)
        out_buf[:, at] = (grad + scale * dec_in[:, at].astype(f32)).astype(bf16)
        stores[k].start()
    for copy in stores:
        copy.wait()


def decode_grad(codes, error, dec, norms, factor):
    half, width = error[0].shape
    mine = dec.shape[0]
    steps = width // PART
    return pl.pallas_call(
        functools.partial(decode_grad_kernel, factor),
        out_shape=jax.ShapeDtypeStruct((mine, width), bf16),
        in_specs=[ANY] * 5 + [VMEM],
        out_specs=ANY,
        scratch_shapes=[
            pltpu.VMEM((2 * half, mine), bf16),
            pltpu.VMEM((2 * half, width), bf16),
            pltpu.VMEM((mine, width), bf16),
            pltpu.VMEM((mine, width), bf16),
            pltpu.SemaphoreType.DMA((2,)),
            pltpu.SemaphoreType.DMA((3, steps)),
            pltpu.SemaphoreType.DMA((steps,)),
        ],
        compiler_params=pltpu.CompilerParams(vmem_limit_bytes=GRAD_BYTES),
        cost_estimate=pl.CostEstimate(
            flops=4 * half * width * mine, bytes_accessed=10_000_000, transcendentals=0
        ),
        name="decode_grad",
    )(*codes, *error, dec, norms)


def encode_grad_kernel(
    rows0, rows1, dpre0, dpre1, out, rows_in, dpre_in, out_buf, sem_dpre, sem_in, sem_out
):
    half, width = rows0.shape
    first = [
        pltpu.make_async_copy(dpre0, dpre_in.at[:half], sem_dpre.at[0]),
        pltpu.make_async_copy(dpre1, dpre_in.at[half:], sem_dpre.at[1]),
    ]
    loads, stores = [], []
    for k in range(width // PART):
        at = slice(k * PART, (k + 1) * PART)
        loads.append((
            pltpu.make_async_copy(rows0.at[:, at], rows_in.at[:half, at], sem_in.at[0, k]),
            pltpu.make_async_copy(rows1.at[:, at], rows_in.at[half:, at], sem_in.at[1, k]),
        ))
        stores.append(pltpu.make_async_copy(out_buf.at[at], out.at[at], sem_out.at[k]))
    for group in (first, *loads):
        for copy in group:
            copy.start()
    for copy in first:
        copy.wait()
    for k in range(width // PART):
        at = slice(k * PART, (k + 1) * PART)
        for copy in loads[k]:
            copy.wait()
        out_buf[at] = jnp.dot(
            rows_in[:, at].T, dpre_in[...], preferred_element_type=f32
        ).astype(bf16)
        stores[k].start()
    for copy in stores:
        copy.wait()


def encode_grad(rows, dpre):
    half, width = rows[0].shape
    mine = dpre[0].shape[1]
    steps = width // PART
    return pl.pallas_call(
        encode_grad_kernel,
        out_shape=jax.ShapeDtypeStruct((width, mine), bf16),
        in_specs=[ANY] * 4,
        out_specs=ANY,
        scratch_shapes=[
            pltpu.VMEM((2 * half, width), bf16),
            pltpu.VMEM((2 * half, mine), bf16),
            pltpu.VMEM((width, mine), bf16),
            pltpu.SemaphoreType.DMA((2,)),
            pltpu.SemaphoreType.DMA((2, steps)),
            pltpu.SemaphoreType.DMA((steps,)),
        ],
        compiler_params=pltpu.CompilerParams(vmem_limit_bytes=GRAD_BYTES),
        cost_estimate=pl.CostEstimate(
            flops=4 * half * width * mine, bytes_accessed=7_000_000, transcendentals=0
        ),
        name="encode_grad",
    )(*rows, *dpre)


def per_device(resid_rows, w_encode, b_encode, w_decode, b_decode):
    local_rows, width = resid_rows.shape
    total_rows = local_rows * 16
    half = total_rows // 2
    rows = half // NWIDE
    factor = 1.0 / math.sqrt(total_rows)

    piece = rows // NZH
    at = (lax.axis_index("c") * 2 + lax.axis_index("zl")) * 4 + lax.axis_index("x")
    block = lax.dynamic_slice_in_dim(resid_rows, at * piece, piece, 0)
    pieces = spread(block, ZH, NZH)
    dec_float = w_decode.astype(f32)
    norms = jnp.sqrt(jnp.sum(dec_float * dec_float, axis=1) + 1e-06)
    slope0 = (0.5 * factor * norms).reshape(1, -1)
    bias0 = b_encode.reshape(1, -1)
    center = b_decode.reshape(1, -1)
    pieces, center, norms, slope0, slope1, bias0, bias1, enc1, dec1 = tie(
        pieces, center, norms.reshape(1, -1), slope0, swap(slope0), bias0, swap(bias0),
        swap(w_encode), swap(w_decode),
    )
    wide_shape = jax.ShapeDtypeStruct((NWIDE, rows, width), bf16)
    block_shape = jax.ShapeDtypeStruct((rows, width), bf16)
    block, centered = small_kernel(
        collect_kernel, (block_shape, wide_shape), pieces, center, name="collect"
    )
    centered = lax.all_to_all(centered, WIDE, 0, 0, tiled=True).reshape(half, width)

    active0, active1, codes0, codes1, part, centered, enc1, dec1 = forward(
        centered, (w_encode, enc1), (w_decode, dec1), (bias0, bias1)
    )
    part = part.reshape(NWIDE, rows, width)
    part = lax.all_to_all(part, WIDE, 0, 0, tiled=True)
    part = small_kernel(
        reduce_kernel, jax.ShapeDtypeStruct((NZH, rows, width), bf16), part, name="reduce"
    )
    part = lax.all_to_all(part, ZH, 0, 0, tiled=True)
    error, block_sum = small_kernel(
        functools.partial(error_kernel, factor),
        (wide_shape, jax.ShapeDtypeStruct((width // 128, 128), f32)),
        part, block, name="error",
    )
    error = lax.all_to_all(error, WIDE, 0, 0, tiled=True).reshape(half, width)
    dpre0, dpre1, sums0, sums1, through, error = backward(
        error, (w_decode, dec1), (w_encode, enc1), (active0, active1), (slope0, slope1),
        block_sum, factor,
    )
    through = through + swap(through)
    their_dpre = swap(dpre1)
    through, centered, error, codes1, sums1 = tie(through, centered, error, codes1, sums1)
    their_codes = swap(codes1)
    their_error, their_rows = swap(error), swap(centered)
    through = spread(through, Z, NZ)
    grad_decode = decode_grad(
        (codes0, their_codes), (error, their_error), w_decode, norms, factor
    )
    through, grad_decode, their_dpre = tie(through, grad_decode, their_dpre)
    through = jnp.sum(spread(jnp.sum(through, axis=0), XY, NXY), axis=0).reshape(width)
    grad_encode = encode_grad((centered, their_rows), (dpre0, their_dpre))
    grad_b_encode = (sums0 + swap(sums1)).reshape(-1)
    return (grad_encode, grad_b_encode, grad_decode, -through)


def solution(mesh):
    fine = Mesh(mesh.devices.reshape(2, 4, 2, 4, 4), ("zl", "x", "c", "zh", "y"))
    latents = LMAJ + LMIN
    in_specs = (P(LMIN, None), P(None, latents), P(latents), P(latents, None), P())
    out_specs = (P(None, latents), P(latents), P(latents, None), P())
    return jax.shard_map(
        per_device, mesh=fine, in_specs=in_specs, out_specs=out_specs, check_vma=False
    )
```

time: 166 us -> 161 us (0.970); the launches traced: 164 us -> 161 us
  matrix products: 11.2 us -> 0 us
  Pallas kernels: 10.3 us -> 21.4 us
  waiting for transfers between devices: 11 us -> 6.66 us
  local copies, waits for them, and re-layouts: 2.08 us -> 4.42 us
    dot_general x2 -> x0, matrix products: 11.2 us -> none  [the longest x1 5.74 us: per_device(): jnp.dot(all_rows.T, all_dpre, preferred_element_type=f32).astype(bf16)]
    pallas_call x1 -> x2, Pallas kernels: 2.32 us -> 10.2 us  [the longest x1 5.29 us: encode_grad(): pl.pallas_call(encode_grad_kernel, out_shape=jax.ShapeDtypeStruct((width,...]
    all_to_all x3, waiting for transfers between devices: 5.6 us -> 2.97 us  [spread(): lax.all_to_all(jnp.broadcast_to(block[None], (n,) + block.shape), axes, 0...]
    unnamed x6 -> x16, local copies, waits for them, and re-layouts: 0.01 us -> 2.3 us
    pallas_call x1, Pallas kernels: 4.07 us -> 6.05 us  [forward(): pl.pallas_call(forward_kernel, out_shape=(flat, flat, half, half, full, f...]
    ppermute x10, waiting for transfers between devices: 5.4 us -> 3.7 us  [swap(): return lax.ppermute(block, 'c', [(0, 1), (1, 0)])]
  transfers between devices with their start and end apart: 13 -> 13, of which waited for: 7 -> 6; matrix products, arithmetic and copies ran while one was open for 11% -> 3% of each run, Pallas kernels for 0% -> 6%
where the time goes in v7:
time: 161 us
  blocking collectives  98.8 us (61%)
  starting transfers between devices  24.7 us (15%)
  Pallas kernels  21.4 us (13%)
  waiting for transfers between devices  6.66 us (4%)
  local copies, waits for them, and re-layouts  4.42 us (3%)
  other arithmetic  3.81 us (2%)
    all_to_all x1, blocking collectives, per_device(): lax.all_to_all(centered, WIDE, 0, 0, tiled=True).reshape(half, width)  29.4 us
    all_to_all x1, blocking collectives, per_device(): part = lax.all_to_all(part, WIDE, 0, 0, tiled=True)  26.5 us
    all_to_all x1, blocking collectives, per_device(): error = lax.all_to_all(error, WIDE, 0, 0, tiled=True).reshape(half, width)  26 us
    all_to_all x1, blocking collectives, per_device(): part = lax.all_to_all(part, ZH, 0, 0, tiled=True)  17 us
    all_to_all x3, starting transfers between devices, spread(): lax.all_to_all(jnp.broadcast_to(block[None], (n,) + block.shape), axes, 0...  13.5 us
    ppermute x10, starting transfers between devices, swap(): return lax.ppermute(block, 'c', [(0, 1), (1, 0)])  11.2 us
    pallas_call x1, Pallas kernels, forward(): pl.pallas_call(forward_kernel, out_shape=(flat, flat, half, half, full, f...  6.05 us
    pallas_call x1, Pallas kernels, encode_grad(): pl.pallas_call(encode_grad_kernel, out_shape=jax.ShapeDtypeStruct((width,...  5.29 us
  transfers between devices with their start and end apart: 13, of which 6 were waited for; matrix products, arithmetic and copies ran while one was open for 3% of the time, Pallas kernels for 6%

profile of v7, /device:TPU:1, one launch (start us, length us, event | category | flops | bytes accessed | tf_op | source)
XLA Modules:
  0.0 160.6 jit_solution(6261835112036731191)
XLA Ops:
  0.6 0.0 copy-start
  0.7 3.3 %collective-permute-start.2 = (bf16[3584,384]{1,0:T(8,128)(2,1)}, bf16[3584,384]{1,0:T(8,128)(2,1)}, u32[]{:S(2)}, u32[]{:S(2)}) collective-permute-start(bf16[3584,384]{1,0:T(8,128)(2,1)} %enc0.3), channel_id=1, source_target_pairs={{0,16},{16,0},{1,17},{17,1},{2,18},{18,2},{3,19},{19,3},{4,20},{20... | collective-permute-start | bytes 8257544 | tf_op jit(solution)/shard_map/ppermute | solution.py:34
  4.0 0.1 collective-permute-start.3
  4.1 0.7 broadcast_in_dim.6
  4.8 6.5 %all-to-all-start = ((bf16[4,2,3584]{2,1,0:T(2,128)(2,1)}), bf16[4,2,3584]{2,1,0:T(2,128)(2,1)S(1)}, u32[]{:S(2)}, u32[]{:S(2)}) async-start(bf16[4,2,3584]{2,1,0:T(2,128)(2,1)} %broadcast_in_dim.6), calls=%async_computation | async-start | bytes 114688 | tf_op jit(solution)/shard_map/all_to_all | solution.py:28
  11.3 2.5 %multiply_reduce_fusion = f32[384]{0:T(512)S(1)} fusion(bf16[384,3584]{1,0:T(8,128)(2,1)} %dec.1), kind=kLoop, calls=%fused_computation | loop fusion | flops 4128384 | bytes 2754048 | tf_op jit(solution)/shard_map/reduce_sum | solution.py:322
  13.8 1.0 collective-permute-start
  14.9 0.1 collective-permute-start.1
  15.0 0.7 collective-permute-done.slope1
  15.7 0.3 collective-permute-done.1.bias1
  16.0 2.2 %all-to-all-done.pieces = bf16[4,2,3584]{2,1,0:T(2,128)(2,1)S(1)} async-done(((bf16[4,2,3584]{2,1,0:T(2,128)(2,1)}), bf16[4,2,3584]{2,1,0:T(2,128)(2,1)S(1)}, u32[]{:S(2)}, u32[]{:S(2)}) %all-to-all-start) | async-done | bytes 57376 | tf_op jit(solution)/shard_map/all_to_all | solution.py:28
  18.3 0.0 collective-permute-done.2.enc1_hbm
  18.3 0.0 collective-permute-done.3.dec1_hbm
  18.3 0.1 collect.1
  18.4 29.4 %all_to_all.35 = bf16[32,8,3584]{2,1,0:T(8,128)(2,1)S(1)} all-to-all(bf16[32,8,3584]{2,1,0:T(8,128)(2,1)S(1)} %get-tuple-element.41), channel_id=1, replica_groups=mesh['zl'=2,'x'=4,'c'=2,'zh'=4,'y'=4] {'zl','x','y'}, dimensions={0} | all-to-all | bytes 3670016 | tf_op jit(solution)/shard_map/all_to_all | solution.py:335
  47.8 6.1 %forward.1 = (f32[256,384]{1,0:T(8,128)S(1)}, f32[256,384]{1,0:T(8,128)S(1)}, bf16[256,384]{1,0:T(8,128)(2,1)S(1)}, bf16[256,384]{1,0:T(8,128)(2,1)}, bf16[256,3...) custom-call(bf16[256,3584]{1,0:T(8,128)(2,1)S(1)} %bitcast.6, ...), custom_call_target="tpu_custom_call" | custom-call | flops 2818572288 | bytes 16000000 | tf_op jit(solution)/shard_map/forward/pallas_call | solution.py:116
  53.8 26.5 %all_to_all.36.parts = bf16[32,8,3584]{2,1,0:T(8,128)(2,1)S(1)} all-to-all(bf16[32,8,3584]{2,1,0:T(8,128)(2,1)S(1)} %bitcast.7), channel_id=1, replica_groups=mesh['zl'=2,'x'=4,'c'=2,'zh'=4,'y'=4] {'zl','x','y'}, dimensions={0} | all-to-all | bytes 3670016 | tf_op jit(solution)/shard_map/all_to_all | solution.py:341
  80.3 0.2 reduce.3
  80.5 17.0 %all_to_all.37.parts = bf16[4,8,3584]{2,1,0:T(8,128)(2,1)S(1)} all-to-all(bf16[4,8,3584]{2,1,0:T(8,128)(2,1)S(1)} %reduce.3), channel_id=1, replica_groups=mesh['zl'=2,'x'=4,'c'=2,'zh'=4,'y'=4] {'zh'}, dimensions={0} | all-to-all | bytes 458752 | tf_op jit(solution)/shard_map/all_to_all | solution.py:345
  97.5 0.1 error.1
  97.7 26.0 %all_to_all.38 = bf16[32,8,3584]{2,1,0:T(8,128)(2,1)S(1)} all-to-all(bf16[32,8,3584]{2,1,0:T(8,128)(2,1)S(1)} %get-tuple-element.48), channel_id=1, replica_groups=mesh['zl'=2,'x'=4,'c'=2,'zh'=4,'y'=4] {'zl','x','y'}, dimensions={0} | all-to-all | bytes 3670016 | tf_op jit(solution)/shard_map/all_to_all | solution.py:351
  123.7 4.6 %backward.1 = (bf16[256,384]{1,0:T(8,128)(2,1)S(1)}, bf16[256,384]{1,0:T(8,128)(2,1)S(1)}, f32[1,384]{1,0:T(1,128)S(1)}, f32[1,384]{1,0:T(1,128)S(1)}, f32[28,128]{1,0:T(8,128)S(1)}, /*index=5*/bf16[256,3584]{1,0:T(8,128)(2,1)}) custom-call(bf16[256,3584]{1,0:T(8,128)(2,1)S(1)} %bitcast.5, bf16[384,3584]{1,0:T(8,128)(2,1)S(1)} %copy-done.1, ...), custom_call_target="tpu_custom_call" | custom-call | flops 2113929216 | bytes 15000000 | tf_op jit(solution)/shard_map/backward/pallas_call | solution.py:172
  128.3 0.7 copy-done.5
  129.0 5.2 %collective-permute-start.4 = (f32[28,128]{1,0:T(8,128)S(1)}, f32[28,128]{1,0:T(8,128)S(1)}, u32[]{:S(2)}, u32[]{:S(2)}) collective-permute-start(f32[28,128]{1,0:T(8,128)S(1)} %get-tuple-element.56), channel_id=1, source_target_pairs={{0,16},{16,0},{1,17},{17,1},{2,18},{18,2},{3,19},{19,3},{4,20},{20... | collective-permute-start | bytes 43016 | tf_op jit(solution)/shard_map/ppermute | solution.py:34
  134.1 0.8 collective-permute-done.4
  135.0 0.3 collective-permute-start.7
  135.3 0.2 collective-permute-start.5
  135.5 0.3 collective-permute-start.6
  135.8 0.7 broadcast_in_dim.7
  136.5 3.4 %all-to-all-start.5 = ((f32[8,28,128]{2,1,0:T(8,128)}), f32[8,28,128]{2,1,0:T(8,128)S(1)}, u32[]{:S(2)}, u32[]{:S(2)}) async-start(f32[8,28,128]{2,1,0:T(8,128)} %broadcast_in_dim.7), calls=%async_computation.5 | async-start | bytes 262144 | tf_op jit(solution)/shard_map/all_to_all | solution.py:28
  139.9 0.3 collective-permute-start.8
  140.1 0.3 collective-permute-start.9
  140.5 1.8 %collective-permute-done.6.codes1 = bf16[256,384]{1,0:T(8,128)(2,1)} collective-permute-done((bf16[256,384]{1,0:T(8,128)(2,1)}, bf16[256,384]{1,0:T(8,128)(2,1)}, u32[]{:S(2)}, u32[]{:S(2)}) %collective-permute-start.6) | collective-permute-done | bytes 196640 | tf_op jit(solution)/shard_map/ppermute | solution.py:34
  142.3 0.0 collective-permute-done.7.error1
  142.3 4.9 %decode_grad.1 = bf16[384,3584]{1,0:T(8,128)(2,1)} custom-call(bf16[256,384]{1,0:T(8,128)(2,1)S(1)} %get-tuple-element.64.codes0, bf16[256,384]{1,0:T(8,128)(2,1)} %collective-permute-done.6.codes1, bf16[256,3584]{1,0:T(8,128)(2,1)} %get-tuple-element.66.error0, bf16[256,3584]{1,0:T(8,128)(2,1)} %collective-permute-done.7.error1, ...), custom_call_target="tpu_custom_call" | custom-call | flops 1409286144 | bytes 10000000 | tf_op jit(solution)/shard_map/decode_grad/pallas_call | solution.py:230
  147.3 0.0 collective-permute-done.8.dpre1
  147.3 0.0 copy-start.3
  147.3 0.7 copy-done.3
  148.0 0.0 all-to-all-done.5
  148.0 0.8 broadcast_in_dim.8
  148.7 3.7 %all-to-all-start.6 = ((f32[16,28,128]{2,1,0:T(8,128)}), f32[16,28,128]{2,1,0:T(8,128)S(1)}, u32[]{:S(2)}, u32[]{:S(2)}) async-start(f32[16,28,128]{2,1,0:T(8,128)} %broadcast_in_dim.8), calls=%async_computation.6 | async-start | bytes 524288 | tf_op jit(solution)/shard_map/all_to_all | solution.py:28
  152.4 0.0 collective-permute-done.9
  152.4 0.6 add_reduce_fusion
  153.0 0.0 collective-permute-done.5.rows1
  153.0 0.9 copy-done.4
  154.0 5.3 %encode_grad.1 = bf16[3584,384]{1,0:T(8,128)(2,1)} custom-call(bf16[256,3584]{1,0:T(8,128)(2,1)} %get-tuple-element.61.rows0, bf16[256,3584]{1,0:T(8,128)(2,1)} %collective-permute-done.5.rows1, bf16[256,384]{1,0:T(8,128)(2,1)S(1)} %get-tuple-element.62.dpre0, bf16[256,384]{1,0:T(8,128)(2,1)S(1)} %copy-done.4), custom_call_target="tpu_custom_call" | custom-call | flops 1409286144 | bytes 7000000 | tf_op jit(solution)/shard_map/encode_grad/pallas_call | solution.py:289
  159.3 0.7 all-to-all-done.6
  160.0 0.6 negate_bitcast_fusion
  (20 shorter events, 0.1 us)
Async XLA Ops:
  0.6 3.5 %copy-start = (bf16[32,3584]{1,0:T(8,128)(2,1)S(1)}, bf16[32,3584]{1,0:T(8,128)(2,1)}, u32[]{:S(2)}) copy-start(bf16[32,3584]{1,0:T(8,128)(2,1)} %param.5) | copy-start | bytes 688132
  0.6 14.2 %copy-start.7 = (f32[384]{0:T(512)S(1)}, f32[384]{0:T(512)}, u32[]{:S(2)}) copy-start(f32[384]{0:T(512)} %param.7) | copy-start | bytes 4612
  0.7 14.3 %copy-start.6 = (f32[3584]{0:T(1024)S(1)}, f32[3584]{0:T(1024)}, u32[]{:S(2)}) copy-start(f32[3584]{0:T(1024)} %param.9) | copy-start | bytes 43012
  0.7 17.6 %collective-permute-start.2 = (bf16[3584,384]{1,0:T(8,128)(2,1)}, bf16[3584,384]{1,0:T(8,128)(2,1)}, u32[]{:S(2)}, u32[]{:S(2)}) collective-permute-start(bf16[3584,384]{1,0:T(8,128)(2,1)} %enc0.3), channel_id=1, source_target_pairs={{0,16},{16,0},{1,17},{17,1},{2,18},{18,2},{3,19},{19,3},{4,20},{20... | collective-permute-start | bytes 8257544 | tf_op jit(solution)/shard_map/ppermute | solution.py:34
  4.0 14.3 %collective-permute-start.3 = (bf16[384,3584]{1,0:T(8,128)(2,1)}, bf16[384,3584]{1,0:T(8,128)(2,1)}, u32[]{:S(2)}, u32[]{:S(2)}) collective-permute-start(bf16[384,3584]{1,0:T(8,128)(2,1)} %dec.1), channel_id=1, source_target_pairs={{0,16},{16,0},{1,17},{17,1},{2,18},{18,2},{3,19},{19,3},{4,20},{20... | collective-permute-start | bytes 8257544 | tf_op jit(solution)/shard_map/ppermute | solution.py:34
  4.8 13.5 %all-to-all-start = ((bf16[4,2,3584]{2,1,0:T(2,128)(2,1)}), bf16[4,2,3584]{2,1,0:T(2,128)(2,1)S(1)}, u32[]{:S(2)}, u32[]{:S(2)}) async-start(bf16[4,2,3584]{2,1,0:T(2,128)(2,1)} %broadcast_in_dim.6), calls=%async_computation | async-start | bytes 114688 | tf_op jit(solution)/shard_map/all_to_all | solution.py:28
  11.3 36.5 %copy-start.1 = (bf16[384,3584]{1,0:T(8,128)(2,1)S(1)}, bf16[384,3584]{1,0:T(8,128)(2,1)}, u32[]{:S(2)}) copy-start(bf16[384,3584]{1,0:T(8,128)(2,1)} %dec.1) | copy-start | bytes 8257540
  13.8 1.9 %collective-permute-start = (f32[1,384]{1,0:T(1,128)S(1)}, f32[1,384]{1,0:T(1,128)S(1)}, u32[]{:S(2)}, u32[]{:S(2)}) collective-permute-start(f32[1,384]{1,0:T(1,128)S(1)} %broadcast_multiply_fusion.slope0), channel_id=1, source_target_pairs={{0,16},{16,0},{1,17},{17,1},{2,18},{18,2},{3,19},{19,3},{4,20},{20... | collective-permute-start | bytes 4616 | tf_op jit(solution)/shard_map/ppermute | solution.py:34
  14.9 1.2 collective-permute-start.1
  18.3 29.5 %copy-start.2 = (bf16[3584,384]{1,0:T(8,128)(2,1)S(1)}, bf16[3584,384]{1,0:T(8,128)(2,1)}, u32[]{:S(2)}) copy-start(bf16[3584,384]{1,0:T(8,128)(2,1)} %enc0.3) | copy-start | bytes 8257540
  128.3 0.7 copy-start.5
  129.0 6.0 %collective-permute-start.4 = (f32[28,128]{1,0:T(8,128)S(1)}, f32[28,128]{1,0:T(8,128)S(1)}, u32[]{:S(2)}, u32[]{:S(2)}) collective-permute-start(f32[28,128]{1,0:T(8,128)S(1)} %get-tuple-element.56), channel_id=1, source_target_pairs={{0,16},{16,0},{1,17},{17,1},{2,18},{18,2},{3,19},{19,3},{4,20},{20... | collective-permute-start | bytes 43016 | tf_op jit(solution)/shard_map/ppermute | solution.py:34
  135.0 7.3 %collective-permute-start.7 = (bf16[256,3584]{1,0:T(8,128)(2,1)}, bf16[256,3584]{1,0:T(8,128)(2,1)}, u32[]{:S(2)}, u32[]{:S(2)}) collective-permute-start(bf16[256,3584]{1,0:T(8,128)(2,1)} %get-tuple-element.66.error0), channel_id=1, source_target_pairs={{0,16},{16,0},{1,17},{17,1},{2,18},{18,2},{3,19},{19,3},{4,20},{20... | collective-permute-start | bytes 5505032 | tf_op jit(solution)/shard_map/ppermute | solution.py:34
  135.3 17.7 %collective-permute-start.5 = (bf16[256,3584]{1,0:T(8,128)(2,1)}, bf16[256,3584]{1,0:T(8,128)(2,1)}, u32[]{:S(2)}, u32[]{:S(2)}) collective-permute-start(bf16[256,3584]{1,0:T(8,128)(2,1)} %get-tuple-element.61.rows0), channel_id=1, source_target_pairs={{0,16},{16,0},{1,17},{17,1},{2,18},{18,2},{3,19},{19,3},{4,20},{20... | collective-permute-start | bytes 5505032 | tf_op jit(solution)/shard_map/ppermute | solution.py:34
  135.5 6.8 %collective-permute-start.6 = (bf16[256,384]{1,0:T(8,128)(2,1)}, bf16[256,384]{1,0:T(8,128)(2,1)}, u32[]{:S(2)}, u32[]{:S(2)}) collective-permute-start(bf16[256,384]{1,0:T(8,128)(2,1)} %get-tuple-element.65), channel_id=1, source_target_pairs={{0,16},{16,0},{1,17},{17,1},{2,18},{18,2},{3,19},{19,3},{4,20},{20... | collective-permute-start | bytes 589832 | tf_op jit(solution)/shard_map/ppermute | solution.py:34
  136.5 11.5 %all-to-all-start.5 = ((f32[8,28,128]{2,1,0:T(8,128)}), f32[8,28,128]{2,1,0:T(8,128)S(1)}, u32[]{:S(2)}, u32[]{:S(2)}) async-start(f32[8,28,128]{2,1,0:T(8,128)} %broadcast_in_dim.7), calls=%async_computation.5 | async-start | bytes 262144 | tf_op jit(solution)/shard_map/all_to_all | solution.py:28
  139.9 7.4 %collective-permute-start.8 = (bf16[256,384]{1,0:T(8,128)(2,1)}, bf16[256,384]{1,0:T(8,128)(2,1)S(1)}, u32[]{:S(2)}, u32[]{:S(2)}) collective-permute-start(bf16[256,384]{1,0:T(8,128)(2,1)} %copy-done.5), channel_id=1, source_target_pairs={{0,16},{16,0},{1,17},{17,1},{2,18},{18,2},{3,19},{19,3},{4,20},{20... | collective-permute-start | bytes 589832 | tf_op jit(solution)/shard_map/ppermute | solution.py:34
  140.1 12.3 %collective-permute-start.9 = (f32[1,384]{1,0:T(1,128)S(1)}, f32[1,384]{1,0:T(1,128)S(1)}, u32[]{:S(2)}, u32[]{:S(2)}) collective-permute-start(f32[1,384]{1,0:T(1,128)S(1)} %get-tuple-element.71), channel_id=1, source_target_pairs={{0,16},{16,0},{1,17},{17,1},{2,18},{18,2},{3,19},{19,3},{4,20},{20... | collective-permute-start | bytes 4616 | tf_op jit(solution)/shard_map/ppermute | solution.py:34
  147.3 0.7 copy-start.3
  148.7 11.2 %all-to-all-start.6 = ((f32[16,28,128]{2,1,0:T(8,128)}), f32[16,28,128]{2,1,0:T(8,128)S(1)}, u32[]{:S(2)}, u32[]{:S(2)}) async-start(f32[16,28,128]{2,1,0:T(8,128)} %broadcast_in_dim.8), calls=%async_computation.6 | async-start | bytes 524288 | tf_op jit(solution)/shard_map/all_to_all | solution.py:28
  153.0 0.9 copy-start.4

commit v8 on v7

--- a/solution.py
+++ b/solution.py
@@ -16,11 +16,13 @@
 ZH, NZH = ("zh",), 4
 f32, bf16 = jnp.float32, jnp.bfloat16
 VMEM = pl.BlockSpec(memory_space=pltpu.VMEM)
-ANY = pl.BlockSpec(memory_space=pl.ANY)
+HBM = pl.BlockSpec(memory_space=pl.ANY)
 VMEM_BYTES = 16 * 1024 * 1024
 SMALL_BYTES = 6 * 1024 * 1024
 GRAD_BYTES = 24 * 1024 * 1024
 PART = 896
+ENC_PIECE = 448
+DEC_PIECE = 48
 NT = (((1,), (1,)), ((), ()))
 
 
@@ -54,11 +56,53 @@
         out[k] = value
 
 
-def collect_kernel(pieces, bias, block, out):
+def collect_kernel(pieces, bias, enc_hbm, dec_hbm, block, out, enc, dec, sem):
+    first = lax.axis_index("c") == 0
+
+    def load(source, to, rows, k):
+        at = pl.ds(pl.multiple_of(k * rows, rows), rows)
+        copy = pltpu.make_async_copy(source.at[at], to.at[at], sem.at[0])
+        copy.start()
+        copy.wait()
+
+    @pl.when(first)
+    def _():
+        pl.loop(0, enc.shape[0] // ENC_PIECE)(functools.partial(load, enc_hbm, enc, ENC_PIECE))
+        pl.loop(0, dec.shape[0] // DEC_PIECE)(functools.partial(load, dec_hbm, dec, DEC_PIECE))
+
+    @pl.when(jnp.logical_not(first))
+    def _():
+        copies = (
+            pltpu.make_async_copy(enc_hbm, enc, sem.at[0]),
+            pltpu.make_async_copy(dec_hbm, dec, sem.at[1]),
+        )
+        for copy in copies:
+            copy.start()
+        for copy in copies:
+            copy.wait()
+
     value = jnp.concatenate([pieces[k] for k in range(pieces.shape[0])], axis=0)
     value = (value.astype(f32) - bias[...]).astype(bf16)
     block[...] = value
     repeat_into(out, value)
+
+
+def collect(pieces, bias, enc, dec, wide):
+    count, rows, width = pieces.shape
+    return pl.pallas_call(
+        collect_kernel,
+        out_shape=(
+            jax.ShapeDtypeStruct((count * rows, width), bf16),
+            jax.ShapeDtypeStruct((wide, count * rows, width), bf16),
+            jax.ShapeDtypeStruct(enc.shape, bf16),
+            jax.ShapeDtypeStruct(dec.shape, bf16),
+        ),
+        in_specs=[VMEM, VMEM, HBM, HBM],
+        out_specs=(VMEM,) * 4,
+        scratch_shapes=[pltpu.SemaphoreType.DMA((2,))],
+        compiler_params=pltpu.CompilerParams(vmem_limit_bytes=SMALL_BYTES),
+        name="collect",
+    )(pieces, bias, enc, dec)
 
 
 def reduce_kernel(parts, out):
@@ -80,26 +124,19 @@
 
 
 def forward_kernel(
-    rows, enc0, enc1_hbm, dec0, dec1_hbm, bias0, bias1,
-    active0, active1, codes0, codes1, part, rows_out, enc1, dec1, sem,
+    rows, enc0, enc1, dec0, dec1, bias0, bias1,
+    active0, active1, codes0, codes1, part, rows_out, sem,
 ):
-    load_enc = pltpu.make_async_copy(enc1_hbm, enc1, sem.at[0])
-    load_dec = pltpu.make_async_copy(dec1_hbm, dec1, sem.at[1])
-    copy = pltpu.make_async_copy(rows, rows_out, sem.at[2])
-    load_enc.start()
-    load_dec.start()
-
-    def encode(enc, bias, active, codes):
+    copy = pltpu.make_async_copy(rows, rows_out, sem)
+    copy.start()
+    for enc, bias, active, codes in (
+        (enc0, bias0, active0, codes0),
+        (enc1, bias1, active1, codes1),
+    ):
         pre = jnp.dot(rows[...], enc[...], preferred_element_type=f32) + bias[...]
         value = jnp.maximum(pre, 0.0)
         active[...] = value
         codes[...] = (value * value).astype(bf16)
-
-    encode(enc0, bias0, active0, codes0)
-    load_enc.wait()
-    encode(enc1, bias1, active1, codes1)
-    copy.start()
-    load_dec.wait()
     total = jnp.dot(codes0[...], dec0[...], preferred_element_type=f32)
     total += jnp.dot(codes1[...], dec1[...], preferred_element_type=f32)
     part[...] = total.astype(bf16)
@@ -112,19 +149,18 @@
     flat = jax.ShapeDtypeStruct((count, mine), f32)
     half = jax.ShapeDtypeStruct((count, mine), bf16)
     full = jax.ShapeDtypeStruct((count, width), bf16)
-    weights = (jax.ShapeDtypeStruct(w.shape, bf16) for w in (enc[1], dec[1]))
     return pl.pallas_call(
         forward_kernel,
-        out_shape=(flat, flat, half, half, full, full, *weights),
-        in_specs=[VMEM, VMEM, ANY, VMEM, ANY, VMEM, VMEM],
-        out_specs=(VMEM,) * 5 + (ANY,) + (VMEM,) * 2,
-        scratch_shapes=[pltpu.SemaphoreType.DMA((3,))],
+        out_shape=(flat, flat, half, half, full, full),
+        in_specs=[VMEM] * 7,
+        out_specs=(VMEM,) * 5 + (HBM,),
+        scratch_shapes=[pltpu.SemaphoreType.DMA],
         compiler_params=pltpu.CompilerParams(vmem_limit_bytes=VMEM_BYTES),
         cost_estimate=pl.CostEstimate(
             flops=8 * count * width * mine, bytes_accessed=16_000_000, transcendentals=0
         ),
         name="forward",
-    )(rows, enc[0], enc[1], dec[0], dec[1], *bias)
+    )(rows, *enc, *dec, *bias)
 
 
 def backward_kernel(
@@ -176,7 +212,7 @@
             jax.ShapeDtypeStruct((count, width), bf16),
         ),
         in_specs=[VMEM] * 10,
-        out_specs=(ANY,) * 2 + (VMEM,) * 3 + (ANY,),
+        out_specs=(HBM,) * 2 + (VMEM,) * 3 + (HBM,),
         scratch_shapes=[pltpu.VMEM((2, count, mine), bf16), pltpu.SemaphoreType.DMA((3,))],
         compiler_params=pltpu.CompilerParams(vmem_limit_bytes=VMEM_BYTES),
         cost_estimate=pl.CostEstimate(
@@ -230,8 +266,8 @@
     return pl.pallas_call(
         functools.partial(decode_grad_kernel, factor),
         out_shape=jax.ShapeDtypeStruct((mine, width), bf16),
-        in_specs=[ANY] * 5 + [VMEM],
-        out_specs=ANY,
+        in_specs=[HBM] * 5 + [VMEM],
+        out_specs=HBM,
         scratch_shapes=[
             pltpu.VMEM((2 * half, mine), bf16),
             pltpu.VMEM((2 * half, width), bf16),
@@ -289,8 +325,8 @@
     return pl.pallas_call(
         encode_grad_kernel,
         out_shape=jax.ShapeDtypeStruct((width, mine), bf16),
-        in_specs=[ANY] * 4,
-        out_specs=ANY,
+        in_specs=[HBM] * 4,
+        out_specs=HBM,
         scratch_shapes=[
             pltpu.VMEM((2 * half, width), bf16),
             pltpu.VMEM((2 * half, mine), bf16),
@@ -328,13 +364,10 @@
         swap(w_encode), swap(w_decode),
     )
     wide_shape = jax.ShapeDtypeStruct((NWIDE, rows, width), bf16)
-    block_shape = jax.ShapeDtypeStruct((rows, width), bf16)
-    block, centered = small_kernel(
-        collect_kernel, (block_shape, wide_shape), pieces, center, name="collect"
-    )
+    block, centered, enc1, dec1 = collect(pieces, center, enc1, dec1, NWIDE)
     centered = lax.all_to_all(centered, WIDE, 0, 0, tiled=True).reshape(half, width)
 
-    active0, active1, codes0, codes1, part, centered, enc1, dec1 = forward(
+    active0, active1, codes0, codes1, part, centered = forward(
         centered, (w_encode, enc1), (w_decode, dec1), (bias0, bias1)
     )
     part = part.reshape(NWIDE, rows, width)

time: 161 us -> 151 us (0.938)
  blocking collectives: 98.8 us -> 80.2 us
  starting transfers between devices: 24.7 us -> 31.8 us
    ppermute x10, starting transfers between devices: 11.2 us -> 18.3 us  [swap(): return lax.ppermute(block, 'c', [(0, 1), (1, 0)])]
    all_to_all x1, blocking collectives: 29.4 us -> 23.4 us  [per_device(): lax.all_to_all(centered, WIDE, 0, 0, tiled=True).reshape(half, width)]
    all_to_all x1, blocking collectives: 26.5 us -> 20.5 us  [per_device(): part = lax.all_to_all(part, WIDE, 0, 0, tiled=True)]
    all_to_all x1, blocking collectives: 26 us -> 20.5 us  [per_device(): error = lax.all_to_all(error, WIDE, 0, 0, tiled=True).reshape(half, width)]
    pallas_call x0 -> x1, Pallas kernels: none -> 2.47 us  [collect(): pl.pallas_call(collect_kernel, out_shape=(jax.ShapeDtypeStruct((count * r...]
  transfers between devices with their start and end apart: 13 -> 13, of which waited for: 6 -> 6; matrix products, arithmetic and copies ran while one was open for 3% -> 3% of each run, Pallas kernels for 6% -> 7%
where the time goes in v8:
time: 151 us; the launch traced here: 150 us
  blocking collectives  80.2 us (53%)
  starting transfers between devices  31.8 us (21%)
  Pallas kernels  22.7 us (15%)
  waiting for transfers between devices  6.81 us (5%)
  local copies, waits for them, and re-layouts  4.4 us (3%)
  other arithmetic  3.66 us (2%)
    all_to_all x1, blocking collectives, per_device(): lax.all_to_all(centered, WIDE, 0, 0, tiled=True).reshape(half, width)  23.4 us
    all_to_all x1, blocking collectives, per_device(): part = lax.all_to_all(part, WIDE, 0, 0, tiled=True)  20.5 us
    all_to_all x1, blocking collectives, per_device(): error = lax.all_to_all(error, WIDE, 0, 0, tiled=True).reshape(half, width)  20.5 us
    ppermute x10, starting transfers between devices, swap(): return lax.ppermute(block, 'c', [(0, 1), (1, 0)])  18.3 us
    all_to_all x1, blocking collectives, per_device(): part = lax.all_to_all(part, ZH, 0, 0, tiled=True)  15.9 us
    all_to_all x3, starting transfers between devices, spread(): lax.all_to_all(jnp.broadcast_to(block[None], (n,) + block.shape), axes, 0...  13.5 us
    pallas_call x1, Pallas kernels, encode_grad(): pl.pallas_call(encode_grad_kernel, out_shape=jax.ShapeDtypeStruct((width,...  5.29 us
    pallas_call x1, Pallas kernels, forward(): pl.pallas_call(forward_kernel, out_shape=(flat, flat, half, half, full, f...  5.05 us
  transfers between devices with their start and end apart: 13, of which 6 were waited for; matrix products, arithmetic and copies ran while one was open for 3% of the time, Pallas kernels for 7%

profile of v8, /device:TPU:1, one launch (start us, length us, event | category | flops | bytes accessed | tf_op | source)
XLA Modules:
  0.0 150.4 jit_solution(724394831887117995)
XLA Ops:
  0.6 0.0 copy-start
  0.7 3.3 %collective-permute-start.2 = (bf16[3584,384]{1,0:T(8,128)(2,1)}, bf16[3584,384]{1,0:T(8,128)(2,1)S(1)}, u32[]{:S(2)}, u32[]{:S(2)}) collective-permute-start(bf16[3584,384]{1,0:T(8,128)(2,1)} %enc0.3), channel_id=1, source_target_pairs={{0,16},{16,0},{1,17},{17,1},{2,18},{18,2},{3,19},{19,3},{4,20},{20... | collective-permute-start | bytes 8257544 | tf_op jit(solution)/shard_map/ppermute | solution.py:36
  4.0 0.1 collective-permute-start.3
  4.1 0.7 broadcast_in_dim.6
  4.8 6.5 %all-to-all-start = ((bf16[4,2,3584]{2,1,0:T(2,128)(2,1)}), bf16[4,2,3584]{2,1,0:T(2,128)(2,1)S(1)}, u32[]{:S(2)}, u32[]{:S(2)}) async-start(bf16[4,2,3584]{2,1,0:T(2,128)(2,1)} %broadcast_in_dim.6), calls=%async_computation | async-start | bytes 114688 | tf_op jit(solution)/shard_map/all_to_all | solution.py:30
  11.3 2.4 %multiply_reduce_fusion = f32[384]{0:T(512)S(1)} fusion(bf16[384,3584]{1,0:T(8,128)(2,1)} %dec.1), kind=kLoop, calls=%fused_computation | loop fusion | flops 4128384 | bytes 2754048 | tf_op jit(solution)/shard_map/reduce_sum | solution.py:358
  13.7 1.0 collective-permute-start
  14.7 0.1 collective-permute-start.1
  14.9 0.7 collective-permute-done.slope1
  15.5 0.3 collective-permute-done.1.bias1
  15.9 2.4 %all-to-all-done.pieces = bf16[4,2,3584]{2,1,0:T(2,128)(2,1)S(1)} async-done(((bf16[4,2,3584]{2,1,0:T(2,128)(2,1)}), bf16[4,2,3584]{2,1,0:T(2,128)(2,1)S(1)}, u32[]{:S(2)}, u32[]{:S(2)}) %all-to-all-start) | async-done | bytes 57376 | tf_op jit(solution)/shard_map/all_to_all | solution.py:30
  18.3 0.0 collective-permute-done.2.enc_hbm
  18.3 0.0 collective-permute-done.3.dec_hbm
  18.3 2.5 %collect.1 = (bf16[8,3584]{1,0:T(8,128)(2,1)S(1)}, bf16[32,8,3584]{2,1,0:T(8,128)(2,1)S(1)}, bf16[3584,384]{1,0:T(8,128)(2,1)S(1)}, bf16[384,3584]{1,0:T(8,128)(2,1)S(1)}) custom-call(bf16[4,2,3584]{2,1,0:T(2,128)(2,1)S(1)} %all-to-all-done.pieces, f32[1,3584]{1,0:T(1,128)S(1)} %reshape.53.bias, bf16[3584,384]{1,0:T(8,128)(2,1)S(1)} %collective-permute-done.2.enc_hbm, ...), custom_call_target="tpu_custom_call" | custom-call | tf_op jit(solution)/shard_map/collect/pallas_call | solution.py:92
  20.7 0.0 copy-start.1
  20.8 23.4 %all_to_all.35 = bf16[32,8,3584]{2,1,0:T(8,128)(2,1)S(1)} all-to-all(bf16[32,8,3584]{2,1,0:T(8,128)(2,1)S(1)} %get-tuple-element.43), channel_id=1, replica_groups=mesh['zl'=2,'x'=4,'c'=2,'zh'=4,'y'=4] {'zl','x','y'}, dimensions={0} | all-to-all | bytes 3670016 | tf_op jit(solution)/shard_map/all_to_all | solution.py:368
  44.1 5.0 %forward.1 = (f32[256,384]{1,0:T(8,128)S(1)}, f32[256,384]{1,0:T(8,128)S(1)}, bf16[256,384]{1,0:T(8,128)(2,1)S(1)}, bf16[256,384]{1,0:T(8,128)(2,1)}, bf16[256,3...) custom-call(bf16[256,3584]{1,0:T(8,128)(2,1)S(1)} %bitcast.6, bf16[3584,384]{1,0:T(8,128)(2,1)S(1)} %copy-done.2, ...), custom_call_target="tpu_custom_call" | custom-call | flops 2818572288 | bytes 16000000 | tf_op jit(solution)/shard_map/forward/pallas_call | solution.py:152
  49.2 20.5 %all_to_all.36.parts = bf16[32,8,3584]{2,1,0:T(8,128)(2,1)S(1)} all-to-all(bf16[32,8,3584]{2,1,0:T(8,128)(2,1)S(1)} %bitcast.7), channel_id=1, replica_groups=mesh['zl'=2,'x'=4,'c'=2,'zh'=4,'y'=4] {'zl','x','y'}, dimensions={0} | all-to-all | bytes 3670016 | tf_op jit(solution)/shard_map/all_to_all | solution.py:374
  69.7 0.2 reduce.3
  69.9 15.9 %all_to_all.37.parts = bf16[4,8,3584]{2,1,0:T(8,128)(2,1)S(1)} all-to-all(bf16[4,8,3584]{2,1,0:T(8,128)(2,1)S(1)} %reduce.3), channel_id=1, replica_groups=mesh['zl'=2,'x'=4,'c'=2,'zh'=4,'y'=4] {'zh'}, dimensions={0} | all-to-all | bytes 458752 | tf_op jit(solution)/shard_map/all_to_all | solution.py:378
  85.8 0.1 error.1
  86.0 20.5 %all_to_all.38 = bf16[32,8,3584]{2,1,0:T(8,128)(2,1)S(1)} all-to-all(bf16[32,8,3584]{2,1,0:T(8,128)(2,1)S(1)} %get-tuple-element.50), channel_id=1, replica_groups=mesh['zl'=2,'x'=4,'c'=2,'zh'=4,'y'=4] {'zl','x','y'}, dimensions={0} | all-to-all | bytes 3670016 | tf_op jit(solution)/shard_map/all_to_all | solution.py:384
  106.5 4.6 %backward.1 = (bf16[256,384]{1,0:T(8,128)(2,1)S(1)}, bf16[256,384]{1,0:T(8,128)(2,1)S(1)}, f32[1,384]{1,0:T(1,128)S(1)}, f32[1,384]{1,0:T(1,128)S(1)}, f32[28,128]{1,0:T(8,128)S(1)}, /*index=5*/bf16[256,3584]{1,0:T(8,128)(2,1)}) custom-call(bf16[256,3584]{1,0:T(8,128)(2,1)S(1)} %bitcast.5, bf16[384,3584]{1,0:T(8,128)(2,1)S(1)} %copy-done.1, ...), custom_call_target="tpu_custom_call" | custom-call | flops 2113929216 | bytes 15000000 | tf_op jit(solution)/shard_map/backward/pallas_call | solution.py:208
  111.0 0.7 copy-done.5
  111.7 12.2 %collective-permute-start.4 = (f32[28,128]{1,0:T(8,128)S(1)}, f32[28,128]{1,0:T(8,128)S(1)}, u32[]{:S(2)}, u32[]{:S(2)}) collective-permute-start(f32[28,128]{1,0:T(8,128)S(1)} %get-tuple-element.56), channel_id=1, source_target_pairs={{0,16},{16,0},{1,17},{17,1},{2,18},{18,2},{3,19},{19,3},{4,20},{20... | collective-permute-start | bytes 43016 | tf_op jit(solution)/shard_map/ppermute | solution.py:36
  124.0 0.8 collective-permute-done.4
  124.8 0.3 collective-permute-start.7
  125.2 0.2 collective-permute-start.5
  125.3 0.3 collective-permute-start.6
  125.7 0.7 broadcast_in_dim.7
  126.3 3.4 %all-to-all-start.5 = ((f32[8,28,128]{2,1,0:T(8,128)}), f32[8,28,128]{2,1,0:T(8,128)S(1)}, u32[]{:S(2)}, u32[]{:S(2)}) async-start(f32[8,28,128]{2,1,0:T(8,128)} %broadcast_in_dim.7), calls=%async_computation.5 | async-start | bytes 262144 | tf_op jit(solution)/shard_map/all_to_all | solution.py:30
  129.7 0.3 collective-permute-start.8
  130.0 0.3 collective-permute-start.9
  130.3 1.8 %collective-permute-done.6.codes1 = bf16[256,384]{1,0:T(8,128)(2,1)} collective-permute-done((bf16[256,384]{1,0:T(8,128)(2,1)}, bf16[256,384]{1,0:T(8,128)(2,1)}, u32[]{:S(2)}, u32[]{:S(2)}) %collective-permute-start.6) | collective-permute-done | bytes 196640 | tf_op jit(solution)/shard_map/ppermute | solution.py:36
  132.1 0.0 collective-permute-done.7.error1
  132.1 5.0 %decode_grad.1 = bf16[384,3584]{1,0:T(8,128)(2,1)} custom-call(bf16[256,384]{1,0:T(8,128)(2,1)S(1)} %get-tuple-element.64.codes0, bf16[256,384]{1,0:T(8,128)(2,1)} %collective-permute-done.6.codes1, bf16[256,3584]{1,0:T(8,128)(2,1)} %get-tuple-element.66.error0, bf16[256,3584]{1,0:T(8,128)(2,1)} %collective-permute-done.7.error1, ...), custom_call_target="tpu_custom_call" | custom-call | flops 1409286144 | bytes 10000000 | tf_op jit(solution)/shard_map/decode_grad/pallas_call | solution.py:266
  137.1 0.0 collective-permute-done.8.dpre1
  137.1 0.0 copy-start.3
  137.1 0.7 copy-done.3
  137.8 0.0 all-to-all-done.5
  137.8 0.7 broadcast_in_dim.8
  138.5 3.7 %all-to-all-start.6 = ((f32[16,28,128]{2,1,0:T(8,128)}), f32[16,28,128]{2,1,0:T(8,128)S(1)}, u32[]{:S(2)}, u32[]{:S(2)}) async-start(f32[16,28,128]{2,1,0:T(8,128)} %broadcast_in_dim.8), calls=%async_computation.6 | async-start | bytes 524288 | tf_op jit(solution)/shard_map/all_to_all | solution.py:30
  142.2 0.0 collective-permute-done.9
  142.2 0.6 add_reduce_fusion
  142.8 0.9 copy-done.4
  143.7 5.3 %encode_grad.1 = bf16[3584,384]{1,0:T(8,128)(2,1)} custom-call(bf16[256,3584]{1,0:T(8,128)(2,1)} %get-tuple-element.61.rows0, bf16[256,3584]{1,0:T(8,128)(2,1)} %collective-permute-done.5.rows1, bf16[256,384]{1,0:T(8,128)(2,1)S(1)} %get-tuple-element.62.dpre0, bf16[256,384]{1,0:T(8,128)(2,1)S(1)} %copy-done.4), custom_call_target="tpu_custom_call" | custom-call | flops 1409286144 | bytes 7000000 | tf_op jit(solution)/shard_map/encode_grad/pallas_call | solution.py:325
  149.0 0.7 all-to-all-done.6
  149.8 0.6 negate_bitcast_fusion
  (20 shorter events, 0.1 us)
Async XLA Ops:
  0.6 3.5 %copy-start = (bf16[32,3584]{1,0:T(8,128)(2,1)S(1)}, bf16[32,3584]{1,0:T(8,128)(2,1)}, u32[]{:S(2)}) copy-start(bf16[32,3584]{1,0:T(8,128)(2,1)} %param.5) | copy-start | bytes 688132
  0.6 14.1 %copy-start.7 = (f32[384]{0:T(512)S(1)}, f32[384]{0:T(512)}, u32[]{:S(2)}) copy-start(f32[384]{0:T(512)} %param.7) | copy-start | bytes 4612
  0.7 14.2 %copy-start.6 = (f32[3584]{0:T(1024)S(1)}, f32[3584]{0:T(1024)}, u32[]{:S(2)}) copy-start(f32[3584]{0:T(1024)} %param.9) | copy-start | bytes 43012
  0.7 17.6 %collective-permute-start.2 = (bf16[3584,384]{1,0:T(8,128)(2,1)}, bf16[3584,384]{1,0:T(8,128)(2,1)S(1)}, u32[]{:S(2)}, u32[]{:S(2)}) collective-permute-start(bf16[3584,384]{1,0:T(8,128)(2,1)} %enc0.3), channel_id=1, source_target_pairs={{0,16},{16,0},{1,17},{17,1},{2,18},{18,2},{3,19},{19,3},{4,20},{20... | collective-permute-start | bytes 8257544 | tf_op jit(solution)/shard_map/ppermute | solution.py:36
  4.0 14.3 %collective-permute-start.3 = (bf16[384,3584]{1,0:T(8,128)(2,1)}, bf16[384,3584]{1,0:T(8,128)(2,1)}, u32[]{:S(2)}, u32[]{:S(2)}) collective-permute-start(bf16[384,3584]{1,0:T(8,128)(2,1)} %dec.1), channel_id=1, source_target_pairs={{0,16},{16,0},{1,17},{17,1},{2,18},{18,2},{3,19},{19,3},{4,20},{20... | collective-permute-start | bytes 8257544 | tf_op jit(solution)/shard_map/ppermute | solution.py:36
  4.8 13.5 %all-to-all-start = ((bf16[4,2,3584]{2,1,0:T(2,128)(2,1)}), bf16[4,2,3584]{2,1,0:T(2,128)(2,1)S(1)}, u32[]{:S(2)}, u32[]{:S(2)}) async-start(bf16[4,2,3584]{2,1,0:T(2,128)(2,1)} %broadcast_in_dim.6), calls=%async_computation | async-start | bytes 114688 | tf_op jit(solution)/shard_map/all_to_all | solution.py:30
  13.7 1.9 %collective-permute-start = (f32[1,384]{1,0:T(1,128)S(1)}, f32[1,384]{1,0:T(1,128)S(1)}, u32[]{:S(2)}, u32[]{:S(2)}) collective-permute-start(f32[1,384]{1,0:T(1,128)S(1)} %broadcast_multiply_fusion.slope0), channel_id=1, source_target_pairs={{0,16},{16,0},{1,17},{17,1},{2,18},{18,2},{3,19},{19,3},{4,20},{20... | collective-permute-start | bytes 4616 | tf_op jit(solution)/shard_map/ppermute | solution.py:36
  14.7 1.2 collective-permute-start.1
  18.3 25.9 %copy-start.2 = (bf16[3584,384]{1,0:T(8,128)(2,1)S(1)}, bf16[3584,384]{1,0:T(8,128)(2,1)}, u32[]{:S(2)}) copy-start(bf16[3584,384]{1,0:T(8,128)(2,1)} %enc0.3) | copy-start | bytes 8257540
  20.7 23.4 %copy-start.1 = (bf16[384,3584]{1,0:T(8,128)(2,1)S(1)}, bf16[384,3584]{1,0:T(8,128)(2,1)}, u32[]{:S(2)}) copy-start(bf16[384,3584]{1,0:T(8,128)(2,1)} %dec.1) | copy-start | bytes 8257540
  111.0 0.7 copy-start.5
  111.7 13.1 %collective-permute-start.4 = (f32[28,128]{1,0:T(8,128)S(1)}, f32[28,128]{1,0:T(8,128)S(1)}, u32[]{:S(2)}, u32[]{:S(2)}) collective-permute-start(f32[28,128]{1,0:T(8,128)S(1)} %get-tuple-element.56), channel_id=1, source_target_pairs={{0,16},{16,0},{1,17},{17,1},{2,18},{18,2},{3,19},{19,3},{4,20},{20... | collective-permute-start | bytes 43016 | tf_op jit(solution)/shard_map/ppermute | solution.py:36
  124.8 7.3 %collective-permute-start.7 = (bf16[256,3584]{1,0:T(8,128)(2,1)}, bf16[256,3584]{1,0:T(8,128)(2,1)}, u32[]{:S(2)}, u32[]{:S(2)}) collective-permute-start(bf16[256,3584]{1,0:T(8,128)(2,1)} %get-tuple-element.66.error0), channel_id=1, source_target_pairs={{0,16},{16,0},{1,17},{17,1},{2,18},{18,2},{3,19},{19,3},{4,20},{20... | collective-permute-start | bytes 5505032 | tf_op jit(solution)/shard_map/ppermute | solution.py:36
  125.2 17.7 %collective-permute-start.5 = (bf16[256,3584]{1,0:T(8,128)(2,1)}, bf16[256,3584]{1,0:T(8,128)(2,1)}, u32[]{:S(2)}, u32[]{:S(2)}) collective-permute-start(bf16[256,3584]{1,0:T(8,128)(2,1)} %get-tuple-element.61.rows0), channel_id=1, source_target_pairs={{0,16},{16,0},{1,17},{17,1},{2,18},{18,2},{3,19},{19,3},{4,20},{20... | collective-permute-start | bytes 5505032 | tf_op jit(solution)/shard_map/ppermute | solution.py:36
  125.3 6.8 %collective-permute-start.6 = (bf16[256,384]{1,0:T(8,128)(2,1)}, bf16[256,384]{1,0:T(8,128)(2,1)}, u32[]{:S(2)}, u32[]{:S(2)}) collective-permute-start(bf16[256,384]{1,0:T(8,128)(2,1)} %get-tuple-element.65), channel_id=1, source_target_pairs={{0,16},{16,0},{1,17},{17,1},{2,18},{18,2},{3,19},{19,3},{4,20},{20... | collective-permute-start | bytes 589832 | tf_op jit(solution)/shard_map/ppermute | solution.py:36
  126.3 11.5 %all-to-all-start.5 = ((f32[8,28,128]{2,1,0:T(8,128)}), f32[8,28,128]{2,1,0:T(8,128)S(1)}, u32[]{:S(2)}, u32[]{:S(2)}) async-start(f32[8,28,128]{2,1,0:T(8,128)} %broadcast_in_dim.7), calls=%async_computation.5 | async-start | bytes 262144 | tf_op jit(solution)/shard_map/all_to_all | solution.py:30
  129.7 7.4 %collective-permute-start.8 = (bf16[256,384]{1,0:T(8,128)(2,1)}, bf16[256,384]{1,0:T(8,128)(2,1)S(1)}, u32[]{:S(2)}, u32[]{:S(2)}) collective-permute-start(bf16[256,384]{1,0:T(8,128)(2,1)} %copy-done.5), channel_id=1, source_target_pairs={{0,16},{16,0},{1,17},{17,1},{2,18},{18,2},{3,19},{19,3},{4,20},{20... | collective-permute-start | bytes 589832 | tf_op jit(solution)/shard_map/ppermute | solution.py:36
  130.0 12.2 %collective-permute-start.9 = (f32[1,384]{1,0:T(1,128)S(1)}, f32[1,384]{1,0:T(1,128)S(1)}, u32[]{:S(2)}, u32[]{:S(2)}) collective-permute-start(f32[1,384]{1,0:T(1,128)S(1)} %get-tuple-element.71), channel_id=1, source_target_pairs={{0,16},{16,0},{1,17},{17,1},{2,18},{18,2},{3,19},{19,3},{4,20},{20... | collective-permute-start | bytes 4616 | tf_op jit(solution)/shard_map/ppermute | solution.py:36
  137.1 0.7 copy-start.3
  138.5 11.2 %all-to-all-start.6 = ((f32[16,28,128]{2,1,0:T(8,128)}), f32[16,28,128]{2,1,0:T(8,128)S(1)}, u32[]{:S(2)}, u32[]{:S(2)}) async-start(f32[16,28,128]{2,1,0:T(8,128)} %broadcast_in_dim.8), calls=%async_computation.6 | async-start | bytes 524288 | tf_op jit(solution)/shard_map/all_to_all | solution.py:30
  142.8 0.9 copy-start.4

commit v9 on v8

--- a/solution.py
+++ b/solution.py
@@ -125,22 +125,28 @@
 
 def forward_kernel(
     rows, enc0, enc1, dec0, dec1, bias0, bias1,
-    active0, active1, codes0, codes1, part, rows_out, sem,
+    active0, active1, codes0_out, codes1_out, part, rows_out, codes0, codes1, sem,
 ):
-    copy = pltpu.make_async_copy(rows, rows_out, sem)
-    copy.start()
-    for enc, bias, active, codes in (
+    copies = [
+        pltpu.make_async_copy(codes0, codes0_out, sem.at[0]),
+        pltpu.make_async_copy(codes1, codes1_out, sem.at[1]),
+        pltpu.make_async_copy(rows, rows_out, sem.at[2]),
+    ]
+    copies[2].start()
+    for k, (enc, bias, active, codes) in enumerate((
         (enc0, bias0, active0, codes0),
         (enc1, bias1, active1, codes1),
-    ):
+    )):
         pre = jnp.dot(rows[...], enc[...], preferred_element_type=f32) + bias[...]
         value = jnp.maximum(pre, 0.0)
         active[...] = value
         codes[...] = (value * value).astype(bf16)
+        copies[k].start()
     total = jnp.dot(codes0[...], dec0[...], preferred_element_type=f32)
     total += jnp.dot(codes1[...], dec1[...], preferred_element_type=f32)
     part[...] = total.astype(bf16)
-    copy.wait()
+    for copy in copies:
+        copy.wait()
 
 
 def forward(rows, enc, dec, bias):
@@ -153,8 +159,12 @@
         forward_kernel,
         out_shape=(flat, flat, half, half, full, full),
         in_specs=[VMEM] * 7,
-        out_specs=(VMEM,) * 5 + (HBM,),
-        scratch_shapes=[pltpu.SemaphoreType.DMA],
+        out_specs=(VMEM, VMEM, HBM, HBM, VMEM, HBM),
+        scratch_shapes=[
+            pltpu.VMEM((count, mine), bf16),
+            pltpu.VMEM((count, mine), bf16),
+            pltpu.SemaphoreType.DMA((3,)),
+        ],
         compiler_params=pltpu.CompilerParams(vmem_limit_bytes=VMEM_BYTES),
         cost_estimate=pl.CostEstimate(
             flops=8 * count * width * mine, bytes_accessed=16_000_000, transcendentals=0
@@ -165,13 +175,15 @@
 
 def backward_kernel(
     factor, error, dec0, dec1, enc0, enc1, active0, active1, slope0, slope1, block_sum,
-    dpre0, dpre1, sums0, sums1, through, error_out, rounded, sem,
+    sums0, sums1, through, out, rounded, sem,
 ):
+    width, mine = error.shape[1], rounded.shape[2]
     copies = [
-        pltpu.make_async_copy(rounded.at[0], dpre0, sem.at[0]),
-        pltpu.make_async_copy(rounded.at[1], dpre1, sem.at[1]),
-        pltpu.make_async_copy(error, error_out, sem.at[2]),
+        pltpu.make_async_copy(rounded.at[0], out.at[:, width : width + mine], sem.at[0]),
+        pltpu.make_async_copy(rounded.at[1], out.at[:, width + mine :], sem.at[1]),
+        pltpu.make_async_copy(error, out.at[:, :width], sem.at[2]),
     ]
+    copies[2].start()
     product = None
     for k, (dec, enc, active, slope, sums) in enumerate((
         (dec0, enc0, active0, slope0, sums0),
@@ -192,7 +204,6 @@
         )
         term = lax.dot_general(parts, enc[...], NT, preferred_element_type=f32)
         product = term if product is None else product + term
-    copies[2].start()
     row = product[0:1] + product[1:2] + product[2:3]
     for k in range(through.shape[0]):
         through[k : k + 1, :] = row[:, 128 * k : 128 * (k + 1)] - block_sum[k : k + 1, :]
@@ -203,16 +214,15 @@
 def backward(error, dec, enc, active, slope, block_sum, factor):
     count, width = error.shape
     mine = enc[0].shape[1]
-    half = jax.ShapeDtypeStruct((count, mine), bf16)
     line = jax.ShapeDtypeStruct((1, mine), f32)
     return pl.pallas_call(
         functools.partial(backward_kernel, factor),
         out_shape=(
-            half, half, line, line, jax.ShapeDtypeStruct(block_sum.shape, f32),
-            jax.ShapeDtypeStruct((count, width), bf16),
+            line, line, jax.ShapeDtypeStruct(block_sum.shape, f32),
+            jax.ShapeDtypeStruct((count, width + 2 * mine), bf16),
         ),
         in_specs=[VMEM] * 10,
-        out_specs=(HBM,) * 2 + (VMEM,) * 3 + (HBM,),
+        out_specs=(VMEM,) * 3 + (HBM,),
         scratch_shapes=[pltpu.VMEM((2, count, mine), bf16), pltpu.SemaphoreType.DMA((3,))],
         compiler_params=pltpu.CompilerParams(vmem_limit_bytes=VMEM_BYTES),
         cost_estimate=pl.CostEstimate(
@@ -226,7 +236,7 @@
     factor, codes0, codes1, error0, error1, dec, norms, out,
     codes_in, error_in, dec_in, out_buf, sem_codes, sem_in, sem_out,
 ):
-    half, width = error0.shape
+    half, width = error0.shape[0], dec.shape[1]
     first = [
         pltpu.make_async_copy(codes0, codes_in.at[:half], sem_codes.at[0]),
         pltpu.make_async_copy(codes1, codes_in.at[half:], sem_codes.at[1]),
@@ -260,8 +270,8 @@
 
 
 def decode_grad(codes, error, dec, norms, factor):
-    half, width = error[0].shape
-    mine = dec.shape[0]
+    half = error[0].shape[0]
+    mine, width = dec.shape
     steps = width // PART
     return pl.pallas_call(
         functools.partial(decode_grad_kernel, factor),
@@ -286,9 +296,12 @@
 
 
 def encode_grad_kernel(
-    rows0, rows1, dpre0, dpre1, out, rows_in, dpre_in, out_buf, sem_dpre, sem_in, sem_out
+    rows0, rows1, error0, error1, out, rows_in, dpre_in, out_buf, sem_dpre, sem_in, sem_out
 ):
     half, width = rows0.shape
+    mine = out.shape[1]
+    dpre0 = error0.at[:, width : width + mine]
+    dpre1 = error1.at[:, width + mine :]
     first = [
         pltpu.make_async_copy(dpre0, dpre_in.at[:half], sem_dpre.at[0]),
         pltpu.make_async_copy(dpre1, dpre_in.at[half:], sem_dpre.at[1]),
@@ -318,9 +331,9 @@
         copy.wait()
 
 
-def encode_grad(rows, dpre):
+def encode_grad(rows, error):
     half, width = rows[0].shape
-    mine = dpre[0].shape[1]
+    mine = (error[0].shape[1] - width) // 2
     steps = width // PART
     return pl.pallas_call(
         encode_grad_kernel,
@@ -340,7 +353,7 @@
             flops=4 * half * width * mine, bytes_accessed=7_000_000, transcendentals=0
         ),
         name="encode_grad",
-    )(*rows, *dpre)
+    )(*rows, *error)
 
 
 def per_device(resid_rows, w_encode, b_encode, w_decode, b_decode):
@@ -382,12 +395,11 @@
         part, block, name="error",
     )
     error = lax.all_to_all(error, WIDE, 0, 0, tiled=True).reshape(half, width)
-    dpre0, dpre1, sums0, sums1, through, error = backward(
+    sums0, sums1, through, error = backward(
         error, (w_decode, dec1), (w_encode, enc1), (active0, active1), (slope0, slope1),
         block_sum, factor,
     )
     through = through + swap(through)
-    their_dpre = swap(dpre1)
     through, centered, error, codes1, sums1 = tie(through, centered, error, codes1, sums1)
     their_codes = swap(codes1)
     their_error, their_rows = swap(error), swap(centered)
@@ -395,9 +407,9 @@
     grad_decode = decode_grad(
         (codes0, their_codes), (error, their_error), w_decode, norms, factor
     )
-    through, grad_decode, their_dpre = tie(through, grad_decode, their_dpre)
+    through, grad_decode, their_rows = tie(through, grad_decode, their_rows)
     through = jnp.sum(spread(jnp.sum(through, axis=0), XY, NXY), axis=0).reshape(width)
-    grad_encode = encode_grad((centered, their_rows), (dpre0, their_dpre))
+    grad_encode = encode_grad((centered, their_rows), (error, their_error))
     grad_b_encode = (sums0 + swap(sums1)).reshape(-1)
     return (grad_encode, grad_b_encode, grad_decode, -through)
 

time: 151 us -> 149 us (0.987)
  local copies, waits for them, and re-layouts: 4.4 us -> 2.13 us
    unnamed x16 -> x10, local copies, waits for them, and re-layouts: 2.32 us -> 0.03 us
    all_to_all x3, waiting for transfers between devices: 3.12 us -> 5.16 us  [spread(): lax.all_to_all(jnp.broadcast_to(block[None], (n,) + block.shape), axes, 0...]
    ppermute x10 -> x9, waiting for transfers between devices: 3.7 us -> 1.87 us  [swap(): return lax.ppermute(block, 'c', [(0, 1), (1, 0)])]
    ppermute x10 -> x9, starting transfers between devices: 18.3 us -> 18 us  [swap(): return lax.ppermute(block, 'c', [(0, 1), (1, 0)])]
  transfers between devices with their start and end apart: 13 -> 12, of which waited for: 6 -> 6; matrix products, arithmetic and copies ran while one was open for 3% -> 3% of each run, Pallas kernels for 7% -> 7%
where the time goes in v9:
time: 149 us; the launch traced here: 147 us
  blocking collectives  80.2 us (54%)
  starting transfers between devices  31.5 us (21%)
  Pallas kernels  21.7 us (15%)
  waiting for transfers between devices  7.03 us (5%)
  other arithmetic  3.66 us (2%)
  local copies, waits for them, and re-layouts  2.13 us (1%)
    all_to_all x1, blocking collectives, per_device(): lax.all_to_all(centered, WIDE, 0, 0, tiled=True).reshape(half, width)  23.4 us
    all_to_all x1, blocking collectives, per_device(): part = lax.all_to_all(part, WIDE, 0, 0, tiled=True)  20.5 us
    all_to_all x1, blocking collectives, per_device(): error = lax.all_to_all(error, WIDE, 0, 0, tiled=True).reshape(half, width)  20.5 us
    ppermute x9, starting transfers between devices, swap(): return lax.ppermute(block, 'c', [(0, 1), (1, 0)])  18 us
    all_to_all x1, blocking collectives, per_device(): part = lax.all_to_all(part, ZH, 0, 0, tiled=True)  15.9 us
    all_to_all x3, starting transfers between devices, spread(): lax.all_to_all(jnp.broadcast_to(block[None], (n,) + block.shape), axes, 0...  13.5 us
    pallas_call x1, Pallas kernels, encode_grad(): pl.pallas_call(encode_grad_kernel, out_shape=jax.ShapeDtypeStruct((width,...  5.63 us
    all_to_all x3, waiting for transfers between devices, spread(): lax.all_to_all(jnp.broadcast_to(block[None], (n,) + block.shape), axes, 0...  5.16 us
  transfers between devices with their start and end apart: 12, of which 6 were waited for; matrix products, arithmetic and copies ran while one was open for 3% of the time, Pallas kernels for 7%

profile of v9, /device:TPU:1, one launch (start us, length us, event | category | flops | bytes accessed | tf_op | source)
XLA Modules:
  0.0 147.0 jit_solution(1847377509320683661)
XLA Ops:
  0.6 0.0 copy-start
  0.6 0.0 copy-start.4
  0.7 0.0 copy-start.3
  0.7 3.3 %collective-permute-start.2 = (bf16[3584,384]{1,0:T(8,128)(2,1)}, bf16[3584,384]{1,0:T(8,128)(2,1)S(1)}, u32[]{:S(2)}, u32[]{:S(2)}) collective-permute-start(bf16[3584,384]{1,0:T(8,128)(2,1)} %enc0.3), channel_id=1, source_target_pairs={{0,16},{16,0},{1,17},{17,1},{2,18},{18,2},{3,19},{19,3},{4,20},{20... | collective-permute-start | bytes 8257544 | tf_op jit(solution)/shard_map/ppermute | solution.py:36
  4.0 0.1 collective-permute-start.3
  4.1 0.0 copy-done
  4.1 0.7 broadcast_in_dim.6
  4.8 6.5 %all-to-all-start = ((bf16[4,2,3584]{2,1,0:T(2,128)(2,1)}), bf16[4,2,3584]{2,1,0:T(2,128)(2,1)S(1)}, u32[]{:S(2)}, u32[]{:S(2)}) async-start(bf16[4,2,3584]{2,1,0:T(2,128)(2,1)} %broadcast_in_dim.6), calls=%async_computation | async-start | bytes 114688 | tf_op jit(solution)/shard_map/all_to_all | solution.py:30
  11.3 2.4 %multiply_reduce_fusion = f32[384]{0:T(512)S(1)} fusion(bf16[384,3584]{1,0:T(8,128)(2,1)} %dec.1), kind=kLoop, calls=%fused_computation | loop fusion | flops 4128384 | bytes 2754048 | tf_op jit(solution)/shard_map/reduce_sum | solution.py:371
  13.7 1.0 collective-permute-start
  14.7 0.1 collective-permute-start.1
  14.8 0.0 copy-done.3
  14.9 0.7 collective-permute-done.slope1
  15.5 0.3 collective-permute-done.1.bias1
  15.9 2.4 %all-to-all-done.pieces = bf16[4,2,3584]{2,1,0:T(2,128)(2,1)S(1)} async-done(((bf16[4,2,3584]{2,1,0:T(2,128)(2,1)}), bf16[4,2,3584]{2,1,0:T(2,128)(2,1)S(1)}, u32[]{:S(2)}, u32[]{:S(2)}) %all-to-all-start) | async-done | bytes 57376 | tf_op jit(solution)/shard_map/all_to_all | solution.py:30
  18.3 0.0 collective-permute-done.2.enc_hbm
  18.3 0.0 collective-permute-done.3.dec_hbm
  18.3 2.5 %collect.1 = (bf16[8,3584]{1,0:T(8,128)(2,1)S(1)}, bf16[32,8,3584]{2,1,0:T(8,128)(2,1)S(1)}, bf16[3584,384]{1,0:T(8,128)(2,1)S(1)}, bf16[384,3584]{1,0:T(8,128)(2,1)S(1)}) custom-call(bf16[4,2,3584]{2,1,0:T(2,128)(2,1)S(1)} %all-to-all-done.pieces, f32[1,3584]{1,0:T(1,128)S(1)} %reshape.53.bias, bf16[3584,384]{1,0:T(8,128)(2,1)S(1)} %collective-permute-done.2.enc_hbm, ...), custom_call_target="tpu_custom_call" | custom-call | tf_op jit(solution)/shard_map/collect/pallas_call | solution.py:92
  20.7 0.0 copy-start.1
  20.8 23.4 %all_to_all.35 = bf16[32,8,3584]{2,1,0:T(8,128)(2,1)S(1)} all-to-all(bf16[32,8,3584]{2,1,0:T(8,128)(2,1)S(1)} %get-tuple-element.41), channel_id=1, replica_groups=mesh['zl'=2,'x'=4,'c'=2,'zh'=4,'y'=4] {'zl','x','y'}, dimensions={0} | all-to-all | bytes 3670016 | tf_op jit(solution)/shard_map/all_to_all | solution.py:381
  44.1 0.0 copy-done.2
  44.1 4.6 %forward.1 = (f32[256,384]{1,0:T(8,128)S(1)}, f32[256,384]{1,0:T(8,128)S(1)}, bf16[256,384]{1,0:T(8,128)(2,1)S(1)}, bf16[256,384]{1,0:T(8,128)(2,1)}, bf16[256,3...) custom-call(bf16[256,3584]{1,0:T(8,128)(2,1)S(1)} %bitcast.6, bf16[3584,384]{1,0:T(8,128)(2,1)S(1)} %copy-done.2, ...), custom_call_target="tpu_custom_call" | custom-call | flops 2818572288 | bytes 16000000 | tf_op jit(solution)/shard_map/forward/pallas_call | solution.py:158
  48.7 20.5 %all_to_all.36.parts = bf16[32,8,3584]{2,1,0:T(8,128)(2,1)S(1)} all-to-all(bf16[32,8,3584]{2,1,0:T(8,128)(2,1)S(1)} %bitcast.7), channel_id=1, replica_groups=mesh['zl'=2,'x'=4,'c'=2,'zh'=4,'y'=4] {'zl','x','y'}, dimensions={0} | all-to-all | bytes 3670016 | tf_op jit(solution)/shard_map/all_to_all | solution.py:387
  69.2 0.2 reduce.3
  69.5 15.9 %all_to_all.37.parts = bf16[4,8,3584]{2,1,0:T(8,128)(2,1)S(1)} all-to-all(bf16[4,8,3584]{2,1,0:T(8,128)(2,1)S(1)} %reduce.3), channel_id=1, replica_groups=mesh['zl'=2,'x'=4,'c'=2,'zh'=4,'y'=4] {'zh'}, dimensions={0} | all-to-all | bytes 458752 | tf_op jit(solution)/shard_map/all_to_all | solution.py:391
  85.3 0.1 error.1
  85.5 20.5 %all_to_all.38 = bf16[32,8,3584]{2,1,0:T(8,128)(2,1)S(1)} all-to-all(bf16[32,8,3584]{2,1,0:T(8,128)(2,1)S(1)} %get-tuple-element.48), channel_id=1, replica_groups=mesh['zl'=2,'x'=4,'c'=2,'zh'=4,'y'=4] {'zl','x','y'}, dimensions={0} | all-to-all | bytes 3670016 | tf_op jit(solution)/shard_map/all_to_all | solution.py:397
  106.0 3.6 %backward.1 = (f32[1,384]{1,0:T(1,128)S(1)}, f32[1,384]{1,0:T(1,128)S(1)}, f32[28,128]{1,0:T(8,128)S(1)}, bf16[256,4352]{1,0:T(8,128)(2,1)}) custom-call(bf16[256,3584]{1,0:T(8,128)(2,1)S(1)} %bitcast.5, bf16[384,3584]{1,0:T(8,128)(2,1)S(1)} %copy-done.1, bf16[384,3584]{1,0:T(8,128)(2,1)S(1)} %get-tuple-element.43.dec1, bf16[3584,384]{1,0:T(8,128)(2,1)S(1)} %copy-done.2, ...), custom_call_target="tpu_custom_call" | custom-call | flops 2113929216 | bytes 15000000 | tf_op jit(solution)/shard_map/backward/pallas_call | solution.py:218
  109.6 12.3 %collective-permute-start.4 = (f32[28,128]{1,0:T(8,128)S(1)}, f32[28,128]{1,0:T(8,128)S(1)}, u32[]{:S(2)}, u32[]{:S(2)}) collective-permute-start(f32[28,128]{1,0:T(8,128)S(1)} %get-tuple-element.54), channel_id=1, source_target_pairs={{0,16},{16,0},{1,17},{17,1},{2,18},{18,2},{3,19},{19,3},{4,20},{20... | collective-permute-start | bytes 43016 | tf_op jit(solution)/shard_map/ppermute | solution.py:36
  121.9 0.8 collective-permute-done.4
  122.7 0.3 collective-permute-start.6
  123.1 0.2 collective-permute-start.7
  123.2 0.3 collective-permute-start.5
  123.6 0.7 broadcast_in_dim.7
  124.3 3.4 %all-to-all-start.5 = ((f32[8,28,128]{2,1,0:T(8,128)}), f32[8,28,128]{2,1,0:T(8,128)S(1)}, u32[]{:S(2)}, u32[]{:S(2)}) async-start(f32[8,28,128]{2,1,0:T(8,128)} %broadcast_in_dim.7), calls=%async_computation.5 | async-start | bytes 262144 | tf_op jit(solution)/shard_map/all_to_all | solution.py:30
  127.6 0.3 collective-permute-start.8
  127.9 0.0 collective-permute-done.5.codes1
  127.9 0.0 collective-permute-done.6.error1
  127.9 5.0 %decode_grad.1 = bf16[384,3584]{1,0:T(8,128)(2,1)} custom-call(bf16[256,384]{1,0:T(8,128)(2,1)S(1)} %get-tuple-element.61.codes0, bf16[256,384]{1,0:T(8,128)(2,1)S(1)} %collective-permute-done.5.codes1, bf16[256,4352]{1,0:T(8,128)(2,1)} %get-tuple-element.63.error0, bf16[256,4352]{1,0:T(8,128)(2,1)} %collective-permute-done.6.error1, ...), custom_call_target="tpu_custom_call" | custom-call | flops 1409286144 | bytes 10000000 | tf_op jit(solution)/shard_map/decode_grad/pallas_call | solution.py:276
  132.9 1.7 %all-to-all-done.5 = f32[8,28,128]{2,1,0:T(8,128)S(1)} async-done(((f32[8,28,128]{2,1,0:T(8,128)}), f32[8,28,128]{2,1,0:T(8,128)S(1)}, u32[]{:S(2)}, u32[]{:S(2)}) %all-to-all-start.5) | async-done | bytes 114720 | tf_op jit(solution)/shard_map/all_to_all | solution.py:30
  134.6 0.0 collective-permute-done.7.rows1
  134.6 0.7 broadcast_in_dim.8
  135.4 3.7 %all-to-all-start.6 = ((f32[16,28,128]{2,1,0:T(8,128)}), f32[16,28,128]{2,1,0:T(8,128)S(1)}, u32[]{:S(2)}, u32[]{:S(2)}) async-start(f32[16,28,128]{2,1,0:T(8,128)} %broadcast_in_dim.8), calls=%async_computation.6 | async-start | bytes 524288 | tf_op jit(solution)/shard_map/all_to_all | solution.py:30
  139.0 0.0 collective-permute-done.8
  139.1 0.6 add_reduce_fusion
  139.7 5.6 %encode_grad.1 = bf16[3584,384]{1,0:T(8,128)(2,1)} custom-call(bf16[256,3584]{1,0:T(8,128)(2,1)} %get-tuple-element.59.rows0, bf16[256,3584]{1,0:T(8,128)(2,1)} %collective-permute-done.7.rows1, bf16[256,4352]{1,0:T(8,128)(2,1)} %get-tuple-element.63.error0, bf16[256,4352]{1,0:T(8,128)(2,1)} %collective-permute-done.6.error1), custom_call_target="tpu_custom_call" | custom-call | flops 1409286144 | bytes 7000000 | tf_op jit(solution)/shard_map/encode_grad/pallas_call | solution.py:338
  145.3 1.1 all-to-all-done.6
  146.4 0.6 negate_bitcast_fusion
  (12 shorter events, 0.1 us)
Async XLA Ops:
  0.6 3.5 %copy-start = (bf16[32,3584]{1,0:T(8,128)(2,1)S(1)}, bf16[32,3584]{1,0:T(8,128)(2,1)}, u32[]{:S(2)}) copy-start(bf16[32,3584]{1,0:T(8,128)(2,1)} %param.5) | copy-start | bytes 688132
  0.6 14.1 %copy-start.4 = (f32[384]{0:T(512)S(1)}, f32[384]{0:T(512)}, u32[]{:S(2)}) copy-start(f32[384]{0:T(512)} %param.7) | copy-start | bytes 4612
  0.7 14.2 %copy-start.3 = (f32[3584]{0:T(1024)S(1)}, f32[3584]{0:T(1024)}, u32[]{:S(2)}) copy-start(f32[3584]{0:T(1024)} %param.9) | copy-start | bytes 43012
  0.7 17.6 %collective-permute-start.2 = (bf16[3584,384]{1,0:T(8,128)(2,1)}, bf16[3584,384]{1,0:T(8,128)(2,1)S(1)}, u32[]{:S(2)}, u32[]{:S(2)}) collective-permute-start(bf16[3584,384]{1,0:T(8,128)(2,1)} %enc0.3), channel_id=1, source_target_pairs={{0,16},{16,0},{1,17},{17,1},{2,18},{18,2},{3,19},{19,3},{4,20},{20... | collective-permute-start | bytes 8257544 | tf_op jit(solution)/shard_map/ppermute | solution.py:36
  4.0 14.3 %collective-permute-start.3 = (bf16[384,3584]{1,0:T(8,128)(2,1)}, bf16[384,3584]{1,0:T(8,128)(2,1)}, u32[]{:S(2)}, u32[]{:S(2)}) collective-permute-start(bf16[384,3584]{1,0:T(8,128)(2,1)} %dec.1), channel_id=1, source_target_pairs={{0,16},{16,0},{1,17},{17,1},{2,18},{18,2},{3,19},{19,3},{4,20},{20... | collective-permute-start | bytes 8257544 | tf_op jit(solution)/shard_map/ppermute | solution.py:36
  4.8 13.5 %all-to-all-start = ((bf16[4,2,3584]{2,1,0:T(2,128)(2,1)}), bf16[4,2,3584]{2,1,0:T(2,128)(2,1)S(1)}, u32[]{:S(2)}, u32[]{:S(2)}) async-start(bf16[4,2,3584]{2,1,0:T(2,128)(2,1)} %broadcast_in_dim.6), calls=%async_computation | async-start | bytes 114688 | tf_op jit(solution)/shard_map/all_to_all | solution.py:30
  13.7 1.9 %collective-permute-start = (f32[1,384]{1,0:T(1,128)S(1)}, f32[1,384]{1,0:T(1,128)S(1)}, u32[]{:S(2)}, u32[]{:S(2)}) collective-permute-start(f32[1,384]{1,0:T(1,128)S(1)} %broadcast_multiply_fusion.slope0), channel_id=1, source_target_pairs={{0,16},{16,0},{1,17},{17,1},{2,18},{18,2},{3,19},{19,3},{4,20},{20... | collective-permute-start | bytes 4616 | tf_op jit(solution)/shard_map/ppermute | solution.py:36
  14.7 1.2 collective-permute-start.1
  18.3 25.9 %copy-start.2 = (bf16[3584,384]{1,0:T(8,128)(2,1)S(1)}, bf16[3584,384]{1,0:T(8,128)(2,1)}, u32[]{:S(2)}) copy-start(bf16[3584,384]{1,0:T(8,128)(2,1)} %enc0.3) | copy-start | bytes 8257540
  20.7 23.4 %copy-start.1 = (bf16[384,3584]{1,0:T(8,128)(2,1)S(1)}, bf16[384,3584]{1,0:T(8,128)(2,1)}, u32[]{:S(2)}) copy-start(bf16[384,3584]{1,0:T(8,128)(2,1)} %dec.1) | copy-start | bytes 8257540
  109.6 13.2 %collective-permute-start.4 = (f32[28,128]{1,0:T(8,128)S(1)}, f32[28,128]{1,0:T(8,128)S(1)}, u32[]{:S(2)}, u32[]{:S(2)}) collective-permute-start(f32[28,128]{1,0:T(8,128)S(1)} %get-tuple-element.54), channel_id=1, source_target_pairs={{0,16},{16,0},{1,17},{17,1},{2,18},{18,2},{3,19},{19,3},{4,20},{20... | collective-permute-start | bytes 43016 | tf_op jit(solution)/shard_map/ppermute | solution.py:36
  122.7 5.2 %collective-permute-start.6 = (bf16[256,4352]{1,0:T(8,128)(2,1)}, bf16[256,4352]{1,0:T(8,128)(2,1)}, u32[]{:S(2)}, u32[]{:S(2)}) collective-permute-start(bf16[256,4352]{1,0:T(8,128)(2,1)} %get-tuple-element.63.error0), channel_id=1, source_target_pairs={{0,16},{16,0},{1,17},{17,1},{2,18},{18,2},{3,19},{19,3},{4,20},{20... | collective-permute-start | bytes 6684680 | tf_op jit(solution)/shard_map/ppermute | solution.py:36
  123.1 11.5 %collective-permute-start.7 = (bf16[256,3584]{1,0:T(8,128)(2,1)}, bf16[256,3584]{1,0:T(8,128)(2,1)}, u32[]{:S(2)}, u32[]{:S(2)}) collective-permute-start(bf16[256,3584]{1,0:T(8,128)(2,1)} %get-tuple-element.59.rows0), channel_id=1, source_target_pairs={{0,16},{16,0},{1,17},{17,1},{2,18},{18,2},{3,19},{19,3},{4,20},{20... | collective-permute-start | bytes 5505032 | tf_op jit(solution)/shard_map/ppermute | solution.py:36
  123.2 4.6 %collective-permute-start.5 = (bf16[256,384]{1,0:T(8,128)(2,1)}, bf16[256,384]{1,0:T(8,128)(2,1)S(1)}, u32[]{:S(2)}, u32[]{:S(2)}) collective-permute-start(bf16[256,384]{1,0:T(8,128)(2,1)} %get-tuple-element.62), channel_id=1, source_target_pairs={{0,16},{16,0},{1,17},{17,1},{2,18},{18,2},{3,19},{19,3},{4,20},{20... | collective-permute-start | bytes 589832 | tf_op jit(solution)/shard_map/ppermute | solution.py:36
  124.3 10.4 %all-to-all-start.5 = ((f32[8,28,128]{2,1,0:T(8,128)}), f32[8,28,128]{2,1,0:T(8,128)S(1)}, u32[]{:S(2)}, u32[]{:S(2)}) async-start(f32[8,28,128]{2,1,0:T(8,128)} %broadcast_in_dim.7), calls=%async_computation.5 | async-start | bytes 262144 | tf_op jit(solution)/shard_map/all_to_all | solution.py:30
  127.6 11.4 %collective-permute-start.8 = (f32[1,384]{1,0:T(1,128)S(1)}, f32[1,384]{1,0:T(1,128)S(1)}, u32[]{:S(2)}, u32[]{:S(2)}) collective-permute-start(f32[1,384]{1,0:T(1,128)S(1)} %get-tuple-element.67), channel_id=1, source_target_pairs={{0,16},{16,0},{1,17},{17,1},{2,18},{18,2},{3,19},{19,3},{4,20},{20... | collective-permute-start | bytes 4616 | tf_op jit(solution)/shard_map/ppermute | solution.py:36
  135.4 11.0 %all-to-all-start.6 = ((f32[16,28,128]{2,1,0:T(8,128)}), f32[16,28,128]{2,1,0:T(8,128)S(1)}, u32[]{:S(2)}, u32[]{:S(2)}) async-start(f32[16,28,128]{2,1,0:T(8,128)} %broadcast_in_dim.8), calls=%async_computation.6 | async-start | bytes 524288 | tf_op jit(solution)/shard_map/all_to_all | solution.py:30

commit v10 on v9

--- a/solution.py
+++ b/solution.py
@@ -121,6 +121,17 @@
     row = (2.0 * factor / parts.shape[0]) * jnp.sum(error.astype(f32), axis=0, keepdims=True)
     for k in range(block_sum.shape[0]):
         block_sum[k : k + 1, :] = row[:, 128 * k : 128 * (k + 1)]
+
+
+def add_kernel(mine, theirs, out):
+    repeat_into(out, mine[...] + theirs[...])
+
+
+def minus_sum_kernel(parts, out):
+    total = parts[0]
+    for k in range(1, parts.shape[0]):
+        total += parts[k]
+    repeat_into(out, -total)
 
 
 def forward_kernel(
@@ -399,19 +410,27 @@
         error, (w_decode, dec1), (w_encode, enc1), (active0, active1), (slope0, slope1),
         block_sum, factor,
     )
-    through = through + swap(through)
+    lines = through.shape
+    through = small_kernel(
+        add_kernel, jax.ShapeDtypeStruct((NZ,) + lines, f32), through, swap(through), name="add"
+    )
     through, centered, error, codes1, sums1 = tie(through, centered, error, codes1, sums1)
     their_codes = swap(codes1)
     their_error, their_rows = swap(error), swap(centered)
-    through = spread(through, Z, NZ)
+    through = lax.all_to_all(through, Z, 0, 0, tiled=True)
+    grad_b_encode = (sums0 + swap(sums1)).reshape(-1)
     grad_decode = decode_grad(
         (codes0, their_codes), (error, their_error), w_decode, norms, factor
     )
-    through, grad_decode, their_rows = tie(through, grad_decode, their_rows)
-    through = jnp.sum(spread(jnp.sum(through, axis=0), XY, NXY), axis=0).reshape(width)
+    through, grad_decode, their_rows, grad_b_encode = tie(
+        through, grad_decode, their_rows, grad_b_encode
+    )
+    through = small_kernel(
+        minus_sum_kernel, jax.ShapeDtypeStruct((NXY,) + lines, f32), through, name="minus_sum"
+    )
+    grad_b_decode = jnp.sum(lax.all_to_all(through, XY, 0, 0, tiled=True), axis=0)
     grad_encode = encode_grad((centered, their_rows), (error, their_error))
-    grad_b_encode = (sums0 + swap(sums1)).reshape(-1)
-    return (grad_encode, grad_b_encode, grad_decode, -through)
+    return (grad_encode, grad_b_encode, grad_decode, grad_b_decode.reshape(width))
 
 
 def solution(mesh):

time: 149 us -> 149 us (level)
    all_to_all x0 -> x2, starting transfers between devices: none -> 7.03 us  [the longest x1 3.66 us: per_device(): lax.all_to_all(through, XY, 0, 0, tiled=True)]
    all_to_all x3 -> x1, starting transfers between devices: 13.5 us -> 6.48 us  [spread(): lax.all_to_all(jnp.broadcast_to(block[None], (n,) + block.shape), axes, 0...]
    all_to_all x0 -> x2, waiting for transfers between devices: none -> 3.01 us  [the longest x1 1.68 us: per_device(): lax.all_to_all(through, XY, 0, 0, tiled=True)]
    all_to_all x3 -> x1, waiting for transfers between devices: 5.16 us -> 2.38 us  [spread(): lax.all_to_all(jnp.broadcast_to(block[None], (n,) + block.shape), axes, 0...]
  transfers between devices with their start and end apart: 12 -> 12, of which waited for: 6 -> 7; matrix products, arithmetic and copies ran while one was open for 3% -> 3% of each run, Pallas kernels for 7% -> 7%
where the time goes in v10:
time: 149 us; the launch traced here: 147 us
  blocking collectives  80.2 us (54%)
  starting transfers between devices  31.4 us (21%)
  Pallas kernels  23 us (15%)
  waiting for transfers between devices  7.37 us (5%)
  other arithmetic  3.64 us (2%)
    all_to_all x1, blocking collectives, per_device(): lax.all_to_all(centered, WIDE, 0, 0, tiled=True).reshape(half, width)  23.4 us
    all_to_all x1, blocking collectives, per_device(): part = lax.all_to_all(part, WIDE, 0, 0, tiled=True)  20.5 us
    all_to_all x1, blocking collectives, per_device(): error = lax.all_to_all(error, WIDE, 0, 0, tiled=True).reshape(half, width)  20.5 us
    ppermute x9, starting transfers between devices, swap(): return lax.ppermute(block, 'c', [(0, 1), (1, 0)])  17.9 us
    all_to_all x1, blocking collectives, per_device(): part = lax.all_to_all(part, ZH, 0, 0, tiled=True)  15.9 us
    all_to_all x1, starting transfers between devices, spread(): lax.all_to_all(jnp.broadcast_to(block[None], (n,) + block.shape), axes, 0...  6.48 us
    pallas_call x1, Pallas kernels, encode_grad(): pl.pallas_call(encode_grad_kernel, out_shape=jax.ShapeDtypeStruct((width,...  5.63 us
    pallas_call x1, Pallas kernels, decode_grad(): pl.pallas_call(functools.partial(decode_grad_kernel, factor), out_shape=j...  4.99 us
  transfers between devices with their start and end apart: 12, of which 7 were waited for; matrix products, arithmetic and copies ran while one was open for 3% of the time, Pallas kernels for 7%

profile of v10, /device:TPU:1, one launch (start us, length us, event | category | flops | bytes accessed | tf_op | source)
XLA Modules:
  0.0 147.2 jit_solution(8490237792395277240)
XLA Ops:
  0.6 0.0 copy-start
  0.6 0.0 copy-start.4
  0.7 0.0 copy-start.3
  0.7 3.3 %collective-permute-start.2 = (bf16[3584,384]{1,0:T(8,128)(2,1)}, bf16[3584,384]{1,0:T(8,128)(2,1)S(1)}, u32[]{:S(2)}, u32[]{:S(2)}) collective-permute-start(bf16[3584,384]{1,0:T(8,128)(2,1)} %enc0.3), channel_id=1, source_target_pairs={{0,16},{16,0},{1,17},{17,1},{2,18},{18,2},{3,19},{19,3},{4,20},{20... | collective-permute-start | bytes 8257544 | tf_op jit(solution)/shard_map/ppermute | solution.py:36
  4.0 0.1 collective-permute-start.3
  4.1 0.0 copy-done
  4.1 0.7 broadcast_in_dim.2
  4.8 6.5 %all-to-all-start = ((bf16[4,2,3584]{2,1,0:T(2,128)(2,1)}), bf16[4,2,3584]{2,1,0:T(2,128)(2,1)S(1)}, u32[]{:S(2)}, u32[]{:S(2)}) async-start(bf16[4,2,3584]{2,1,0:T(2,128)(2,1)} %broadcast_in_dim.2), calls=%async_computation | async-start | bytes 114688 | tf_op jit(solution)/shard_map/all_to_all | solution.py:30
  11.3 2.4 %multiply_reduce_fusion = f32[384]{0:T(512)S(1)} fusion(bf16[384,3584]{1,0:T(8,128)(2,1)} %dec.1), kind=kLoop, calls=%fused_computation | loop fusion | flops 4128384 | bytes 2754048 | tf_op jit(solution)/shard_map/reduce_sum | solution.py:382
  13.7 1.0 collective-permute-start
  14.7 0.1 collective-permute-start.1
  14.8 0.0 copy-done.3
  14.9 0.7 collective-permute-done.slope1
  15.5 0.3 collective-permute-done.1.bias1
  15.9 2.4 %all-to-all-done.pieces = bf16[4,2,3584]{2,1,0:T(2,128)(2,1)S(1)} async-done(((bf16[4,2,3584]{2,1,0:T(2,128)(2,1)}), bf16[4,2,3584]{2,1,0:T(2,128)(2,1)S(1)}, u32[]{:S(2)}, u32[]{:S(2)}) %all-to-all-start) | async-done | bytes 57376 | tf_op jit(solution)/shard_map/all_to_all | solution.py:30
  18.3 0.0 collective-permute-done.2.enc_hbm
  18.3 0.0 collective-permute-done.3.dec_hbm
  18.3 2.5 %collect.1 = (bf16[8,3584]{1,0:T(8,128)(2,1)S(1)}, bf16[32,8,3584]{2,1,0:T(8,128)(2,1)S(1)}, bf16[3584,384]{1,0:T(8,128)(2,1)S(1)}, bf16[384,3584]{1,0:T(8,128)(2,1)S(1)}) custom-call(bf16[4,2,3584]{2,1,0:T(2,128)(2,1)S(1)} %all-to-all-done.pieces, f32[1,3584]{1,0:T(1,128)S(1)} %reshape.52.bias, bf16[3584,384]{1,0:T(8,128)(2,1)S(1)} %collective-permute-done.2.enc_hbm, ...), custom_call_target="tpu_custom_call" | custom-call | tf_op jit(solution)/shard_map/collect/pallas_call | solution.py:92
  20.7 0.0 copy-start.1
  20.8 23.4 %all_to_all.35 = bf16[32,8,3584]{2,1,0:T(8,128)(2,1)S(1)} all-to-all(bf16[32,8,3584]{2,1,0:T(8,128)(2,1)S(1)} %get-tuple-element.42), channel_id=1, replica_groups=mesh['zl'=2,'x'=4,'c'=2,'zh'=4,'y'=4] {'zl','x','y'}, dimensions={0} | all-to-all | bytes 3670016 | tf_op jit(solution)/shard_map/all_to_all | solution.py:392
  44.1 0.0 copy-done.2
  44.1 4.5 %forward.1 = (f32[256,384]{1,0:T(8,128)S(1)}, f32[256,384]{1,0:T(8,128)S(1)}, bf16[256,384]{1,0:T(8,128)(2,1)S(1)}, bf16[256,384]{1,0:T(8,128)(2,1)}, bf16[256,3...) custom-call(bf16[256,3584]{1,0:T(8,128)(2,1)S(1)} %bitcast.5, bf16[3584,384]{1,0:T(8,128)(2,1)S(1)} %copy-done.2, ...), custom_call_target="tpu_custom_call" | custom-call | flops 2818572288 | bytes 16000000 | tf_op jit(solution)/shard_map/forward/pallas_call | solution.py:169
  48.7 20.5 %all_to_all.36.parts = bf16[32,8,3584]{2,1,0:T(8,128)(2,1)S(1)} all-to-all(bf16[32,8,3584]{2,1,0:T(8,128)(2,1)S(1)} %bitcast.6), channel_id=1, replica_groups=mesh['zl'=2,'x'=4,'c'=2,'zh'=4,'y'=4] {'zl','x','y'}, dimensions={0} | all-to-all | bytes 3670016 | tf_op jit(solution)/shard_map/all_to_all | solution.py:398
  69.2 0.2 reduce.3
  69.4 15.9 %all_to_all.37.parts = bf16[4,8,3584]{2,1,0:T(8,128)(2,1)S(1)} all-to-all(bf16[4,8,3584]{2,1,0:T(8,128)(2,1)S(1)} %reduce.3), channel_id=1, replica_groups=mesh['zl'=2,'x'=4,'c'=2,'zh'=4,'y'=4] {'zh'}, dimensions={0} | all-to-all | bytes 458752 | tf_op jit(solution)/shard_map/all_to_all | solution.py:402
  85.3 0.1 error.1
  85.4 20.5 %all_to_all.38 = bf16[32,8,3584]{2,1,0:T(8,128)(2,1)S(1)} all-to-all(bf16[32,8,3584]{2,1,0:T(8,128)(2,1)S(1)} %get-tuple-element.49), channel_id=1, replica_groups=mesh['zl'=2,'x'=4,'c'=2,'zh'=4,'y'=4] {'zl','x','y'}, dimensions={0} | all-to-all | bytes 3670016 | tf_op jit(solution)/shard_map/all_to_all | solution.py:408
  105.9 3.6 %backward.1 = (f32[1,384]{1,0:T(1,128)S(1)}, f32[1,384]{1,0:T(1,128)S(1)}, f32[28,128]{1,0:T(8,128)S(1)}, bf16[256,4352]{1,0:T(8,128)(2,1)}) custom-call(bf16[256,3584]{1,0:T(8,128)(2,1)S(1)} %bitcast.4, bf16[384,3584]{1,0:T(8,128)(2,1)S(1)} %copy-done.1, bf16[384,3584]{1,0:T(8,128)(2,1)S(1)} %get-tuple-element.44.dec1, bf16[3584,384]{1,0:T(8,128)(2,1)S(1)} %copy-done.2, ...), custom_call_target="tpu_custom_call" | custom-call | flops 2113929216 | bytes 15000000 | tf_op jit(solution)/shard_map/backward/pallas_call | solution.py:229
  109.5 12.3 %collective-permute-start.4 = (f32[28,128]{1,0:T(8,128)S(1)}, f32[28,128]{1,0:T(8,128)S(1)}, u32[]{:S(2)}, u32[]{:S(2)}) collective-permute-start(f32[28,128]{1,0:T(8,128)S(1)} %get-tuple-element.55.mine), channel_id=1, source_target_pairs={{0,16},{16,0},{1,17},{17,1},{2,18},{18,2},{3,19},{19,3},{4,20},{20... | collective-permute-start | bytes 43016 | tf_op jit(solution)/shard_map/ppermute | solution.py:36
  121.8 0.8 collective-permute-done.4.theirs
  122.7 0.7 add.41
  123.3 0.3 collective-permute-start.6
  123.7 0.2 collective-permute-start.7
  123.9 0.3 collective-permute-start.5
  124.2 0.2 collective-permute-start.8
  124.4 3.4 %all-to-all-start.5 = ((f32[8,28,128]{2,1,0:T(8,128)}), f32[8,28,128]{2,1,0:T(8,128)S(1)}, u32[]{:S(2)}, u32[]{:S(2)}) async-start(f32[8,28,128]{2,1,0:T(8,128)} %add.41), calls=%async_computation.5 | async-start | bytes 262144 | tf_op jit(solution)/shard_map/all_to_all | solution.py:420
  127.7 0.0 collective-permute-done.8
  127.8 0.6 add_reduce_fusion
  128.4 0.1 collective-permute-done.5.codes1
  128.5 0.0 collective-permute-done.6.error1
  128.5 5.0 %decode_grad.1 = bf16[384,3584]{1,0:T(8,128)(2,1)} custom-call(bf16[256,384]{1,0:T(8,128)(2,1)S(1)} %get-tuple-element.62.codes0, bf16[256,384]{1,0:T(8,128)(2,1)S(1)} %collective-permute-done.5.codes1, bf16[256,4352]{1,0:T(8,128)(2,1)} %get-tuple-element.64.error0, bf16[256,4352]{1,0:T(8,128)(2,1)} %collective-permute-done.6.error1, ...), custom_call_target="tpu_custom_call" | custom-call | flops 1409286144 | bytes 10000000 | tf_op jit(solution)/shard_map/decode_grad/pallas_call | solution.py:287
  133.5 1.3 all-to-all-done.5.parts
  134.8 0.0 collective-permute-done.7.rows1
  134.8 0.7 minus_sum.1
  135.5 3.7 %all-to-all-start.6 = ((f32[16,28,128]{2,1,0:T(8,128)}), f32[16,28,128]{2,1,0:T(8,128)S(1)}, u32[]{:S(2)}, u32[]{:S(2)}) async-start(f32[16,28,128]{2,1,0:T(8,128)} %minus_sum.1), calls=%async_computation.6 | async-start | bytes 524288 | tf_op jit(solution)/shard_map/all_to_all | solution.py:431
  139.2 5.6 %encode_grad.1 = bf16[3584,384]{1,0:T(8,128)(2,1)} custom-call(bf16[256,3584]{1,0:T(8,128)(2,1)} %get-tuple-element.60.rows0, bf16[256,3584]{1,0:T(8,128)(2,1)} %collective-permute-done.7.rows1, bf16[256,4352]{1,0:T(8,128)(2,1)} %get-tuple-element.64.error0, bf16[256,4352]{1,0:T(8,128)(2,1)} %collective-permute-done.6.error1), custom_call_target="tpu_custom_call" | custom-call | flops 1409286144 | bytes 7000000 | tf_op jit(solution)/shard_map/encode_grad/pallas_call | solution.py:349
  144.9 1.7 %all-to-all-done.6 = f32[16,28,128]{2,1,0:T(8,128)S(1)} async-done(((f32[16,28,128]{2,1,0:T(8,128)}), f32[16,28,128]{2,1,0:T(8,128)S(1)}, u32[]{:S(2)}, u32[]{:S(2)}) %all-to-all-start.6) | async-done | bytes 229408 | tf_op jit(solution)/shard_map/all_to_all | solution.py:431
  146.5 0.6 reduce_sum.19
  (9 shorter events, 0.1 us)
Async XLA Ops:
  0.6 3.5 %copy-start = (bf16[32,3584]{1,0:T(8,128)(2,1)S(1)}, bf16[32,3584]{1,0:T(8,128)(2,1)}, u32[]{:S(2)}) copy-start(bf16[32,3584]{1,0:T(8,128)(2,1)} %param.5) | copy-start | bytes 688132
  0.6 14.1 %copy-start.4 = (f32[384]{0:T(512)S(1)}, f32[384]{0:T(512)}, u32[]{:S(2)}) copy-start(f32[384]{0:T(512)} %param.7) | copy-start | bytes 4612
  0.7 14.2 %copy-start.3 = (f32[3584]{0:T(1024)S(1)}, f32[3584]{0:T(1024)}, u32[]{:S(2)}) copy-start(f32[3584]{0:T(1024)} %param.9) | copy-start | bytes 43012
  0.7 17.6 %collective-permute-start.2 = (bf16[3584,384]{1,0:T(8,128)(2,1)}, bf16[3584,384]{1,0:T(8,128)(2,1)S(1)}, u32[]{:S(2)}, u32[]{:S(2)}) collective-permute-start(bf16[3584,384]{1,0:T(8,128)(2,1)} %enc0.3), channel_id=1, source_target_pairs={{0,16},{16,0},{1,17},{17,1},{2,18},{18,2},{3,19},{19,3},{4,20},{20... | collective-permute-start | bytes 8257544 | tf_op jit(solution)/shard_map/ppermute | solution.py:36
  4.0 14.3 %collective-permute-start.3 = (bf16[384,3584]{1,0:T(8,128)(2,1)}, bf16[384,3584]{1,0:T(8,128)(2,1)}, u32[]{:S(2)}, u32[]{:S(2)}) collective-permute-start(bf16[384,3584]{1,0:T(8,128)(2,1)} %dec.1), channel_id=1, source_target_pairs={{0,16},{16,0},{1,17},{17,1},{2,18},{18,2},{3,19},{19,3},{4,20},{20... | collective-permute-start | bytes 8257544 | tf_op jit(solution)/shard_map/ppermute | solution.py:36
  4.8 13.5 %all-to-all-start = ((bf16[4,2,3584]{2,1,0:T(2,128)(2,1)}), bf16[4,2,3584]{2,1,0:T(2,128)(2,1)S(1)}, u32[]{:S(2)}, u32[]{:S(2)}) async-start(bf16[4,2,3584]{2,1,0:T(2,128)(2,1)} %broadcast_in_dim.2), calls=%async_computation | async-start | bytes 114688 | tf_op jit(solution)/shard_map/all_to_all | solution.py:30
  13.7 1.9 %collective-permute-start = (f32[1,384]{1,0:T(1,128)S(1)}, f32[1,384]{1,0:T(1,128)S(1)}, u32[]{:S(2)}, u32[]{:S(2)}) collective-permute-start(f32[1,384]{1,0:T(1,128)S(1)} %broadcast_multiply_fusion.slope0), channel_id=1, source_target_pairs={{0,16},{16,0},{1,17},{17,1},{2,18},{18,2},{3,19},{19,3},{4,20},{20... | collective-permute-start | bytes 4616 | tf_op jit(solution)/shard_map/ppermute | solution.py:36
  14.7 1.2 collective-permute-start.1
  18.3 25.9 %copy-start.2 = (bf16[3584,384]{1,0:T(8,128)(2,1)S(1)}, bf16[3584,384]{1,0:T(8,128)(2,1)}, u32[]{:S(2)}) copy-start(bf16[3584,384]{1,0:T(8,128)(2,1)} %enc0.3) | copy-start | bytes 8257540
  20.7 23.4 %copy-start.1 = (bf16[384,3584]{1,0:T(8,128)(2,1)S(1)}, bf16[384,3584]{1,0:T(8,128)(2,1)}, u32[]{:S(2)}) copy-start(bf16[384,3584]{1,0:T(8,128)(2,1)} %dec.1) | copy-start | bytes 8257540
  109.5 13.2 %collective-permute-start.4 = (f32[28,128]{1,0:T(8,128)S(1)}, f32[28,128]{1,0:T(8,128)S(1)}, u32[]{:S(2)}, u32[]{:S(2)}) collective-permute-start(f32[28,128]{1,0:T(8,128)S(1)} %get-tuple-element.55.mine), channel_id=1, source_target_pairs={{0,16},{16,0},{1,17},{17,1},{2,18},{18,2},{3,19},{19,3},{4,20},{20... | collective-permute-start | bytes 43016 | tf_op jit(solution)/shard_map/ppermute | solution.py:36
  123.3 5.1 %collective-permute-start.6 = (bf16[256,4352]{1,0:T(8,128)(2,1)}, bf16[256,4352]{1,0:T(8,128)(2,1)}, u32[]{:S(2)}, u32[]{:S(2)}) collective-permute-start(bf16[256,4352]{1,0:T(8,128)(2,1)} %get-tuple-element.64.error0), channel_id=1, source_target_pairs={{0,16},{16,0},{1,17},{17,1},{2,18},{18,2},{3,19},{19,3},{4,20},{20... | collective-permute-start | bytes 6684680 | tf_op jit(solution)/shard_map/ppermute | solution.py:36
  123.7 11.1 %collective-permute-start.7 = (bf16[256,3584]{1,0:T(8,128)(2,1)}, bf16[256,3584]{1,0:T(8,128)(2,1)}, u32[]{:S(2)}, u32[]{:S(2)}) collective-permute-start(bf16[256,3584]{1,0:T(8,128)(2,1)} %get-tuple-element.60.rows0), channel_id=1, source_target_pairs={{0,16},{16,0},{1,17},{17,1},{2,18},{18,2},{3,19},{19,3},{4,20},{20... | collective-permute-start | bytes 5505032 | tf_op jit(solution)/shard_map/ppermute | solution.py:36
  123.9 4.6 %collective-permute-start.5 = (bf16[256,384]{1,0:T(8,128)(2,1)}, bf16[256,384]{1,0:T(8,128)(2,1)S(1)}, u32[]{:S(2)}, u32[]{:S(2)}) collective-permute-start(bf16[256,384]{1,0:T(8,128)(2,1)} %get-tuple-element.63), channel_id=1, source_target_pairs={{0,16},{16,0},{1,17},{17,1},{2,18},{18,2},{3,19},{19,3},{4,20},{20... | collective-permute-start | bytes 589832 | tf_op jit(solution)/shard_map/ppermute | solution.py:36
  124.2 3.5 %collective-permute-start.8 = (f32[1,384]{1,0:T(1,128)S(1)}, f32[1,384]{1,0:T(1,128)S(1)}, u32[]{:S(2)}, u32[]{:S(2)}) collective-permute-start(f32[1,384]{1,0:T(1,128)S(1)} %get-tuple-element.67), channel_id=1, source_target_pairs={{0,16},{16,0},{1,17},{17,1},{2,18},{18,2},{3,19},{19,3},{4,20},{20... | collective-permute-start | bytes 4616 | tf_op jit(solution)/shard_map/ppermute | solution.py:36
  124.4 10.4 %all-to-all-start.5 = ((f32[8,28,128]{2,1,0:T(8,128)}), f32[8,28,128]{2,1,0:T(8,128)S(1)}, u32[]{:S(2)}, u32[]{:S(2)}) async-start(f32[8,28,128]{2,1,0:T(8,128)} %add.41), calls=%async_computation.5 | async-start | bytes 262144 | tf_op jit(solution)/shard_map/all_to_all | solution.py:420
  135.5 11.0 %all-to-all-start.6 = ((f32[16,28,128]{2,1,0:T(8,128)}), f32[16,28,128]{2,1,0:T(8,128)S(1)}, u32[]{:S(2)}, u32[]{:S(2)}) async-start(f32[16,28,128]{2,1,0:T(8,128)} %minus_sum.1), calls=%async_computation.6 | async-start | bytes 524288 | tf_op jit(solution)/shard_map/all_to_all | solution.py:431

commit v11 on v10

--- a/solution.py
+++ b/solution.py
@@ -12,7 +12,7 @@
 LMIN = ("zh", "y")
 WIDE, NWIDE = ("zl", "x", "y"), 32
 XY, NXY = ("x", "y"), 16
-Z, NZ = ("zl", "zh"), 8
+ZC, NZC = ("zl", "c", "zh"), 16
 ZH, NZH = ("zh",), 4
 f32, bf16 = jnp.float32, jnp.bfloat16
 VMEM = pl.BlockSpec(memory_space=pltpu.VMEM)
@@ -121,10 +121,6 @@
     row = (2.0 * factor / parts.shape[0]) * jnp.sum(error.astype(f32), axis=0, keepdims=True)
     for k in range(block_sum.shape[0]):
         block_sum[k : k + 1, :] = row[:, 128 * k : 128 * (k + 1)]
-
-
-def add_kernel(mine, theirs, out):
-    repeat_into(out, mine[...] + theirs[...])
 
 
 def minus_sum_kernel(parts, out):
@@ -216,8 +212,8 @@
         term = lax.dot_general(parts, enc[...], NT, preferred_element_type=f32)
         product = term if product is None else product + term
     row = product[0:1] + product[1:2] + product[2:3]
-    for k in range(through.shape[0]):
-        through[k : k + 1, :] = row[:, 128 * k : 128 * (k + 1)] - block_sum[k : k + 1, :]
+    lines = [row[:, 128 * k : 128 * (k + 1)] for k in range(through.shape[1])]
+    repeat_into(through, jnp.concatenate(lines, axis=0) - block_sum[...])
     for copy in copies:
         copy.wait()
 
@@ -229,7 +225,7 @@
     return pl.pallas_call(
         functools.partial(backward_kernel, factor),
         out_shape=(
-            line, line, jax.ShapeDtypeStruct(block_sum.shape, f32),
+            line, line, jax.ShapeDtypeStruct((NZC,) + block_sum.shape, f32),
             jax.ShapeDtypeStruct((count, width + 2 * mine), bf16),
         ),
         in_specs=[VMEM] * 10,
@@ -410,14 +406,10 @@
         error, (w_decode, dec1), (w_encode, enc1), (active0, active1), (slope0, slope1),
         block_sum, factor,
     )
-    lines = through.shape
-    through = small_kernel(
-        add_kernel, jax.ShapeDtypeStruct((NZ,) + lines, f32), through, swap(through), name="add"
-    )
     through, centered, error, codes1, sums1 = tie(through, centered, error, codes1, sums1)
     their_codes = swap(codes1)
     their_error, their_rows = swap(error), swap(centered)
-    through = lax.all_to_all(through, Z, 0, 0, tiled=True)
+    through = lax.all_to_all(through, ZC, 0, 0, tiled=True)
     grad_b_encode = (sums0 + swap(sums1)).reshape(-1)
     grad_decode = decode_grad(
         (codes0, their_codes), (error, their_error), w_decode, norms, factor
@@ -426,7 +418,7 @@
         through, grad_decode, their_rows, grad_b_encode
     )
     through = small_kernel(
-        minus_sum_kernel, jax.ShapeDtypeStruct((NXY,) + lines, f32), through, name="minus_sum"
+        minus_sum_kernel, jax.ShapeDtypeStruct((NXY,) + block_sum.shape, f32), through, name="minus_sum"
     )
     grad_b_decode = jnp.sum(lax.all_to_all(through, XY, 0, 0, tiled=True), axis=0)
     grad_encode = encode_grad((centered, their_rows), (error, their_error))

time: 149 us -> 152 us (1.020)
  waiting for transfers between devices: 7.37 us -> 11 us
    all_to_all x1, waiting for transfers between devices: 1.33 us -> 3.39 us  [per_device(): through = lax.all_to_all(through, ZC, 0, 0, tiled=True)]
    ppermute x9 -> x8, waiting for transfers between devices: 1.98 us -> 3.22 us  [swap(): return lax.ppermute(block, 'c', [(0, 1), (1, 0)])]
    ppermute x9 -> x8, starting transfers between devices: 17.9 us -> 17.8 us  [swap(): return lax.ppermute(block, 'c', [(0, 1), (1, 0)])]
  transfers between devices with their start and end apart: 12 -> 11, of which waited for: 7 -> 6; matrix products, arithmetic and copies ran while one was open for 3% -> 2% of each run, Pallas kernels for 7% -> 7%
where the time goes in v11:
time: 152 us; the launch traced here: 151 us
  blocking collectives  80.2 us (53%)
  starting transfers between devices  31.5 us (21%)
  Pallas kernels  23.5 us (15%)
  waiting for transfers between devices  11 us (7%)
  other arithmetic  3.63 us (2%)
    all_to_all x1, blocking collectives, per_device(): lax.all_to_all(centered, WIDE, 0, 0, tiled=True).reshape(half, width)  23.4 us
    all_to_all x1, blocking collectives, per_device(): part = lax.all_to_all(part, WIDE, 0, 0, tiled=True)  20.5 us
    all_to_all x1, blocking collectives, per_device(): error = lax.all_to_all(error, WIDE, 0, 0, tiled=True).reshape(half, width)  20.5 us
    ppermute x8, starting transfers between devices, swap(): return lax.ppermute(block, 'c', [(0, 1), (1, 0)])  17.8 us
    all_to_all x1, blocking collectives, per_device(): part = lax.all_to_all(part, ZH, 0, 0, tiled=True)  15.9 us
    all_to_all x1, starting transfers between devices, spread(): lax.all_to_all(jnp.broadcast_to(block[None], (n,) + block.shape), axes, 0...  6.48 us
    pallas_call x1, Pallas kernels, encode_grad(): pl.pallas_call(encode_grad_kernel, out_shape=jax.ShapeDtypeStruct((width,...  5.64 us
    pallas_call x1, Pallas kernels, decode_grad(): pl.pallas_call(functools.partial(decode_grad_kernel, factor), out_shape=j...  5 us
  transfers between devices with their start and end apart: 11, of which 6 were waited for; matrix products, arithmetic and copies ran while one was open for 2% of the time, Pallas kernels for 7%

profile of v11, /device:TPU:1, one launch (start us, length us, event | category | flops | bytes accessed | tf_op | source)
XLA Modules:
  0.0 151.3 jit_solution(15753760216650802538)
XLA Ops:
  0.6 0.0 copy-start
  0.6 0.0 copy-start.5
  0.7 0.0 copy-start.4
  0.7 3.3 %collective-permute-start.2 = (bf16[3584,384]{1,0:T(8,128)(2,1)}, bf16[3584,384]{1,0:T(8,128)(2,1)S(1)}, u32[]{:S(2)}, u32[]{:S(2)}) collective-permute-start(bf16[3584,384]{1,0:T(8,128)(2,1)} %enc0.3), channel_id=1, source_target_pairs={{0,16},{16,0},{1,17},{17,1},{2,18},{18,2},{3,19},{19,3},{4,20},{20... | collective-permute-start | bytes 8257544 | tf_op jit(solution)/shard_map/ppermute | solution.py:36
  4.0 0.1 collective-permute-start.3
  4.1 0.0 copy-done
  4.1 0.7 broadcast_in_dim.2
  4.8 6.5 %all-to-all-start = ((bf16[4,2,3584]{2,1,0:T(2,128)(2,1)}), bf16[4,2,3584]{2,1,0:T(2,128)(2,1)S(1)}, u32[]{:S(2)}, u32[]{:S(2)}) async-start(bf16[4,2,3584]{2,1,0:T(2,128)(2,1)} %broadcast_in_dim.2), calls=%async_computation | async-start | bytes 114688 | tf_op jit(solution)/shard_map/all_to_all | solution.py:30
  11.3 2.4 %multiply_reduce_fusion = f32[384]{0:T(512)S(1)} fusion(bf16[384,3584]{1,0:T(8,128)(2,1)} %dec.1), kind=kLoop, calls=%fused_computation | loop fusion | flops 4128384 | bytes 2754048 | tf_op jit(solution)/shard_map/reduce_sum | solution.py:378
  13.7 1.0 collective-permute-start
  14.7 0.0 copy-done.5
  14.7 0.1 collective-permute-start.1
  14.8 0.0 copy-done.4
  14.9 0.7 collective-permute-done.slope1
  15.5 0.3 collective-permute-done.1.bias1
  15.9 2.4 %all-to-all-done.pieces = bf16[4,2,3584]{2,1,0:T(2,128)(2,1)S(1)} async-done(((bf16[4,2,3584]{2,1,0:T(2,128)(2,1)}), bf16[4,2,3584]{2,1,0:T(2,128)(2,1)S(1)}, u32[]{:S(2)}, u32[]{:S(2)}) %all-to-all-start) | async-done | bytes 57376 | tf_op jit(solution)/shard_map/all_to_all | solution.py:30
  18.3 0.0 collective-permute-done.2.enc_hbm
  18.3 0.0 collective-permute-done.3.dec_hbm
  18.3 2.5 %collect.1 = (bf16[8,3584]{1,0:T(8,128)(2,1)S(1)}, bf16[32,8,3584]{2,1,0:T(8,128)(2,1)S(1)}, bf16[3584,384]{1,0:T(8,128)(2,1)S(1)}, bf16[384,3584]{1,0:T(8,128)(2,1)S(1)}) custom-call(bf16[4,2,3584]{2,1,0:T(2,128)(2,1)S(1)} %all-to-all-done.pieces, f32[1,3584]{1,0:T(1,128)S(1)} %reshape.52.bias, bf16[3584,384]{1,0:T(8,128)(2,1)S(1)} %collective-permute-done.2.enc_hbm, ...), custom_call_target="tpu_custom_call" | custom-call | tf_op jit(solution)/shard_map/collect/pallas_call | solution.py:92
  20.7 0.0 copy-start.1
  20.8 23.4 %all_to_all.35 = bf16[32,8,3584]{2,1,0:T(8,128)(2,1)S(1)} all-to-all(bf16[32,8,3584]{2,1,0:T(8,128)(2,1)S(1)} %get-tuple-element.42), channel_id=1, replica_groups=mesh['zl'=2,'x'=4,'c'=2,'zh'=4,'y'=4] {'zl','x','y'}, dimensions={0} | all-to-all | bytes 3670016 | tf_op jit(solution)/shard_map/all_to_all | solution.py:388
  44.1 0.0 copy-done.2
  44.1 0.0 copy-done.1
  44.1 4.9 %forward.1 = (f32[256,384]{1,0:T(8,128)S(1)}, f32[256,384]{1,0:T(8,128)S(1)}, bf16[256,384]{1,0:T(8,128)(2,1)S(1)}, bf16[256,384]{1,0:T(8,128)(2,1)S(1)}, bf16[2...) custom-call(bf16[256,3584]{1,0:T(8,128)(2,1)S(1)} %bitcast.5, bf16[3584,384]{1,0:T(8,128)(2,1)S(1)} %copy-done.2, ...), custom_call_target="tpu_custom_call" | custom-call | flops 2818572288 | bytes 16000000 | tf_op jit(solution)/shard_map/forward/pallas_call | solution.py:165
  49.1 0.0 copy-start.3
  49.1 20.5 %all_to_all.36.parts = bf16[32,8,3584]{2,1,0:T(8,128)(2,1)S(1)} all-to-all(bf16[32,8,3584]{2,1,0:T(8,128)(2,1)S(1)} %bitcast.6), channel_id=1, replica_groups=mesh['zl'=2,'x'=4,'c'=2,'zh'=4,'y'=4] {'zl','x','y'}, dimensions={0} | all-to-all | bytes 3670016 | tf_op jit(solution)/shard_map/all_to_all | solution.py:394
  69.6 0.2 reduce.3
  69.8 15.9 %all_to_all.37.parts = bf16[4,8,3584]{2,1,0:T(8,128)(2,1)S(1)} all-to-all(bf16[4,8,3584]{2,1,0:T(8,128)(2,1)S(1)} %reduce.3), channel_id=1, replica_groups=mesh['zl'=2,'x'=4,'c'=2,'zh'=4,'y'=4] {'zh'}, dimensions={0} | all-to-all | bytes 458752 | tf_op jit(solution)/shard_map/all_to_all | solution.py:398
  85.7 0.1 error.1
  85.8 20.5 %all_to_all.38 = bf16[32,8,3584]{2,1,0:T(8,128)(2,1)S(1)} all-to-all(bf16[32,8,3584]{2,1,0:T(8,128)(2,1)S(1)} %get-tuple-element.49), channel_id=1, replica_groups=mesh['zl'=2,'x'=4,'c'=2,'zh'=4,'y'=4] {'zl','x','y'}, dimensions={0} | all-to-all | bytes 3670016 | tf_op jit(solution)/shard_map/all_to_all | solution.py:404
  106.3 4.3 %backward.1 = (f32[1,384]{1,0:T(1,128)S(1)}, f32[1,384]{1,0:T(1,128)S(1)}, f32[16,28,128]{2,1,0:T(8,128)}, bf16[256,4352]{1,0:T(8,128)(2,1)}) custom-call(bf16[256,3584]{1,0:T(8,128)(2,1)S(1)} %bitcast.4, bf16[384,3584]{1,0:T(8,128)(2,1)S(1)} %copy-done.1, bf16[384,3584]{1,0:T(8,128)(2,1)S(1)} %get-tuple-element.44.dec1, bf16[3584,384]{1,0:T(8,128)(2,1)S(1)} %copy-done.2, ...), custom_call_target="tpu_custom_call" | custom-call | flops 2113929216 | bytes 15000000 | tf_op jit(solution)/shard_map/backward/pallas_call | solution.py:225
  110.6 12.3 %collective-permute-start.5 = (bf16[256,4352]{1,0:T(8,128)(2,1)}, bf16[256,4352]{1,0:T(8,128)(2,1)}, u32[]{:S(2)}, u32[]{:S(2)}) collective-permute-start(bf16[256,4352]{1,0:T(8,128)(2,1)} %get-tuple-element.64.error0), channel_id=1, source_target_pairs={{0,16},{16,0},{1,17},{17,1},{2,18},{18,2},{3,19},{19,3},{4,20},{20... | collective-permute-start | bytes 6684680 | tf_op jit(solution)/shard_map/ppermute | solution.py:36
  123.0 0.3 collective-permute-start.6
  123.2 3.6 %all-to-all-start.5 = ((f32[16,28,128]{2,1,0:T(8,128)}), f32[16,28,128]{2,1,0:T(8,128)S(1)}, u32[]{:S(2)}, u32[]{:S(2)}) async-start(f32[16,28,128]{2,1,0:T(8,128)} %get-tuple-element.61), calls=%async_computation.5 | async-start | bytes 524288 | tf_op jit(solution)/shard_map/all_to_all | solution.py:412
  126.8 0.3 collective-permute-start.4
  127.1 0.3 collective-permute-start.7
  127.4 2.2 %collective-permute-done.7 = f32[1,384]{1,0:T(1,128)S(1)} collective-permute-done((f32[1,384]{1,0:T(1,128)S(1)}, f32[1,384]{1,0:T(1,128)S(1)}, u32[]{:S(2)}, u32[]{:S(2)}) %collective-permute-start.7) | collective-permute-done | bytes 1568 | tf_op jit(solution)/shard_map/ppermute | solution.py:36
  129.6 0.6 add_reduce_fusion
  130.2 0.0 collective-permute-done.4.codes1
  130.2 0.0 collective-permute-done.5.error1
  130.2 5.0 %decode_grad.1 = bf16[384,3584]{1,0:T(8,128)(2,1)} custom-call(bf16[256,384]{1,0:T(8,128)(2,1)S(1)} %get-tuple-element.62.codes0, bf16[256,384]{1,0:T(8,128)(2,1)S(1)} %collective-permute-done.4.codes1, bf16[256,4352]{1,0:T(8,128)(2,1)} %get-tuple-element.64.error0, bf16[256,4352]{1,0:T(8,128)(2,1)} %collective-permute-done.5.error1, ...), custom_call_target="tpu_custom_call" | custom-call | flops 1409286144 | bytes 10000000 | tf_op jit(solution)/shard_map/decode_grad/pallas_call | solution.py:283
  135.2 3.4 %all-to-all-done.5.parts = f32[16,28,128]{2,1,0:T(8,128)S(1)} async-done(((f32[16,28,128]{2,1,0:T(8,128)}), f32[16,28,128]{2,1,0:T(8,128)S(1)}, u32[]{:S(2)}, u32[]{:S(2)}) %all-to-all-start.5) | async-done | bytes 229408 | tf_op jit(solution)/shard_map/all_to_all | solution.py:412
  138.6 0.0 collective-permute-done.6.rows1
  138.6 0.8 minus_sum.1
  139.3 3.7 %all-to-all-start.6 = ((f32[16,28,128]{2,1,0:T(8,128)}), f32[16,28,128]{2,1,0:T(8,128)S(1)}, u32[]{:S(2)}, u32[]{:S(2)}) async-start(f32[16,28,128]{2,1,0:T(8,128)} %minus_sum.1), calls=%async_computation.6 | async-start | bytes 524288 | tf_op jit(solution)/shard_map/all_to_all | solution.py:423
  143.0 5.6 %encode_grad.1 = bf16[3584,384]{1,0:T(8,128)(2,1)} custom-call(bf16[256,3584]{1,0:T(8,128)(2,1)} %get-tuple-element.60.rows0, bf16[256,3584]{1,0:T(8,128)(2,1)} %collective-permute-done.6.rows1, bf16[256,4352]{1,0:T(8,128)(2,1)} %get-tuple-element.64.error0, bf16[256,4352]{1,0:T(8,128)(2,1)} %collective-permute-done.5.error1), custom_call_target="tpu_custom_call" | custom-call | flops 1409286144 | bytes 7000000 | tf_op jit(solution)/shard_map/encode_grad/pallas_call | solution.py:345
  148.6 2.0 %all-to-all-done.6 = f32[16,28,128]{2,1,0:T(8,128)S(1)} async-done(((f32[16,28,128]{2,1,0:T(8,128)}), f32[16,28,128]{2,1,0:T(8,128)S(1)}, u32[]{:S(2)}, u32[]{:S(2)}) %all-to-all-start.6) | async-done | bytes 229408 | tf_op jit(solution)/shard_map/all_to_all | solution.py:423
  150.7 0.6 reduce_sum.19
  (8 shorter events, 0.1 us)
Async XLA Ops:
  0.6 3.5 %copy-start = (bf16[32,3584]{1,0:T(8,128)(2,1)S(1)}, bf16[32,3584]{1,0:T(8,128)(2,1)}, u32[]{:S(2)}) copy-start(bf16[32,3584]{1,0:T(8,128)(2,1)} %param.5) | copy-start | bytes 688132
  0.6 14.1 %copy-start.5 = (f32[384]{0:T(512)S(1)}, f32[384]{0:T(512)}, u32[]{:S(2)}) copy-start(f32[384]{0:T(512)} %param.7) | copy-start | bytes 4612
  0.7 14.2 %copy-start.4 = (f32[3584]{0:T(1024)S(1)}, f32[3584]{0:T(1024)}, u32[]{:S(2)}) copy-start(f32[3584]{0:T(1024)} %param.9) | copy-start | bytes 43012
  0.7 17.6 %collective-permute-start.2 = (bf16[3584,384]{1,0:T(8,128)(2,1)}, bf16[3584,384]{1,0:T(8,128)(2,1)S(1)}, u32[]{:S(2)}, u32[]{:S(2)}) collective-permute-start(bf16[3584,384]{1,0:T(8,128)(2,1)} %enc0.3), channel_id=1, source_target_pairs={{0,16},{16,0},{1,17},{17,1},{2,18},{18,2},{3,19},{19,3},{4,20},{20... | collective-permute-start | bytes 8257544 | tf_op jit(solution)/shard_map/ppermute | solution.py:36
  4.0 14.3 %collective-permute-start.3 = (bf16[384,3584]{1,0:T(8,128)(2,1)}, bf16[384,3584]{1,0:T(8,128)(2,1)}, u32[]{:S(2)}, u32[]{:S(2)}) collective-permute-start(bf16[384,3584]{1,0:T(8,128)(2,1)} %dec.1), channel_id=1, source_target_pairs={{0,16},{16,0},{1,17},{17,1},{2,18},{18,2},{3,19},{19,3},{4,20},{20... | collective-permute-start | bytes 8257544 | tf_op jit(solution)/shard_map/ppermute | solution.py:36
  4.8 13.5 %all-to-all-start = ((bf16[4,2,3584]{2,1,0:T(2,128)(2,1)}), bf16[4,2,3584]{2,1,0:T(2,128)(2,1)S(1)}, u32[]{:S(2)}, u32[]{:S(2)}) async-start(bf16[4,2,3584]{2,1,0:T(2,128)(2,1)} %broadcast_in_dim.2), calls=%async_computation | async-start | bytes 114688 | tf_op jit(solution)/shard_map/all_to_all | solution.py:30
  13.7 1.9 %collective-permute-start = (f32[1,384]{1,0:T(1,128)S(1)}, f32[1,384]{1,0:T(1,128)S(1)}, u32[]{:S(2)}, u32[]{:S(2)}) collective-permute-start(f32[1,384]{1,0:T(1,128)S(1)} %broadcast_multiply_fusion.slope0), channel_id=1, source_target_pairs={{0,16},{16,0},{1,17},{17,1},{2,18},{18,2},{3,19},{19,3},{4,20},{20... | collective-permute-start | bytes 4616 | tf_op jit(solution)/shard_map/ppermute | solution.py:36
  14.7 1.2 collective-permute-start.1
  18.3 25.9 %copy-start.2 = (bf16[3584,384]{1,0:T(8,128)(2,1)S(1)}, bf16[3584,384]{1,0:T(8,128)(2,1)}, u32[]{:S(2)}) copy-start(bf16[3584,384]{1,0:T(8,128)(2,1)} %enc0.3) | copy-start | bytes 8257540
  20.7 23.4 %copy-start.1 = (bf16[384,3584]{1,0:T(8,128)(2,1)S(1)}, bf16[384,3584]{1,0:T(8,128)(2,1)}, u32[]{:S(2)}) copy-start(bf16[384,3584]{1,0:T(8,128)(2,1)} %dec.1) | copy-start | bytes 8257540
  49.1 20.8 %copy-start.3 = (bf16[256,384]{1,0:T(8,128)(2,1)}, bf16[256,384]{1,0:T(8,128)(2,1)S(1)}, u32[]{:S(2)}) copy-start(bf16[256,384]{1,0:T(8,128)(2,1)S(1)} %get-tuple-element.63) | copy-start | bytes 589828
  110.6 19.5 %collective-permute-start.5 = (bf16[256,4352]{1,0:T(8,128)(2,1)}, bf16[256,4352]{1,0:T(8,128)(2,1)}, u32[]{:S(2)}, u32[]{:S(2)}) collective-permute-start(bf16[256,4352]{1,0:T(8,128)(2,1)} %get-tuple-element.64.error0), channel_id=1, source_target_pairs={{0,16},{16,0},{1,17},{17,1},{2,18},{18,2},{3,19},{19,3},{4,20},{20... | collective-permute-start | bytes 6684680 | tf_op jit(solution)/shard_map/ppermute | solution.py:36
  123.0 15.6 %collective-permute-start.6 = (bf16[256,3584]{1,0:T(8,128)(2,1)}, bf16[256,3584]{1,0:T(8,128)(2,1)}, u32[]{:S(2)}, u32[]{:S(2)}) collective-permute-start(bf16[256,3584]{1,0:T(8,128)(2,1)} %get-tuple-element.60.rows0), channel_id=1, source_target_pairs={{0,16},{16,0},{1,17},{17,1},{2,18},{18,2},{3,19},{19,3},{4,20},{20... | collective-permute-start | bytes 5505032 | tf_op jit(solution)/shard_map/ppermute | solution.py:36
  123.2 15.3 %all-to-all-start.5 = ((f32[16,28,128]{2,1,0:T(8,128)}), f32[16,28,128]{2,1,0:T(8,128)S(1)}, u32[]{:S(2)}, u32[]{:S(2)}) async-start(f32[16,28,128]{2,1,0:T(8,128)} %get-tuple-element.61), calls=%async_computation.5 | async-start | bytes 524288 | tf_op jit(solution)/shard_map/all_to_all | solution.py:412
  126.8 3.3 %collective-permute-start.4 = (bf16[256,384]{1,0:T(8,128)(2,1)}, bf16[256,384]{1,0:T(8,128)(2,1)S(1)}, u32[]{:S(2)}, u32[]{:S(2)}) collective-permute-start(bf16[256,384]{1,0:T(8,128)(2,1)} %copy-done.3), channel_id=1, source_target_pairs={{0,16},{16,0},{1,17},{17,1},{2,18},{18,2},{3,19},{19,3},{4,20},{20... | collective-permute-start | bytes 589832 | tf_op jit(solution)/shard_map/ppermute | solution.py:36
  127.1 2.5 %collective-permute-start.7 = (f32[1,384]{1,0:T(1,128)S(1)}, f32[1,384]{1,0:T(1,128)S(1)}, u32[]{:S(2)}, u32[]{:S(2)}) collective-permute-start(f32[1,384]{1,0:T(1,128)S(1)} %get-tuple-element.67), channel_id=1, source_target_pairs={{0,16},{16,0},{1,17},{17,1},{2,18},{18,2},{3,19},{19,3},{4,20},{20... | collective-permute-start | bytes 4616 | tf_op jit(solution)/shard_map/ppermute | solution.py:36
  139.3 11.3 %all-to-all-start.6 = ((f32[16,28,128]{2,1,0:T(8,128)}), f32[16,28,128]{2,1,0:T(8,128)S(1)}, u32[]{:S(2)}, u32[]{:S(2)}) async-start(f32[16,28,128]{2,1,0:T(8,128)} %minus_sum.1), calls=%async_computation.6 | async-start | bytes 524288 | tf_op jit(solution)/shard_map/all_to_all | solution.py:423
